TPU v7x, 256 devices: a whole 4x4x8 slice. The times are simulated.
256 devices in a mesh: rows: 128 (over z, y, x_hi, core), batch: 2 (over x_lo).
Axes of the slice: x: 4 (x_hi: 2, x_lo: 2; x = x_hi * 2 + x_lo), y: 4, z: 8, core: 2. Of those that a mesh axis runs over, the one named last changes fastest.
Arguments:
- velocity: float32 [4, 512, 4096], P('batch', 'rows'), parts along dimension 0, may hold values from -6 to 6
- cotangent: float32 [4, 512, 4096], P('batch', 'rows'), parts along dimension 0, may hold values from -6 to 6
- w_in: bfloat16 [64, 3, 3, 2], replicated, may hold values from -1.5 to 1.5
- w_mid: bfloat16 [64, 64], replicated, may hold values from -0.75 to 0.75
- w_out: bfloat16 [3, 3, 2, 64], replicated, may hold values from -0.25 to 0.25
Outputs:
- new_velocity: float32 [4, 512, 4096], P('batch', 'rows'), parts along dimension 0
- grad_in: float32 [128, 3, 3, 2], P('batch'), parts along dimension 0
- grad_mid: float32 [128, 64], P('batch'), parts along dimension 0
- grad_out: float32 [6, 3, 2, 64], P('batch'), parts along dimension 0
There are 2 independent parts, one for each index of `batch`. A program takes and returns all parts, laid end to end along the dimension named above; an argument that names none is the same for every part. Nothing has to cross between parts.
All inputs are finite; a program needn't handle non-finite values.
Results may differ from a plain program's by a relative error of at most 0.007.
Values may be sent and summed in bfloat16 or wider, within the bound.
No kernel may reach another device: no remote copies, remote signals or barrier semaphores. Data moves between devices by JAX's collectives and lax.ppermute only.
A program may use at most 128 MiB of HBM per device.

v0:
```python
import math

import jax
import jax.numpy as jnp
from jax import lax
from jax.sharding import PartitionSpec as P

STEP_SIZE = 0.5
GELU_SCALE = 0.7978845608028654
GELU_CUBIC = 0.044715
HIGHEST = lax.Precision.HIGHEST
OFFSETS = ((-1, -1), (-1, 0), (-1, 1), (0, -1), (0, 0), (0, 1), (1, -1), (1, 0), (1, 1))


def with_halo(value, sides, width):
    for axis, dim in sides:
        size, length = (lax.axis_size(axis), value.shape[dim])
        up = [(i, (i + 1) % size) for i in range(size)]
        down = [(j, i) for i, j in up]
        last = lax.slice_in_dim(value, length - width, length, axis=dim)
        leading = lax.slice_in_dim(value, 0, width, axis=dim)
        before = lax.ppermute(last, axis, up)
        after = lax.ppermute(leading, axis, down)
        value = jnp.concatenate([before, value, after], axis=dim)
    return value


def gelu_value(pre):
    tangent = jnp.tanh(GELU_SCALE * (pre + GELU_CUBIC * pre * pre * pre))
    return 0.5 * pre * (1.0 + tangent)


def gelu_slope(pre):
    tangent = jnp.tanh(GELU_SCALE * (pre + GELU_CUBIC * pre * pre * pre))
    return 0.5 * (1.0 + tangent) + 0.5 * pre * (1.0 - tangent * tangent) * GELU_SCALE * (
        1.0 + 3.0 * GELU_CUBIC * pre * pre
    )


def stack_inputs(padded, width, offset, count):
    pieces = []
    for row_shift, col_shift in OFFSETS:
        start = width + offset + row_shift
        pieces.append(jnp.roll(padded[:, start : start + count], -col_shift, axis=2))
    return jnp.concatenate(pieces, axis=0)


def hidden_layers(stacked, w_in, w_mid):
    flat = stacked.reshape(stacked.shape[0], -1)
    pre_one = jnp.dot(w_in.reshape(w_in.shape[0], -1), flat, preferred_element_type=jnp.float32)
    act_one = gelu_value(pre_one).astype(jnp.bfloat16)
    pre_two = jnp.dot(w_mid, act_one, preferred_element_type=jnp.float32)
    act_two = gelu_value(pre_two).astype(jnp.bfloat16)
    return (pre_one, act_one, pre_two, act_two)


def conv_out(act_pad, w_out, count, columns):
    hidden = w_out.shape[3]
    outputs = jnp.dot(w_out.reshape(-1, hidden), act_pad, preferred_element_type=jnp.float32)
    outputs = outputs.reshape(9, w_out.shape[2], count + 2, columns)
    total = jnp.zeros((w_out.shape[2], count, columns), jnp.float32)
    for tap_index, (row_shift, col_shift) in enumerate(OFFSETS):
        window = outputs[tap_index, :, 1 + row_shift : 1 + row_shift + count]
        total = total + jnp.roll(window, -col_shift, axis=2)
    return total


def advection(padded):
    flux_rows = padded[0:1] * padded
    flux_cols = padded[1:2] * padded
    middle = flux_cols[:, 1:-1]
    return 0.5 * (flux_rows[:, 2:] - flux_rows[:, :-2]) + 0.5 * (
        jnp.roll(middle, -1, axis=2) - jnp.roll(middle, 1, axis=2)
    )


def backward_block(
    dcorr_rim,
    stacked_own,
    pre_one_own,
    act_one_own,
    pre_two_own,
    act_pad,
    w_mid,
    w_out,
    count,
    columns,
):
    channels = dcorr_rim.shape[0]
    own = dcorr_rim[:, 1 : 1 + count]
    zero_rows = jnp.zeros((channels, 2, columns), dcorr_rim.dtype)
    zero_pad = jnp.concatenate([zero_rows, own, zero_rows], axis=1)
    shifted = []
    extended = []
    for row_shift, col_shift in OFFSETS:
        shifted.append(
            jnp.roll(dcorr_rim[:, 1 - row_shift : 1 - row_shift + count], col_shift, axis=2)
        )
        extended.append(
            jnp.roll(zero_pad[:, 1 - row_shift : 1 - row_shift + count + 2], col_shift, axis=2)
        )
    shifted = jnp.concatenate(shifted, axis=0).reshape(9 * channels, -1)
    extended = jnp.concatenate(extended, axis=0).reshape(9 * channels, -1)
    w_flat = w_out.reshape(9 * channels, -1)
    contract_last = (((1,), (1,)), ((), ()))
    contract_first = (((0,), (0,)), ((), ()))
    grad_out = lax.dot_general(extended, act_pad, contract_last, preferred_element_type=jnp.float32)
    back_two = lax.dot_general(w_flat, shifted, contract_first, preferred_element_type=jnp.float32)
    delta_two = (back_two * gelu_slope(pre_two_own)).astype(jnp.bfloat16)
    grad_mid = lax.dot_general(
        delta_two, act_one_own, contract_last, preferred_element_type=jnp.float32
    )
    back_one = lax.dot_general(w_mid, delta_two, contract_first, preferred_element_type=jnp.float32)
    delta_one = (back_one * gelu_slope(pre_one_own)).astype(jnp.bfloat16)
    grad_in = lax.dot_general(
        delta_one, stacked_own, contract_last, preferred_element_type=jnp.float32
    )
    return (grad_in, grad_mid, grad_out)


def split_length(length):
    inner = min(length, 128)
    return (length // inner, inner)


def angle_table(first, second, modulus):
    product = lax.broadcasted_iota(jnp.int32, (first, second), 0) * lax.broadcasted_iota(
        jnp.int32, (first, second), 1
    )
    angle = (product % modulus).astype(jnp.float32) * (2.0 * math.pi / modulus)
    return (jnp.cos(angle), jnp.sin(angle))


def rotate(real, imag, table, form, sign):
    cosine, sine = table
    out_real = jnp.einsum(form, real, cosine, precision=HIGHEST)
    out_imag = sign * jnp.einsum(form, real, sine, precision=HIGHEST)
    if imag is not None:
        out_real = out_real - sign * jnp.einsum(form, imag, sine, precision=HIGHEST)
        out_imag = out_imag + jnp.einsum(form, imag, cosine, precision=HIGHEST)
    return (out_real, out_imag)


def twist(real, imag, table, sign):
    cosine, sine = table
    return (real * cosine - sign * imag * sine, imag * cosine + sign * real * sine)


def column_forward(field):
    channels, count, columns = field.shape
    outer, inner = split_length(columns)
    grid = field.reshape(channels, count, outer, inner)
    real, imag = rotate(grid, None, angle_table(outer, outer, outer), "hrab,ac->hrcb", -1.0)
    real, imag = twist(real, imag, angle_table(outer, inner, columns), -1.0)
    real, imag = rotate(real, imag, angle_table(inner, inner, inner), "hrcb,bd->hcdr", -1.0)
    return (real.reshape(channels, columns, count), imag.reshape(channels, columns, count))


def column_inverse(real, imag):
    channels, columns, count = real.shape
    outer, inner = split_length(columns)
    real = real.reshape(channels, outer, inner, count)
    imag = imag.reshape(channels, outer, inner, count)
    real, imag = rotate(real, imag, angle_table(inner, inner, inner), "hcdr,db->hrcb", 1.0)
    real, imag = twist(real, imag, angle_table(outer, inner, columns), 1.0)
    cosine, sine = angle_table(outer, outer, outer)
    result = jnp.einsum("hrcb,ca->hrab", real, cosine, precision=HIGHEST) - jnp.einsum(
        "hrcb,ca->hrab", imag, sine, precision=HIGHEST
    )
    return result.reshape(channels, count, columns) / columns


def row_forward(real, imag):
    channels, local, total = real.shape
    outer, inner = split_length(total)
    real = real.reshape(channels, local, outer, inner)
    imag = imag.reshape(channels, local, outer, inner)
    real, imag = rotate(real, imag, angle_table(outer, outer, outer), "hlab,ac->hlcb", -1.0)
    real, imag = twist(real, imag, angle_table(outer, inner, total), -1.0)
    real, imag = rotate(real, imag, angle_table(inner, inner, inner), "hlcb,bd->hlcd", -1.0)
    return (real.reshape(channels, local, total), imag.reshape(channels, local, total))


def row_inverse(real, imag):
    channels, local, total = real.shape
    outer, inner = split_length(total)
    real = real.reshape(channels, local, outer, inner)
    imag = imag.reshape(channels, local, outer, inner)
    real, imag = rotate(real, imag, angle_table(inner, inner, inner), "hlcd,db->hlcb", 1.0)
    real, imag = twist(real, imag, angle_table(outer, inner, total), 1.0)
    real, imag = rotate(real, imag, angle_table(outer, outer, outer), "hlcb,ca->hlab", 1.0)
    return (
        real.reshape(channels, local, total) / total,
        imag.reshape(channels, local, total) / total,
    )


def signed_frequency(index, length):
    signed = jnp.where(2 * index < length, index, index - length)
    signed = jnp.where(2 * index == length, 0, signed)
    return signed.astype(jnp.float32) / length


def remove_divergence(part, wave_row, wave_col, square):
    along = part[0::2]
    across = part[1::2]
    inner_product = (wave_row * along + wave_col * across) / square
    return jnp.stack(
        [along - wave_row * inner_product, across - wave_col * inner_product], axis=1
    ).reshape(part.shape)


def spectral_middle(real, imag):
    channels, columns, count = real.shape
    devices = lax.axis_size("rows")
    total = count * devices
    local = columns // devices
    real, imag = (
        lax.all_to_all(real, "rows", split_axis=1, concat_axis=2, tiled=True),
        lax.all_to_all(imag, "rows", split_axis=1, concat_axis=2, tiled=True),
    )
    real, imag = row_forward(real, imag)
    col_outer, col_inner = split_length(columns)
    row_outer, row_inner = split_length(total)
    spread = lax.axis_index("rows") * local + lax.iota(jnp.int32, local)
    wave_col = signed_frequency(spread // col_inner + col_outer * (spread % col_inner), columns)[
        None, :, None
    ]
    place = lax.iota(jnp.int32, total)
    wave_row = signed_frequency(place // row_inner + row_outer * (place % row_inner), total)[
        None, None, :
    ]
    square = wave_row * wave_row + wave_col * wave_col
    square = jnp.where(square > 0, square, 1.0)
    real = remove_divergence(real, wave_row, wave_col, square)
    imag = remove_divergence(imag, wave_row, wave_col, square)
    real, imag = row_inverse(real, imag)
    return (
        lax.all_to_all(real, "rows", split_axis=2, concat_axis=1, tiled=True),
        lax.all_to_all(imag, "rows", split_axis=2, concat_axis=1, tiled=True),
    )


def project(field):
    real, imag = column_forward(field)
    real, imag = spectral_middle(real, imag)
    return column_inverse(real, imag)


def body(velocity, cotangent, w_in, w_mid, w_out):
    channels, count, columns = velocity.shape
    hidden = w_mid.shape[0]
    devices = lax.axis_size("rows")
    rim = with_halo(velocity, (("rows", 1),), 1)
    stacked = stack_inputs(rim.astype(jnp.bfloat16), 1, 0, count)
    pre_one, act_one, pre_two, act_two = hidden_layers(stacked, w_in, w_mid)
    act_grid = with_halo(act_two.reshape(hidden, count, columns), (("rows", 1),), 1)
    act_pad = act_grid.reshape(hidden, -1)
    stacked_own = stacked.reshape(stacked.shape[0], -1)
    advect = advection(rim)
    correction = conv_out(act_pad, w_out, count, columns)
    provisional = velocity + STEP_SIZE * (correction - advect)
    scale = STEP_SIZE / math.sqrt(count * devices * columns)
    new_velocity = project(provisional)
    dual = project(cotangent)
    grad_corr = (dual * scale).astype(jnp.bfloat16)
    dcorr_rim = with_halo(grad_corr, (("rows", 1),), 1)
    local_in, local_mid, local_out = backward_block(
        dcorr_rim, stacked_own, pre_one, act_one, pre_two, act_pad, w_mid, w_out, count, columns
    )
    grad_in, grad_mid, grad_out = lax.psum((local_in, local_mid, local_out), "rows")
    return (new_velocity, grad_in.reshape(w_in.shape), grad_mid, grad_out.reshape(w_out.shape))


def solution(mesh):
    in_specs = (P("batch", "rows", None), P("batch", "rows", None), P(), P(), P())
    out_specs = (
        P("batch", "rows", None),
        P("batch", None, None, None),
        P("batch", None),
        P("batch", None, None, None),
    )
    return jax.shard_map(body, mesh=mesh, in_specs=in_specs, out_specs=out_specs, check_vma=False)
```

profile of v0, /device:TPU:1, one launch (start us, length us, event | category | flops | bytes accessed | tf_op | source)
XLA Modules:
  0.0 1022.0 jit_solution(7866726210884540466)
XLA Ops:
  1.7 4.2 collective-permute-start
  8.9 3.1 copy.151
  12.0 7.4 reshape.857
  19.4 15.8 %all-to-all-start.5 = ((f32[128,1,256]{2,1,0:T(1,128)}), f32[128,1,256]{2,1,0:T(1,128)S(1)}, u32[]{:S(2)}, u32[]{:S(2)}) async-start(f32[128,1,256]{2,1,0:T(1,128)} %reshape.857), calls=%async_computation.5 | async-start | bytes 262144 | tf_op jit(solution)/shard_map/all_to_all | solution.py:220
  39.7 7.4 reshape.859
  49.1 3.7 multiply_convert_fusion.1
  52.8 3.7 multiply_convert_fusion
  63.1 11.5 %all-to-all-start.4 = ((f32[128,1,256]{2,1,0:T(1,128)}), f32[128,1,256]{2,1,0:T(1,128)S(1)}, u32[]{:S(2)}, u32[]{:S(2)}) async-start(f32[128,1,256]{2,1,0:T(1,128)} %reshape.859), calls=%async_computation.4 | async-start | bytes 262144 | tf_op jit(solution)/shard_map/all_to_all | solution.py:219
  78.3 7.9 reshape.858
  86.2 5.7 copy.152
  93.4 7.9 reshape.860
  101.3 5.7 copy.150
  115.2 3.7 reshape.824
  128.4 4.2 copy.145
  132.7 7.6 reshape.849
  140.2 13.7 %all-to-all-start.1 = ((f32[128,1,256]{2,1,0:T(1,128)}), f32[128,1,256]{2,1,0:T(1,128)}, u32[]{:S(2)}, u32[]{:S(2)}) async-start(f32[128,1,256]{2,1,0:T(1,128)} %reshape.849), calls=%async_computation.1 | async-start | bytes 262144 | tf_op jit(solution)/shard_map/all_to_all | solution.py:220
  155.6 4.3 copy.143
  159.9 7.4 reshape.851
  167.3 14.2 %all-to-all-start = ((f32[128,1,256]{2,1,0:T(1,128)}), f32[128,1,256]{2,1,0:T(1,128)}, u32[]{:S(2)}, u32[]{:S(2)}) async-start(f32[128,1,256]{2,1,0:T(1,128)} %reshape.851), calls=%async_computation | async-start | bytes 262144 | tf_op jit(solution)/shard_map/all_to_all | solution.py:219
  184.9 7.9 reshape.850
  192.8 6.7 copy.146
  204.8 7.9 reshape.852
  212.7 7.1 copy.144
  242.2 14.4 %all-to-all-start.6 = ((f32[128,1,256]{2,1,0:T(1,128)}), f32[128,1,256]{2,1,0:T(1,128)}, u32[]{:S(2)}, u32[]{:S(2)}) async-start(f32[128,1,256]{2,1,0:T(1,128)} %reshape.861), calls=%async_computation.6 | async-start | bytes 262144 | tf_op jit(solution)/shard_map/all_to_all | solution.py:239
  272.4 13.7 %all-to-all-start.7 = ((f32[128,1,256]{2,1,0:T(1,128)}), f32[128,1,256]{2,1,0:T(1,128)S(1)}, u32[]{:S(2)}, u32[]{:S(2)}) async-start(f32[128,1,256]{2,1,0:T(1,128)} %reshape.863), calls=%async_computation.7 | async-start | bytes 262144 | tf_op jit(solution)/shard_map/all_to_all | solution.py:240
  294.8 4.3 all-to-all-done.7
  299.1 10.3 %all-to-all-start.2 = ((f32[128,1,256]{2,1,0:T(1,128)}), f32[128,1,256]{2,1,0:T(1,128)}, u32[]{:S(2)}, u32[]{:S(2)}) async-start(f32[128,1,256]{2,1,0:T(1,128)} %reshape.853), calls=%async_computation.2 | async-start | bytes 262144 | tf_op jit(solution)/shard_map/all_to_all | solution.py:239
  328.2 7.6 concatenate.154
  338.0 16.6 %all-to-all-start.3 = ((f32[128,1,256]{2,1,0:T(1,128)}), f32[128,1,256]{2,1,0:T(1,128)S(1)}, u32[]{:S(2)}, u32[]{:S(2)}) async-start(f32[128,1,256]{2,1,0:T(1,128)} %reshape.855), calls=%async_computation.3 | async-start | bytes 262144 | tf_op jit(solution)/shard_map/all_to_all | solution.py:240
  358.2 9.2 all-to-all-done.3
  378.1 5.5 fusion.14
  383.6 638.0 %all-reduce.2 = (f32[64,3,3,2]{0,3,2,1:T(2,128)}, f32[64,64]{1,0:T(8,128)}, f32[3,3,2,64]{3,2,1,0:T(2,128)}) all-reduce(f32[64,3,3,2]{0,3,2,1:T(2,128)S(1)} %reshape.840, f32[64,64]{1,0:T(8,128)S(1)} %fusion.542, f32[3,3,2,64]{3,2,1,0:T(2,128)S(1)} %reshape.841), channel_id=1, replica_groups=mesh['rows'=128,'batch'=2] {'rows'}, use_global_device_ids=true, to_apply=%region_0.1 | all-reduce | flops 6400 | bytes 51200 | tf_op jit(solution)/shard_map/psum | solution.py:271
  (234 shorter events, 131.5 us)
Async XLA Ops:
  0.6 52.2 %copy-start = (bf16[64,64]{1,0:T(8,128)(2,1)S(1)}, bf16[64,64]{1,0:T(8,128)(2,1)}, u32[]{:S(2)}) copy-start(bf16[64,64]{1,0:T(8,128)(2,1)} %param.8) | copy-start | bytes 24580
  1.7 45.5 %collective-permute-start = (f32[2,1,4096]{2,1,0:T(1,128)S(1)}, f32[2,1,4096]{2,1,0:T(1,128)S(1)}, u32[]{:S(2)}, u32[]{:S(2)}) collective-permute-start(f32[2,1,4096]{2,1,0:T(1,128)S(1)} %get-tuple-element.53), channel_id=1, source_target_pairs={{0,2},{2,4},{4,6},{6,8},{8,10},{10,12},{12,14},{14,16},{16,18},{18... | collective-permute-start | bytes 98312 | tf_op jit(solution)/shard_map/ppermute | solution.py:22
  5.9 41.2 %collective-permute-start.1 = (f32[2,1,4096]{2,1,0:T(1,128)S(1)}, f32[2,1,4096]{2,1,0:T(1,128)S(1)}, u32[]{:S(2)}, u32[]{:S(2)}) collective-permute-start(f32[2,1,4096]{2,1,0:T(1,128)S(1)} %get-tuple-element.54), channel_id=1, source_target_pairs={{2,0},{4,2},{6,4},{8,6},{10,8},{12,10},{14,12},{16,14},{18,16},{20... | collective-permute-start | bytes 98312 | tf_op jit(solution)/shard_map/ppermute | solution.py:23
  8.9 27.7 %copy-start.14 = (bf16[64,3,3,2]{0,3,2,1:T(2,128)(2,1)S(1)}, bf16[64,3,3,2]{0,3,2,1:T(2,128)(2,1)}, u32[]{:S(2)}) copy-start(bf16[64,3,3,2]{0,3,2,1:T(2,128)(2,1)} %param.7) | copy-start | bytes 6916
  8.9 27.7 %copy-start.15 = (bf16[3,3,2,64]{3,2,1,0:T(2,128)(2,1)S(1)}, bf16[3,3,2,64]{3,2,1,0:T(2,128)(2,1)}, u32[]{:S(2)}) copy-start(bf16[3,3,2,64]{3,2,1,0:T(2,128)(2,1)} %param.9) | copy-start | bytes 6916
  19.4 43.6 %all-to-all-start.5 = ((f32[128,1,256]{2,1,0:T(1,128)}), f32[128,1,256]{2,1,0:T(1,128)S(1)}, u32[]{:S(2)}, u32[]{:S(2)}) async-start(f32[128,1,256]{2,1,0:T(1,128)} %reshape.857), calls=%async_computation.5 | async-start | bytes 262144 | tf_op jit(solution)/shard_map/all_to_all | solution.py:220
  36.6 76.6 %copy-start.12 = (bf16[18,64]{1,0:T(8,128)(2,1)}, bf16[18,64]{1,0:T(8,128)(2,1)S(1)}, u32[]{:S(2)}) copy-start(bf16[18,64]{1,0:T(8,128)(2,1)S(1)} %reshape.823) | copy-start | bytes 6916
  36.6 10.6 %copy-start.2 = (f32[2,4,4096]{2,1,0:T(4,128)S(1)}, f32[2,4,4096]{2,1,0:T(4,128)}, u32[]{:S(2)}) copy-start(f32[2,4,4096]{2,1,0:T(4,128)} %param.5) | copy-start | bytes 393220
  49.1 3.7 copy-start.10
  52.8 3.7 copy-start.3
  56.6 1.3 copy-start.1
  59.0 50.1 %collective-permute-start.2 = (bf16[64,1,4096]{2,0,1:T(8,128)(2,1)S(1)}, bf16[64,1,4096]{2,0,1:T(8,128)(2,1)}, u32[]{:S(2)}, u32[]{:S(2)}) collective-permute-start(bf16[64,1,4096]{2,0,1:T(8,128)(2,1)S(1)} %get-tuple-element.14), channel_id=1, source_target_pairs={{0,2},{2,4},{4,6},{6,8},{8,10},{10,12},{12,14},{14,16},{16,18},{18... | collective-permute-start | bytes 1572872 | tf_op jit(solution)/shard_map/ppermute | solution.py:22
  63.1 29.4 %all-to-all-start.4 = ((f32[128,1,256]{2,1,0:T(1,128)}), f32[128,1,256]{2,1,0:T(1,128)S(1)}, u32[]{:S(2)}, u32[]{:S(2)}) async-start(f32[128,1,256]{2,1,0:T(1,128)} %reshape.859), calls=%async_computation.4 | async-start | bytes 262144 | tf_op jit(solution)/shard_map/all_to_all | solution.py:219
  75.5 36.4 %collective-permute-start.3 = (bf16[64,1,4096]{2,0,1:T(8,128)(2,1)}, bf16[64,1,4096]{2,0,1:T(8,128)(2,1)}, u32[]{:S(2)}, u32[]{:S(2)}) collective-permute-start(bf16[64,1,4096]{2,0,1:T(8,128)(2,1)} %get-tuple-element.13), channel_id=1, source_target_pairs={{2,0},{4,2},{6,4},{8,6},{10,8},{12,10},{14,12},{16,14},{18,16},{20... | collective-permute-start | bytes 1572872 | tf_op jit(solution)/shard_map/ppermute | solution.py:23
  92.4 15.1 %copy-start.5 = (f32[2,32,4,128]{3,2,1,0:T(4,128)}, f32[2,32,4,128]{3,2,1,0:T(4,128)S(1)}, u32[]{:S(2)}) copy-start(f32[2,32,4,128]{3,2,1,0:T(4,128)S(1)} %copy.117) | copy-start | bytes 393220
  107.6 1.5 copy-start.7
  124.5 0.6 copy-start.9
  140.2 27.1 %all-to-all-start.1 = ((f32[128,1,256]{2,1,0:T(1,128)}), f32[128,1,256]{2,1,0:T(1,128)}, u32[]{:S(2)}, u32[]{:S(2)}) async-start(f32[128,1,256]{2,1,0:T(1,128)} %reshape.849), calls=%async_computation.1 | async-start | bytes 262144 | tf_op jit(solution)/shard_map/all_to_all | solution.py:220
  155.6 25.9 %copy-start.8 = (f32[2,32,4,128]{3,2,1,0:T(4,128)S(1)}, f32[2,32,4,128]{3,2,1,0:T(4,128)}, u32[]{:S(2)}) copy-start(f32[2,32,4,128]{3,2,1,0:T(4,128)} %copy-done.7) | copy-start | bytes 393220
  155.6 26.3 %copy-start.6 = (f32[2,32,4,128]{3,2,1,0:T(4,128)S(1)}, f32[2,32,4,128]{3,2,1,0:T(4,128)}, u32[]{:S(2)}) copy-start(f32[2,32,4,128]{3,2,1,0:T(4,128)} %copy-done.5) | copy-start | bytes 393220
  167.3 35.6 %all-to-all-start = ((f32[128,1,256]{2,1,0:T(1,128)}), f32[128,1,256]{2,1,0:T(1,128)}, u32[]{:S(2)}, u32[]{:S(2)}) async-start(f32[128,1,256]{2,1,0:T(1,128)} %reshape.851), calls=%async_computation | async-start | bytes 262144 | tf_op jit(solution)/shard_map/all_to_all | solution.py:219
  242.2 30.1 %all-to-all-start.6 = ((f32[128,1,256]{2,1,0:T(1,128)}), f32[128,1,256]{2,1,0:T(1,128)}, u32[]{:S(2)}, u32[]{:S(2)}) async-start(f32[128,1,256]{2,1,0:T(1,128)} %reshape.861), calls=%async_computation.6 | async-start | bytes 262144 | tf_op jit(solution)/shard_map/all_to_all | solution.py:239
  272.4 26.7 %all-to-all-start.7 = ((f32[128,1,256]{2,1,0:T(1,128)}), f32[128,1,256]{2,1,0:T(1,128)S(1)}, u32[]{:S(2)}, u32[]{:S(2)}) async-start(f32[128,1,256]{2,1,0:T(1,128)} %reshape.863), calls=%async_computation.7 | async-start | bytes 262144 | tf_op jit(solution)/shard_map/all_to_all | solution.py:240
  299.1 38.9 %all-to-all-start.2 = ((f32[128,1,256]{2,1,0:T(1,128)}), f32[128,1,256]{2,1,0:T(1,128)}, u32[]{:S(2)}, u32[]{:S(2)}) async-start(f32[128,1,256]{2,1,0:T(1,128)} %reshape.853), calls=%async_computation.2 | async-start | bytes 262144 | tf_op jit(solution)/shard_map/all_to_all | solution.py:239
  321.8 49.9 %collective-permute-start.4 = (bf16[2,1,4096]{2,1,0:T(2,128)(2,1)}, bf16[2,1,4096]{2,1,0:T(2,128)(2,1)S(1)}, u32[]{:S(2)}, u32[]{:S(2)}) collective-permute-start(bf16[2,1,4096]{2,1,0:T(2,128)(2,1)} %get-tuple-element.80), channel_id=1, source_target_pairs={{2,0},{4,2},{6,4},{8,6},{10,8},{12,10},{14,12},{16,14},{18,16},{20... | collective-permute-start | bytes 49160 | tf_op jit(solution)/shard_map/ppermute | solution.py:23
  322.5 49.1 %collective-permute-start.5 = (bf16[2,1,4096]{2,1,0:T(2,128)(2,1)S(1)}, bf16[2,1,4096]{2,1,0:T(2,128)(2,1)S(1)}, u32[]{:S(2)}, u32[]{:S(2)}) collective-permute-start(bf16[2,1,4096]{2,1,0:T(2,128)(2,1)S(1)} %get-tuple-element.79), channel_id=1, source_target_pairs={{0,2},{2,4},{4,6},{6,8},{8,10},{10,12},{12,14},{14,16},{16,18},{18... | collective-permute-start | bytes 49160 | tf_op jit(solution)/shard_map/ppermute | solution.py:22
  338.0 29.5 %all-to-all-start.3 = ((f32[128,1,256]{2,1,0:T(1,128)}), f32[128,1,256]{2,1,0:T(1,128)S(1)}, u32[]{:S(2)}, u32[]{:S(2)}) async-start(f32[128,1,256]{2,1,0:T(1,128)} %reshape.855), calls=%async_computation.3 | async-start | bytes 262144 | tf_op jit(solution)/shard_map/all_to_all | solution.py:240
  368.9 4.9 copy-start.13
  371.6 2.2 copy-start.16
  373.8 3.1 copy-start.4
  377.0 1.1 copy-start.11
where the time goes:
time: 1040 us; the launch traced here: 1020 us
  blocking collectives  638 us (61%)
  local copies, waits for them, and re-layouts  165 us (16%)
  starting transfers between devices  122 us (12%)
  matrix products  59.9 us (6%)
  other arithmetic  21.5 us (2%)
  waiting for transfers between devices  13.6 us (1%)
    psum x1, blocking collectives, body(): lax.psum((local_in, local_mid, local_out), 'rows')  638 us
    unnamed x60, local copies, waits for them, and re-layouts  80.7 us
    all_to_all x2, starting transfers between devices, spectral_middle(): lax.all_to_all(imag, 'rows', split_axis=2, concat_axis=1, tiled=True)  30.4 us
    all_to_all x2, starting transfers between devices, spectral_middle(): lax.all_to_all(imag, 'rows', split_axis=1, concat_axis=2, tiled=True)  29.5 us
    all_to_all x2, starting transfers between devices, spectral_middle(): lax.all_to_all(real, 'rows', split_axis=1, concat_axis=2, tiled=True)  25.7 us
    all_to_all x2, starting transfers between devices, spectral_middle(): lax.all_to_all(real, 'rows', split_axis=2, concat_axis=1, tiled=True)  24.6 us
  transfers between devices with their start and end apart: 14, of which 2 were waited for; matrix products, arithmetic and copies ran while one was open for 16% of the time, Pallas kernels for 0%

commit v1 on v0

v1 whole, which is shorter than its diff:
```python
import math

import jax
import jax.numpy as jnp
import ml_dtypes
import numpy as np
from jax import lax
from jax.experimental import pallas as pl
from jax.experimental.pallas import tpu as pltpu
from jax.sharding import PartitionSpec as P

STEP_SIZE = 0.5
GELU_SCALE = 0.7978845608028654
GELU_CUBIC = 0.044715
BF = jnp.bfloat16
F32 = jnp.float32
TILE = 256
VMEM_LIMIT = 48 * 1024 * 1024

R = 4
D = 128
NX = R * D
OUTER = 32
NY = OUTER * 128
C = OUTER // 2
CH = 2
HID = 64


def table_pair(matrix):
    high = np.asarray(matrix, np.float64).astype(ml_dtypes.bfloat16)
    low = (matrix - high.astype(np.float64)).astype(ml_dtypes.bfloat16)
    return np.stack([high, low])


def column_tables():
    a = np.arange(OUTER)
    b = np.arange(128)
    d = np.arange(D)
    c = np.arange(C)
    eye = np.eye(R * CH).reshape(CH, R, CH, R)
    sign = np.where(a % 2 == 0, 1.0, -1.0)
    angle = 2 * np.pi * np.outer(c, a) / OUTER
    first = np.stack([np.cos(angle), -np.sin(angle)])
    first[0, 0] = 1.0
    first[1, 0] = sign
    forward_a = np.einsum("pca,hrgs->phcrags", first, eye).reshape(256, 256)
    last = np.stack([2 * np.cos(angle), -2 * np.sin(angle)])
    last[0, 0] = 1.0
    last[1, 0] = sign
    last = last / NY
    inverse_a = np.einsum("pca,gshr->agsphcr", last, eye).reshape(256, 256)
    half = np.zeros((2, 4, CH, 2))
    for h in range(CH):
        for e in range(2):
            half[h, h * 2 + e, h, e] = 1.0
    rim = np.zeros((8, CH, 2))
    rim[:4] = np.eye(4).reshape(4, CH, 2)
    inverse_rim = np.einsum("pca,khr->akphcr", last, rim).reshape(256, 128)
    theta = 2 * np.pi * np.outer(c, b) / NY
    cosine = np.cos(theta)
    sine = np.sin(theta)
    cosine[0] = 1.0
    sine[0] = 0.0
    spread = lambda t, n: np.broadcast_to(t[None, :, None, :], (CH, C, n, 128)).reshape(-1, 128)
    twist = np.stack([spread(cosine, R), spread(sine, R)]).astype(np.float32)
    twist_rim = np.stack([spread(cosine, 2), spread(sine, 2)]).astype(np.float32)
    phi = 2 * np.pi * np.outer(d, b) / 128
    matrix = np.zeros((D, 2, 2, 128))
    matrix[:, 0, 0] = np.cos(phi)
    matrix[:, 0, 1] = np.sin(phi)
    matrix[:, 1, 0] = -np.sin(phi)
    matrix[:, 1, 1] = np.cos(phi)
    psi = 2 * np.pi * np.outer(16 + 32 * (d - 64), b) / NY
    alternate = np.where(b % 2 == 0, 1.0, -1.0)
    zero = np.zeros((D, 2, 2, 128))
    zero[:64, 0, 0] = np.cos(phi[:64])
    zero[:64, 1, 0] = -np.sin(phi[:64])
    zero[0, 1, 0] = alternate
    zero[64:, 0, 1] = np.cos(psi[64:])
    zero[64:, 1, 1] = -np.sin(psi[64:])
    back = np.zeros((2, 128, D, 2))
    back[0, :, :, 0] = np.cos(phi).T
    back[0, :, :, 1] = -np.sin(phi).T
    back[1, :, :, 0] = np.sin(phi).T
    back[1, :, :, 1] = np.cos(phi).T
    back_zero = np.zeros((2, 128, D, 2))
    back_zero[0, :, :64, 0] = 2 * np.cos(phi[:64]).T
    back_zero[0, :, :64, 1] = -2 * np.sin(phi[:64]).T
    back_zero[0, :, 0, 0] = 1.0
    back_zero[0, :, 0, 1] = alternate
    back_zero[1, :, 64:, 0] = 2 * np.cos(psi[64:]).T
    back_zero[1, :, 64:, 1] = -2 * np.sin(psi[64:]).T
    return {
        "forward_a": table_pair(forward_a),
        "forward_b": table_pair(matrix.reshape(256, 256)),
        "forward_b0": table_pair(zero.reshape(256, 256)),
        "twist": twist,
        "inverse_b": table_pair(back.reshape(256, 256)),
        "inverse_b0": table_pair(back_zero.reshape(256, 256)),
        "inverse_a": inverse_a,
        "inverse_rim": inverse_rim,
        "untwist": np.ascontiguousarray(twist.transpose(0, 2, 1)),
        "untwist_rim": np.ascontiguousarray(twist_rim.transpose(0, 2, 1)),
    }


def row_tables():
    s = np.arange(D)
    m1 = np.arange(D)
    m2 = np.arange(R)
    phi = 2 * np.pi * np.outer(m1, s) / D
    forward = np.zeros((2, D, D, 2))
    forward[0, :, :, 0] = np.cos(phi)
    forward[0, :, :, 1] = np.sin(phi)
    forward[1, :, :, 0] = -np.sin(phi)
    forward[1, :, :, 1] = np.cos(phi)
    inverse = np.zeros((D, 2, 2, D))
    inverse[:, 0, 0] = np.cos(phi).T
    inverse[:, 0, 1] = -np.sin(phi).T
    inverse[:, 1, 0] = np.sin(phi).T
    inverse[:, 1, 1] = np.cos(phi).T
    inverse = inverse / NX
    eye = np.eye(CH * C)

    def short(rows, flip):
        angle = 2 * np.pi * np.outer(m2, rows) / R
        block = np.zeros((2, R, 2, len(rows)))
        block[0, :, 0] = np.cos(angle)
        block[1, :, 0] = -np.sin(angle) * flip
        block[0, :, 1] = np.sin(angle) * flip
        block[1, :, 1] = np.cos(angle)
        block = np.round(block)
        return np.einsum("pmqr,gk->pgmqkr", block, eye).reshape(2 * CH * C * R, 2, -1)

    own = np.arange(R)
    rim = np.array([-1, R])
    rim_block = np.zeros((256, 2, 128))
    rim_block[:, :, :64] = short(rim, 1.0)

    def lanes(rows):
        theta = 2 * np.pi * np.outer(m1, rows) / NX
        both = np.stack([np.cos(theta), np.sin(theta)])
        wide = np.broadcast_to(both[:, :, None, :], (2, D, CH * C, len(rows))).reshape(2, D, -1)
        out = np.zeros((2, D, 128), np.float32)
        out[:, :, : wide.shape[2]] = wide
        return out

    return {
        "row_forward": table_pair(forward.reshape(256, 256)),
        "row_inverse": table_pair(inverse.reshape(256, 256)),
        "short_forward": short(own, -1.0).reshape(256, 256).astype(ml_dtypes.bfloat16),
        "short_inverse": short(own, 1.0).reshape(256, 256).astype(ml_dtypes.bfloat16),
        "short_rim": rim_block.reshape(256, 256).astype(ml_dtypes.bfloat16),
        "spin": lanes(own),
        "spin_rim": lanes(rim),
    }


def velocity_row(ch, row):
    if 0 <= row < R:
        return ch * R + row
    return 8 + ch * 2 + row + 2 if row < 0 else 12 + ch * 2 + row - R


def dual_row(ch, row):
    if 0 <= row < R:
        return ch * R + row
    return 8 + ch * 2 + (0 if row < 0 else 1)


def network_tables():
    taps = np.zeros((6, 18, 48))
    for i in range(-1, 5):
        for a in range(-1, 2):
            for b in range(-1, 2):
                for ch in range(CH):
                    t = (3 * (a + 1) + b + 1) * 2 + ch
                    taps[i + 1, t, (b + 1) * 16 + velocity_row(ch, i + a)] = 1
    outs = np.zeros((6, 24, 18))
    for k in range(-1, 5):
        for a in range(-1, 2):
            i = k - a
            if 0 <= i < R:
                for b in range(-1, 2):
                    for o in range(CH):
                        outs[k + 1, (b + 1) * 8 + o * R + i, (3 * (a + 1) + b + 1) * 2 + o] = 1
    duals = np.zeros((R, 18, 48))
    for i in range(R):
        for a in range(-1, 2):
            for b in range(-1, 2):
                for o in range(CH):
                    t = (3 * (a + 1) + b + 1) * 2 + o
                    duals[i, t, (b + 1) * 16 + dual_row(o, i - a)] = 1
    place_mid = np.zeros((64, 128))
    place_mid[:, :64] = np.eye(64)
    place_in = np.zeros((R, 48, 128))
    place_in[:, :, 64:82] = taps[1:5].transpose(0, 2, 1)
    place_out = np.zeros((R, 48, 128))
    place_out[:, :, 82:100] = duals.transpose(0, 2, 1)
    spread = np.zeros((64, 2, 2, 2, 64))
    for h in range(64):
        for core in range(2):
            for part in range(2):
                spread[h, core, part, part, h] = 1
    low = lambda t: t.astype(ml_dtypes.bfloat16)
    return {
        "taps": low(taps),
        "outs": low(outs),
        "duals": low(duals),
        "place_mid": low(place_mid),
        "place_in": low(place_in),
        "place_out": low(place_out),
        "spread": low(spread.reshape(256, 128)),
    }


def dot(x, y):
    return jnp.dot(x, y, preferred_element_type=F32)


def dot_nt(x, y):
    return lax.dot_general(x, y, (((1,), (1,)), ((), ())), preferred_element_type=F32)


def dot_tn(x, y):
    return lax.dot_general(x, y, (((0,), (0,)), ((), ())), preferred_element_type=F32)


def halves(x):
    high = x.astype(BF)
    return high, (x - high.astype(F32)).astype(BF)


def exact(form, pair, x):
    high, low = halves(x)
    return form(pair[0], high) + (form(pair[1], high) + form(pair[0], low))


def pair_low(form, pair, x):
    return form(pair[0], x) + form(pair[1], x)


def to_blocks(x):
    return jnp.concatenate([x[:, 128 * a : 128 * a + 128] for a in range(OUTER)], axis=0)


def from_blocks(x):
    rows = x.shape[0] // OUTER
    return jnp.concatenate([x[rows * a : rows * a + rows] for a in range(OUTER)], axis=1)


def column_forward(x, forward_a, forward_b, forward_b0, twist):
    y = exact(dot, forward_a, to_blocks(x))
    real, imag = y[:128], y[128:]
    cosine, sine = twist[0], twist[1]
    both = jnp.concatenate([real * cosine + imag * sine, imag * cosine - real * sine], axis=1)
    general = exact(dot_nt, forward_b, both)
    zero = exact(dot_nt, forward_b0, both)
    lane = lax.broadcasted_iota(jnp.int32, general.shape, 1)
    return jnp.where(lane % 64 < R, zero, general).astype(BF)


def column_inverse_first(x, inverse_b, inverse_b0, untwist, period, width):
    general = pair_low(dot, inverse_b, x)
    zero = pair_low(dot, inverse_b0, x)
    lane = lax.broadcasted_iota(jnp.int32, general.shape, 1)
    y = jnp.where(lane % period < width, zero, general)
    real, imag = y[:128], y[128:]
    cosine, sine = untwist[0], untwist[1]
    return real * cosine - imag * sine, imag * cosine + real * sine


def spectral(x, device, row_forward, short_forward, spin):
    v = pair_low(dot, row_forward, x)
    real, imag = v[:128], v[128:]
    cosine, sine = spin[0], spin[1]
    both = jnp.concatenate([real * cosine + imag * sine, imag * cosine - real * sine], axis=1)
    high, low = halves(both)
    full = dot(high, short_forward) + dot(low, short_forward)
    m1 = lax.broadcasted_iota(jnp.int32, (128, 128), 0)
    lane = lax.broadcasted_iota(jnp.int32, (128, 128), 1)
    m = m1 + 128 * (lane % R)
    m = jnp.where(2 * m < NX, m, jnp.where(2 * m == NX, 0, m - NX))
    c = (lane % 64) // R
    n = c + OUTER * device
    n = jnp.where(2 * n < NY, n, n - NY)
    packed = jnp.where(device < 64, OUTER * device, 16 + OUTER * (device - 64))
    n = jnp.where(c == 0, packed, n)
    wave_row = m.astype(F32) * (1.0 / NX)
    wave_col = n.astype(F32) * (1.0 / NY)
    row_square = wave_row * wave_row
    col_square = wave_col * wave_col
    square = row_square + col_square
    some = square > 0
    inverse = 1.0 / jnp.where(some, square, 1.0)
    same = jnp.where(some, jnp.where(lane < 64, col_square, row_square) * inverse, 1.0)
    cross = -(wave_row * wave_col) * inverse
    real, imag = full[:, :128], full[:, 128:]
    real = same * real + cross * pltpu.roll(real, 64, 1)
    imag = same * imag + cross * pltpu.roll(imag, 64, 1)
    return jnp.concatenate([real, imag], axis=1)


def row_back(both, row_inverse, short, spin):
    high, low = halves(both)
    full = dot(high, short) + dot(low, short)
    real, imag = full[:, :128], full[:, 128:]
    cosine, sine = spin[0], spin[1]
    v = jnp.concatenate([real * cosine - imag * sine, imag * cosine + real * sine], axis=0)
    return exact(dot, row_inverse, v).astype(BF)


def gelu_parts(pre):
    square = pre * pre
    tangent = jnp.tanh(pre * (GELU_SCALE + (GELU_SCALE * GELU_CUBIC) * square))
    gate = 0.5 + 0.5 * tangent
    return square, gate, pre * gate


def slope_of(square, gate, value):
    return gate + value * (1.0 - gate) * (2 * GELU_SCALE + (6 * GELU_SCALE * GELU_CUBIC) * square)


def dual_kernel(field, forward_a, forward_b, forward_b0, twist, sent):
    x = jnp.concatenate([field[0], field[1]], axis=0)
    sent[...] = column_forward(x, forward_a, forward_b, forward_b0, twist).reshape(D, 2, 128)


def network_kernel(
    velocity,
    before,
    after,
    w_in,
    w_mid,
    w_out,
    taps,
    outs,
    forward_a,
    forward_b,
    forward_b0,
    twist,
    sent,
    act_one,
    act_two,
    slope_one,
    slope_two,
    stack,
    act_all,
    partial,
):
    own = jnp.concatenate([velocity[0], velocity[1]], axis=0)
    low_before = before[...].astype(F32)
    low_after = after[...].astype(F32)
    base = jnp.concatenate([own, low_before, low_after], axis=0)
    stack[0:16, :] = pltpu.roll(base, 1, 1).astype(BF)
    stack[16:32, :] = base.astype(BF)
    stack[32:48, :] = pltpu.roll(base, NY - 1, 1).astype(BF)
    first = jnp.concatenate([dot(w_in[...], taps[i]).astype(BF) for i in range(6)], axis=0)
    third = jnp.concatenate([dot(outs[i], w_out[...]).astype(BF) for i in range(6)], axis=1)
    middle = w_mid[...]

    def step(index, _):
        at = pl.ds(pl.multiple_of(index * TILE, TILE), TILE)
        pre = dot(first, stack[:, at])
        for i in range(6):
            keep = 1 <= i <= R
            rows = pl.ds(64 * (i - 1), 64)
            square, gate, value = gelu_parts(pre[64 * i : 64 * i + 64])
            low = value.astype(BF)
            if keep:
                act_one[rows, at] = low
                slope_one[rows, at] = slope_of(square, gate, value).astype(BF)
            square, gate, value = gelu_parts(dot(middle, low))
            low = value.astype(BF)
            act_all[pl.ds(64 * i, 64), :] = low
            if keep:
                act_two[rows, at] = low
                slope_two[rows, at] = slope_of(square, gate, value).astype(BF)
        partial[:, at] = dot(third, act_all[...])
        return 0

    lax.fori_loop(0, NY // TILE, step, 0)
    correction = (
        pltpu.roll(partial[0:8, :], 1, 1) + partial[8:16, :] + pltpu.roll(partial[16:24, :], NY - 1, 1)
    )
    extended = [
        jnp.concatenate([low_before[2 * c + 1 : 2 * c + 2], velocity[c], low_after[2 * c : 2 * c + 1]], axis=0)
        for c in range(CH)
    ]
    across = velocity[1]
    pieces = []
    for c in range(CH):
        flux = extended[0] * extended[c]
        side = across * velocity[c]
        pieces.append(
            (flux[2:] - flux[:-2]) + (pltpu.roll(side, NY - 1, 1) - pltpu.roll(side, 1, 1))
        )
    advect = 0.5 * jnp.concatenate(pieces, axis=0)
    provisional = own + STEP_SIZE * (correction - advect)
    sent[...] = column_forward(provisional, forward_a, forward_b, forward_b0, twist).reshape(D, 2, 128)


def middle_kernel(
    device, got, other, row_forward, row_inverse, short_forward, short_inverse, short_rim, spin, spin_rim, sent
):
    both = spectral(got[...].reshape(256, 128), device[0], row_forward, short_forward[...], spin)
    sent[:, 0] = row_back(both, row_inverse, short_inverse[...], spin).reshape(D, 2, 128)
    sent[:, 1] = row_back(both, row_inverse, short_rim[...], spin_rim).reshape(D, 2, 128)
    sent[:, 2] = other[...]


def backward_kernel(
    device,
    got,
    act_one,
    act_two,
    slope_one,
    slope_two,
    stack,
    w_mid,
    w_out,
    duals,
    place_mid,
    place_in,
    place_out,
    spread,
    row_forward,
    row_inverse,
    short_forward,
    short_inverse,
    spin,
    inverse_b,
    inverse_b0,
    inverse_a,
    inverse_rim,
    untwist,
    untwist_rim,
    sent,
    dual_stack,
    sum_mid,
    sum_in,
    sum_out,
):
    both = spectral(got[:, 2].reshape(256, 128), device[0], row_forward, short_forward[...], spin)
    sent[:, 0] = row_back(both, row_inverse, short_inverse[...], spin).reshape(D, 2, 128)
    real, imag = column_inverse_first(got[:, 0].reshape(256, 128), inverse_b, inverse_b0, untwist, 64, R)
    own = exact(dot_nt, inverse_a, jnp.concatenate([real, imag], axis=1))
    rim = got[:, 1].reshape(256, 128)
    real, imag = column_inverse_first(rim[:, :64], inverse_b, inverse_b0, untwist_rim, 32, 2)
    rim = exact(dot_nt, inverse_rim, jnp.concatenate([real, imag], axis=1))
    base = jnp.concatenate([from_blocks(own), from_blocks(rim)], axis=0)
    dual_stack[0:16, :] = pltpu.roll(base, NY - 1, 1).astype(BF)
    dual_stack[16:32, :] = base.astype(BF)
    dual_stack[32:48, :] = pltpu.roll(base, 1, 1).astype(BF)
    spread_out = jnp.concatenate([dot_tn(w_out[...], duals[i]).astype(BF) for i in range(R)], axis=0)
    middle = w_mid[...]
    sum_mid[...] = jnp.zeros_like(sum_mid)
    sum_in[...] = jnp.zeros_like(sum_in)
    sum_out[...] = jnp.zeros_like(sum_out)

    def step(index, _):
        at = pl.ds(pl.multiple_of(index * TILE, TILE), TILE)
        dual = dual_stack[:, at]
        back_two = dot(spread_out, dual)
        delta_two = (back_two * slope_two[:, at].astype(F32)).astype(BF)
        hidden = act_one[:, at]
        wide = lambda t: jnp.concatenate([t[64 * i : 64 * i + 64] for i in range(R)], axis=1)
        wide_two = wide(delta_two)
        sum_mid[...] += dot_nt(wide_two, wide(hidden))
        back_one = dot_tn(middle, wide_two)
        tall = jnp.concatenate([back_one[:, TILE * i : TILE * i + TILE] for i in range(R)], axis=0)
        delta_one = (tall * slope_one[:, at].astype(F32)).astype(BF)
        sum_in[...] += dot_nt(delta_one, stack[:, at])
        sum_out[...] += dot_nt(act_two[:, at], dual)
        return 0

    lax.fori_loop(0, NY // TILE, step, 0)
    high, low = halves(sum_mid[...])
    total = dot(high, place_mid[...]) + dot(low, place_mid[...])
    for source, place in ((sum_in, place_in), (sum_out, place_out)):
        for i in range(R):
            high, low = halves(source[64 * i : 64 * i + 64, :])
            total = total + (dot(high, place[i]) + dot(low, place[i]))
    high, low = halves(total)
    sent[:, 1] = dot(spread[...], jnp.concatenate([high, low], axis=0)).astype(BF).reshape(D, 2, 128)


def sum_kernel(got, total):
    ones = jnp.ones((64, 256), BF)
    total[...] = dot(ones, got[:, 1].reshape(256, 128))


def field_kernel(got, inverse_b, inverse_b0, inverse_a, untwist, field):
    real, imag = column_inverse_first(got[:, 0].reshape(256, 128), inverse_b, inverse_b0, untwist, 64, R)
    x = from_blocks(exact(dot_nt, inverse_a, jnp.concatenate([real, imag], axis=1)))
    field[0] = x[:R]
    field[1] = x[R:]


def call(kernel, outputs, inputs, scratch=(), scalars=0):
    vmem = pl.BlockSpec(memory_space=pltpu.VMEM)
    smem = pl.BlockSpec(memory_space=pltpu.SMEM)
    single = not isinstance(outputs, list)
    return pl.pallas_call(
        kernel,
        out_shape=outputs,
        in_specs=[smem] * scalars + [vmem] * (len(inputs) - scalars),
        out_specs=vmem if single else [vmem] * len(outputs),
        scratch_shapes=list(scratch),
        compiler_params=pltpu.CompilerParams(vmem_limit_bytes=VMEM_LIMIT),
    )(*inputs)


def exchange(x, groups=None):
    return lax.all_to_all(x, "rows", split_axis=0, concat_axis=0, tiled=True, axis_index_groups=groups)


def body(velocity, cotangent, w_in, w_mid, w_out):
    columns = column_tables()
    rows = row_tables()
    net = network_tables()
    scale = STEP_SIZE / math.sqrt(NX * NY)
    shape = jax.ShapeDtypeStruct
    flat_in = w_in.reshape(HID, 18)
    flat_out = w_out.reshape(18, HID)
    device = lax.axis_index("rows").reshape(1)
    size = D
    up = [(i, (i + 1) % size) for i in range(size)]
    down = [(j, i) for i, j in up]
    low = velocity.astype(BF)
    before = lax.ppermute(low[:, R - 2 :].reshape(4, NY), "rows", up)
    after = lax.ppermute(low[:, :2].reshape(4, NY), "rows", down)

    forward = [columns[k] for k in ("forward_a", "forward_b", "forward_b0", "twist")]
    dual_sent = call(dual_kernel, shape((D, 2, 128), BF), [cotangent, *forward])
    dual_got = exchange(dual_sent)

    big = shape((R * HID, NY), BF)
    field_sent, act_one, act_two, slope_one, slope_two, stack = call(
        network_kernel,
        [shape((D, 2, 128), BF), big, big, big, big, shape((48, NY), BF)],
        [velocity, before, after, flat_in, w_mid, flat_out, net["taps"], net["outs"], *forward],
        [pltpu.VMEM((6 * HID, TILE), BF), pltpu.VMEM((24, NY), F32)],
    )
    middle = [rows[k] for k in ("row_forward", "row_inverse", "short_forward", "short_inverse")]
    second_sent = call(
        middle_kernel,
        shape((D, 3, 2, 128), BF),
        [device, dual_got, field_sent, *middle, rows["short_rim"], rows["spin"], rows["spin_rim"]],
        scalars=1,
    )
    second_got = exchange(second_sent)
    third_sent = call(
        backward_kernel,
        shape((D, 2, 2, 128), BF),
        [
            device,
            second_got,
            act_one,
            act_two,
            slope_one,
            slope_two,
            stack,
            w_mid,
            flat_out,
            net["duals"],
            net["place_mid"],
            net["place_in"],
            net["place_out"],
            net["spread"],
            *middle,
            rows["spin"],
            columns["inverse_b"],
            columns["inverse_b0"],
            table_pair(columns["inverse_a"] * scale),
            table_pair(columns["inverse_rim"] * scale),
            columns["untwist"],
            columns["untwist_rim"],
        ],
        [
            pltpu.VMEM((48, NY), BF),
            pltpu.VMEM((HID, HID), F32),
            pltpu.VMEM((R * HID, 48), F32),
            pltpu.VMEM((R * HID, 48), F32),
        ],
        scalars=1,
    )
    third_got = exchange(third_sent)
    total = call(sum_kernel, shape((64, 128), F32), [third_got])
    groups = [[2 * h + core for h in range(64)] for core in range(2)]
    grads = exchange(total.reshape(64, 1, 128), groups).reshape(64, 128)
    new_velocity = call(
        field_kernel,
        shape((CH, R, NY), F32),
        [third_got, columns["inverse_b"], columns["inverse_b0"], table_pair(columns["inverse_a"]), columns["untwist"]],
    )
    grad_mid = grads[:, :64]
    grad_in = grads[:, 64:82].reshape(HID, 3, 3, 2)
    grad_out = grads[:, 82:100].T.reshape(3, 3, 2, HID)
    return new_velocity, grad_in, grad_mid, grad_out


def solution(mesh):
    in_specs = (P("batch", "rows", None), P("batch", "rows", None), P(), P(), P())
    out_specs = (
        P("batch", "rows", None),
        P("batch", None, None, None),
        P("batch", None),
        P("batch", None, None, None),
    )
    return jax.shard_map(body, mesh=mesh, in_specs=in_specs, out_specs=out_specs, check_vma=False)
```

time: 1040 us -> 152 us (0.15); the launches traced: 1020 us -> 150 us
  blocking collectives: 638 us -> 47.2 us
  local copies, waits for them, and re-layouts: 165 us -> 35.2 us
  starting transfers between devices: 122 us -> 24.9 us
  matrix products: 59.9 us -> 0 us
  Pallas kernels: 0 us -> 30.9 us
  other arithmetic: 21.5 us -> 0.93 us
    psum x1 -> x0, blocking collectives: 638 us -> none  [body(): lax.psum((local_in, local_mid, local_out), 'rows')]
    all_to_all x8 -> x2, starting transfers between devices: 110 us -> 21.6 us  [exchange(): lax.all_to_all(x, 'rows', split_axis=0, concat_axis=0, tiled=True, axis_i...]
    dot_general x63 -> x0, matrix products: 59.9 us -> none  [the longest x14 11.9 us: rotate(): out_real = jnp.einsum(form, real, cosine, precision=HIGHEST)]
    unnamed x60 -> x91, local copies, waits for them, and re-layouts: 80.7 us -> 30.9 us
    all_to_all x0 -> x2, blocking collectives: none -> 47.2 us  [exchange(): lax.all_to_all(x, 'rows', split_axis=0, concat_axis=0, tiled=True, axis_i...]
    all_to_all x17 -> x0, local copies, waits for them, and re-layouts: 34.7 us -> none  [the longest x5 15.8 us: spectral_middle(): lax.all_to_all(real, 'rows', split_axis=1, concat_axis=2, tiled=True)]
    pallas_call x0 -> x6, Pallas kernels: none -> 30.9 us  [call(): pl.pallas_call(kernel, out_shape=outputs, in_specs=[smem] * scalars + [vm...]
    reshape x21 -> x7, local copies, waits for them, and re-layouts: 26.5 us -> 3.99 us  [the longest x2 1.4 us: body(): flat_in = w_in.reshape(HID, 18)]
  transfers between devices with their start and end apart: 14 -> 4, of which waited for: 2 -> 2; matrix products, arithmetic and copies ran while one was open for 16% -> 2% of each run, Pallas kernels for 0% -> 9%
where the time goes in v1:
time: 152 us; the launch traced here: 150 us
  blocking collectives  47.2 us (31%)
  local copies, waits for them, and re-layouts  35.2 us (23%)
  Pallas kernels  30.9 us (20%)
  starting transfers between devices  24.9 us (16%)
  waiting for transfers between devices  10.3 us (7%)
    all_to_all x2, blocking collectives, exchange(): lax.all_to_all(x, 'rows', split_axis=0, concat_axis=0, tiled=True, axis_i...  47.2 us
    pallas_call x6, Pallas kernels, call(): pl.pallas_call(kernel, out_shape=outputs, in_specs=[smem] * scalars + [vm...  30.9 us
    unnamed x91, local copies, waits for them, and re-layouts  30.9 us
    all_to_all x2, starting transfers between devices, exchange(): lax.all_to_all(x, 'rows', split_axis=0, concat_axis=0, tiled=True, axis_i...  21.6 us
    all_to_all x2, waiting for transfers between devices, exchange(): lax.all_to_all(x, 'rows', split_axis=0, concat_axis=0, tiled=True, axis_i...  8.41 us
    ppermute x1, starting transfers between devices, body(): before = lax.ppermute(low[:, R - 2:].reshape(4, NY), 'rows', up)  3.21 us
  transfers between devices with their start and end apart: 4, of which 2 were waited for; matrix products, arithmetic and copies ran while one was open for 2% of the time, Pallas kernels for 9%

profile of v1, /device:TPU:1, one launch (start us, length us, event | category | flops | bytes accessed | tf_op | source)
XLA Modules:
  0.0 150.3 jit_solution(617637273547017106)
XLA Ops:
  0.6 0.9 copy-done.1
  1.6 0.9 copy-done.3
  2.5 0.9 copy-done.5
  3.5 0.9 copy-done.15
  4.4 0.9 copy-done.24
  5.3 1.2 shard_map.309
  6.6 17.0 %all-to-all-start = ((bf16[128,2,128]{2,1,0:T(2,128)(2,1)}), bf16[128,2,128]{2,1,0:T(2,128)(2,1)}, u32[]{:S(2)}, u32[]{:S(2)}) async-start(bf16[128,2,128]{2,1,0:T(2,128)(2,1)} %shard_map.309), calls=%async_computation | async-start | bytes 131072 | tf_op jit(solution)/shard_map/all_to_all | solution.py:516
  23.6 0.9 convert_element_type.3
  24.6 3.2 %collective-permute-start = (bf16[4,4096]{1,0:T(4,128)(2,1)S(1)}, bf16[4,4096]{1,0:T(4,128)(2,1)S(1)}, u32[]{:S(2)}, u32[]{:S(2)}) collective-permute-start(bf16[4,4096]{1,0:T(4,128)(2,1)S(1)} %reshape.36), channel_id=1, source_target_pairs={{0,2},{2,4},{4,6},{6,8},{8,10},{10,12},{12,14},{14,16},{16,18},{18... | collective-permute-start | bytes 98312 | tf_op jit(solution)/shard_map/ppermute | solution.py:532
  27.9 1.3 reshape.39.w_out
  31.2 1.9 %collective-permute-done.1.after = bf16[4,4096]{1,0:T(4,128)(2,1)S(1)} collective-permute-done((bf16[4,4096]{1,0:T(4,128)(2,1)S(1)}, bf16[4,4096]{1,0:T(4,128)(2,1)S(1)}, u32[]{:S(2)}, u32[]{:S(2)}) %collective-permute-start.1) | collective-permute-done | bytes 32800 | tf_op jit(solution)/shard_map/ppermute | solution.py:533
  33.8 0.9 copy-done.2
  34.7 0.9 copy-done.4
  35.7 0.9 copy-done.6
  36.6 0.9 copy-done.16
  37.5 0.9 copy-done.17
  43.6 12.3 %shard_map.310 = (bf16[128,2,128]{2,1,0:T(2,128)(2,1)S(1)}, bf16[256,4096]{1,0:T(8,128)(2,1)S(1)}, bf16[256,4096]{1,0:T(8,128)(2,1)S(1)}, bf16[256,4096]{1,0:T(8...) custom-call(f32[2,4,4096]{2,1,0:T(4,128)S(1)} %copy-done.17, bf16[4,4096]{1,0:T(4,128)(2,1)S(1)} %copy-done.40, ...), custom_call_target="tpu_custom_call" | custom-call | tf_op jit(solution)/shard_map/pallas_call | solution.py:505
  55.9 1.4 copy-done
  58.7 0.9 copy-done.14
  59.6 0.9 copy-done.25
  60.5 0.9 copy-done.26
  62.2 2.2 %shard_map.311 = bf16[128,3,2,128]{3,2,1,0:T(2,128)(2,1)S(1)} custom-call(s32[1]{0:T(128)} %bitcast.device, bf16[128,2,128]{2,1,0:T(2,128)(2,1)} %all-to-all-done.got, bf16[128,2,128]{2,1,0:T(2,128)(2,1)S(1)} %copy-done.32, bf16[2,256,256]{2,1,0:T(8,128)(2,1)S(1)} %copy-done.10, bf16[2,256,256]{2,1,0:T(8,128)(2,1)S(1)} %copy-done.9, ...), custom_call_target="tpu_custom_call" | custom-call | tf_op jit(solution)/shard_map/pallas_call | solution.py:505
  64.4 28.1 %all_to_all.20.got = bf16[128,3,2,128]{3,2,1,0:T(2,128)(2,1)S(1)} all-to-all(bf16[128,3,2,128]{3,2,1,0:T(2,128)(2,1)S(1)} %shard_map.311), channel_id=1, replica_groups=mesh['rows'=128,'batch'=2] {'rows'}, dimensions={0} | all-to-all | bytes 393216 | tf_op jit(solution)/shard_map/all_to_all | solution.py:516
  92.5 0.9 copy-done.20
  93.4 0.9 copy-done.22
  94.3 0.9 copy-done.23
  99.8 13.1 %shard_map.312 = bf16[128,2,2,128]{3,2,1,0:T(2,128)(2,1)S(1)} custom-call(s32[1]{0:T(128)} %bitcast.device, bf16[128,3,2,128]{3,2,1,0:T(2,128)(2,1)S(1)} %all_to_all.20.got, bf16[256,4096]{1,0:T(8,128)(2,1)S(1)} %get-tuple-element.11.act_one, bf16[256,4096]{1,0:T(8,128)(2,1)} %copy-done, bf16[256,4096]{1,0:T(8,128)(2,1)} %get-tuple-element.13.slope_one, ...), custom_call_target="tpu_custom_call" | custom-call | tf_op jit(solution)/shard_map/pallas_call | solution.py:505
  112.9 19.2 %all_to_all.21.got = bf16[128,2,2,128]{3,2,1,0:T(2,128)(2,1)S(1)} all-to-all(bf16[128,2,2,128]{3,2,1,0:T(2,128)(2,1)S(1)} %shard_map.312), channel_id=1, replica_groups=mesh['rows'=128,'batch'=2] {'rows'}, dimensions={0} | all-to-all | bytes 262144 | tf_op jit(solution)/shard_map/all_to_all | solution.py:516
  132.9 4.6 %all-to-all-start.3 = ((f32[64,1,128]{2,1,0:T(1,128)}), f32[64,1,128]{2,1,0:T(1,128)S(1)}, u32[]{:S(2)}, u32[]{:S(2)}) async-start(f32[64,1,128]{2,1,0:T(1,128)} %bitcast.2), calls=%async_computation.3 | async-start | bytes 65536 | tf_op jit(solution)/shard_map/all_to_all | solution.py:516
  137.5 0.9 copy-done.21
  138.4 1.4 shard_map.313
  139.8 8.4 %all-to-all-done.3 = f32[64,1,128]{2,1,0:T(1,128)S(1)} async-done(((f32[64,1,128]{2,1,0:T(1,128)}), f32[64,1,128]{2,1,0:T(1,128)S(1)}, u32[]{:S(2)}, u32[]{:S(2)}) %all-to-all-start.3) | async-done | bytes 32800 | tf_op jit(solution)/shard_map/all_to_all | solution.py:516
  (87 shorter events, 17.7 us)
Async XLA Ops:
  0.6 1.0 copy-start.1
  1.6 0.9 copy-start.3
  2.5 0.9 copy-start.5
  3.5 0.9 copy-start.15
  4.4 0.9 copy-start.24
  5.3 53.3 %copy-start.9 = (bf16[2,256,256]{2,1,0:T(8,128)(2,1)S(1)}, bf16[2,256,256]{2,1,0:T(8,128)(2,1)}, u32[]{:S(2)}) copy-start(bf16[2,256,256]{2,1,0:T(8,128)(2,1)} %constant.63.clone.row_inverse) | copy-start | bytes 786436
  5.3 53.3 %copy-start.10 = (bf16[2,256,256]{2,1,0:T(8,128)(2,1)S(1)}, bf16[2,256,256]{2,1,0:T(8,128)(2,1)}, u32[]{:S(2)}) copy-start(bf16[2,256,256]{2,1,0:T(8,128)(2,1)} %constant.62.clone.row_forward) | copy-start | bytes 786436
  5.3 53.3 %copy-start.12 = (f32[2,128,128]{2,1,0:T(8,128)S(1)}, f32[2,128,128]{2,1,0:T(8,128)}, u32[]{:S(2)}) copy-start(f32[2,128,128]{2,1,0:T(8,128)} %constant.67.clone.spin) | copy-start | bytes 393220
  5.3 53.3 %copy-start.13 = (bf16[256,256]{1,0:T(8,128)(2,1)S(1)}, bf16[256,256]{1,0:T(8,128)(2,1)}, u32[]{:S(2)}) copy-start(bf16[256,256]{1,0:T(8,128)(2,1)} %constant.65.clone.short_inverse) | copy-start | bytes 393220
  5.3 87.1 %copy-start.11 = (f32[2,128,128]{2,1,0:T(8,128)S(1)}, f32[2,128,128]{2,1,0:T(8,128)}, u32[]{:S(2)}) copy-start(f32[2,128,128]{2,1,0:T(8,128)} %constant.78.clone.untwist) | copy-start | bytes 393220
  6.6 85.9 %copy-start.7 = (bf16[2,256,256]{2,1,0:T(8,128)(2,1)S(1)}, bf16[2,256,256]{2,1,0:T(8,128)(2,1)}, u32[]{:S(2)}) copy-start(bf16[2,256,256]{2,1,0:T(8,128)(2,1)} %constant.75.clone.inverse_b0) | copy-start | bytes 786436
  6.6 85.9 %copy-start.8 = (bf16[2,256,256]{2,1,0:T(8,128)(2,1)S(1)}, bf16[2,256,256]{2,1,0:T(8,128)(2,1)}, u32[]{:S(2)}) copy-start(bf16[2,256,256]{2,1,0:T(8,128)(2,1)} %constant.74.clone.inverse_b) | copy-start | bytes 786436
  6.6 85.9 %copy-start.29 = (bf16[64,64]{1,0:T(8,128)(2,1)S(1)}, bf16[64,64]{1,0:T(8,128)(2,1)}, u32[]{:S(2)}) copy-start(bf16[64,64]{1,0:T(8,128)(2,1)} %w_mid.3) | copy-start | bytes 24580
  6.6 52.0 %all-to-all-start = ((bf16[128,2,128]{2,1,0:T(2,128)(2,1)}), bf16[128,2,128]{2,1,0:T(2,128)(2,1)}, u32[]{:S(2)}, u32[]{:S(2)}) async-start(bf16[128,2,128]{2,1,0:T(2,128)(2,1)} %shard_map.309), calls=%async_computation | async-start | bytes 131072 | tf_op jit(solution)/shard_map/all_to_all | solution.py:516
  24.6 6.0 %collective-permute-start = (bf16[4,4096]{1,0:T(4,128)(2,1)S(1)}, bf16[4,4096]{1,0:T(4,128)(2,1)S(1)}, u32[]{:S(2)}, u32[]{:S(2)}) collective-permute-start(bf16[4,4096]{1,0:T(4,128)(2,1)S(1)} %reshape.36), channel_id=1, source_target_pairs={{0,2},{2,4},{4,6},{6,8},{8,10},{10,12},{12,14},{14,16},{16,18},{18... | collective-permute-start | bytes 98312 | tf_op jit(solution)/shard_map/ppermute | solution.py:532
  27.8 5.4 %collective-permute-start.1 = (bf16[4,4096]{1,0:T(4,128)(2,1)S(1)}, bf16[4,4096]{1,0:T(4,128)(2,1)S(1)}, u32[]{:S(2)}, u32[]{:S(2)}) collective-permute-start(bf16[4,4096]{1,0:T(4,128)(2,1)S(1)} %reshape.37), channel_id=1, source_target_pairs={{2,0},{4,2},{6,4},{8,6},{10,8},{12,10},{14,12},{16,14},{18,16},{20... | collective-permute-start | bytes 98312 | tf_op jit(solution)/shard_map/ppermute | solution.py:533
  33.8 0.9 copy-start.2
  34.7 0.9 copy-start.4
  35.7 0.9 copy-start.6
  36.6 0.9 copy-start.16
  37.5 0.9 copy-start.17
  55.9 1.4 copy-start
  58.6 0.9 copy-start.14
  59.5 0.9 copy-start.25
  60.5 0.9 copy-start.26
  62.2 30.3 %copy-start.19 = (bf16[48,4096]{1,0:T(8,128)(2,1)S(1)}, bf16[48,4096]{1,0:T(8,128)(2,1)}, u32[]{:S(2)}) copy-start(bf16[48,4096]{1,0:T(8,128)(2,1)} %copy-done.18) | copy-start | bytes 1179652
  92.5 1.0 copy-start.20
  93.4 0.9 copy-start.22
  94.3 0.9 copy-start.23
  95.2 0.8 copy-start.27
  132.9 15.3 %all-to-all-start.3 = ((f32[64,1,128]{2,1,0:T(1,128)}), f32[64,1,128]{2,1,0:T(1,128)S(1)}, u32[]{:S(2)}, u32[]{:S(2)}) async-start(f32[64,1,128]{2,1,0:T(1,128)} %bitcast.2), calls=%async_computation.3 | async-start | bytes 65536 | tf_op jit(solution)/shard_map/all_to_all | solution.py:516
  137.5 1.0 copy-start.21
  (17 other events, 12.3 us)

commit v2 on v1

--- a/solution.py
+++ b/solution.py
@@ -1,3 +1,4 @@
+import functools
 import math
 
 import jax
@@ -14,8 +15,8 @@
 GELU_CUBIC = 0.044715
 BF = jnp.bfloat16
 F32 = jnp.float32
-TILE = 256
-VMEM_LIMIT = 48 * 1024 * 1024
+TILE = 1024
+VMEM_LIMIT = 24 * 1024 * 1024
 
 R = 4
 D = 128
@@ -198,11 +199,6 @@
     place_in[:, :, 64:82] = taps[1:5].transpose(0, 2, 1)
     place_out = np.zeros((R, 48, 128))
     place_out[:, :, 82:100] = duals.transpose(0, 2, 1)
-    spread = np.zeros((64, 2, 2, 2, 64))
-    for h in range(64):
-        for core in range(2):
-            for part in range(2):
-                spread[h, core, part, part, h] = 1
     low = lambda t: t.astype(ml_dtypes.bfloat16)
     return {
         "taps": low(taps),
@@ -211,7 +207,6 @@
         "place_mid": low(place_mid),
         "place_in": low(place_in),
         "place_out": low(place_out),
-        "spread": low(spread.reshape(256, 128)),
     }
 
 
@@ -271,13 +266,7 @@
     return real * cosine - imag * sine, imag * cosine + real * sine
 
 
-def spectral(x, device, row_forward, short_forward, spin):
-    v = pair_low(dot, row_forward, x)
-    real, imag = v[:128], v[128:]
-    cosine, sine = spin[0], spin[1]
-    both = jnp.concatenate([real * cosine + imag * sine, imag * cosine - real * sine], axis=1)
-    high, low = halves(both)
-    full = dot(high, short_forward) + dot(low, short_forward)
+def multiplier(device):
     m1 = lax.broadcasted_iota(jnp.int32, (128, 128), 0)
     lane = lax.broadcasted_iota(jnp.int32, (128, 128), 1)
     m = m1 + 128 * (lane % R)
@@ -295,20 +284,11 @@
     some = square > 0
     inverse = 1.0 / jnp.where(some, square, 1.0)
     same = jnp.where(some, jnp.where(lane < 64, col_square, row_square) * inverse, 1.0)
-    cross = -(wave_row * wave_col) * inverse
-    real, imag = full[:, :128], full[:, 128:]
-    real = same * real + cross * pltpu.roll(real, 64, 1)
-    imag = same * imag + cross * pltpu.roll(imag, 64, 1)
-    return jnp.concatenate([real, imag], axis=1)
-
-
-def row_back(both, row_inverse, short, spin):
-    high, low = halves(both)
-    full = dot(high, short) + dot(low, short)
-    real, imag = full[:, :128], full[:, 128:]
-    cosine, sine = spin[0], spin[1]
-    v = jnp.concatenate([real * cosine - imag * sine, imag * cosine + real * sine], axis=0)
-    return exact(dot, row_inverse, v).astype(BF)
+    return same, -(wave_row * wave_col) * inverse
+
+
+def side_by_side(parts):
+    return jnp.concatenate(parts, axis=1)
 
 
 def gelu_parts(pre):
@@ -328,9 +308,10 @@
 
 
 def network_kernel(
-    velocity,
+    dual_sent,
     before,
     after,
+    velocity,
     w_in,
     w_mid,
     w_out,
@@ -341,6 +322,11 @@
     forward_b0,
     twist,
     sent,
+    act_one_out,
+    act_two_out,
+    slope_one_out,
+    slope_two_out,
+    stack_out,
     act_one,
     act_two,
     slope_one,
@@ -348,7 +334,12 @@
     stack,
     act_all,
     partial,
+    semaphores,
 ):
+    sent[:, 1] = dual_sent[...]
+    held = (act_one, act_two, slope_one, slope_two)
+    homes = (act_one_out, act_two_out, slope_one_out, slope_two_out)
+    whole = pltpu.make_async_copy(stack, stack_out, semaphores.at[4, 0])
     own = jnp.concatenate([velocity[0], velocity[1]], axis=0)
     low_before = before[...].astype(F32)
     low_after = after[...].astype(F32)
@@ -356,6 +347,8 @@
     stack[0:16, :] = pltpu.roll(base, 1, 1).astype(BF)
     stack[16:32, :] = base.astype(BF)
     stack[32:48, :] = pltpu.roll(base, NY - 1, 1).astype(BF)
+    whole.start()
+    velocity, w_out = velocity.ready(), w_out.ready()
     first = jnp.concatenate([dot(w_in[...], taps[i]).astype(BF) for i in range(6)], axis=0)
     third = jnp.concatenate([dot(outs[i], w_out[...]).astype(BF) for i in range(6)], axis=1)
     middle = w_mid[...]
@@ -378,6 +371,8 @@
                 act_two[rows, at] = low
                 slope_two[rows, at] = slope_of(square, gate, value).astype(BF)
         partial[:, at] = dot(third, act_all[...])
+        for k in range(4):
+            pltpu.make_async_copy(held[k].at[:, at], homes[k].at[:, at], semaphores.at[k, index]).start()
         return 0
 
     lax.fori_loop(0, NY // TILE, step, 0)
@@ -398,69 +393,105 @@
         )
     advect = 0.5 * jnp.concatenate(pieces, axis=0)
     provisional = own + STEP_SIZE * (correction - advect)
-    sent[...] = column_forward(provisional, forward_a, forward_b, forward_b0, twist).reshape(D, 2, 128)
+    sent[:, 0] = column_forward(provisional, forward_a, forward_b, forward_b0, twist).reshape(D, 2, 128)
+    whole.wait()
+    for k in range(4):
+        for index in range(NY // TILE):
+            at = pl.ds(index * TILE, TILE)
+            pltpu.make_async_copy(held[k].at[:, at], homes[k].at[:, at], semaphores.at[k, index]).wait()
 
 
 def middle_kernel(
-    device, got, other, row_forward, row_inverse, short_forward, short_inverse, short_rim, spin, spin_rim, sent
+    device, got, row_forward, spin, short_forward, short_inverse, short_rim, spin_rim, row_inverse, sent
 ):
-    both = spectral(got[...].reshape(256, 128), device[0], row_forward, short_forward[...], spin)
-    sent[:, 0] = row_back(both, row_inverse, short_inverse[...], spin).reshape(D, 2, 128)
-    sent[:, 1] = row_back(both, row_inverse, short_rim[...], spin_rim).reshape(D, 2, 128)
-    sent[:, 2] = other[...]
+    same, cross = multiplier(device[0])
+    v = pair_low(dot, row_forward, side_by_side([got[:, k].reshape(256, 128) for k in range(2)]))
+    cosine, sine = spin[0], spin[1]
+    fields = []
+    for k in range(2):
+        real, imag = v[:128, 128 * k : 128 * k + 128], v[128:, 128 * k : 128 * k + 128]
+        fields.append(side_by_side([real * cosine + imag * sine, imag * cosine - real * sine]))
+    high, low = halves(jnp.concatenate(fields, axis=0))
+    full = dot(high, short_forward[...]) + dot(low, short_forward[...])
+    fields = []
+    for k in range(2):
+        part = full[128 * k : 128 * k + 128]
+        real, imag = part[:, :128], part[:, 128:]
+        real = same * real + cross * pltpu.roll(real, 64, 1)
+        imag = same * imag + cross * pltpu.roll(imag, 64, 1)
+        fields.append(side_by_side([real, imag]))
+    high, low = halves(jnp.concatenate(fields, axis=0))
+    full = dot(high, short_inverse[...]) + dot(low, short_inverse[...])
+    rim = dot(high[128:], short_rim[...]) + dot(low[128:], short_rim[...])
+    parts = []
+    for part, (cosine, sine) in (
+        (full[:128], (cosine, sine)),
+        (full[128:], (cosine, sine)),
+        (rim, (spin_rim[0], spin_rim[1])),
+    ):
+        real, imag = part[:, :128], part[:, 128:]
+        parts.append(jnp.concatenate([real * cosine - imag * sine, imag * cosine + real * sine], axis=0))
+    out = exact(dot, row_inverse, side_by_side(parts)).astype(BF)
+    for k in range(3):
+        sent[:, k] = out[:, 128 * k : 128 * k + 128].reshape(D, 2, 128)
 
 
 def backward_kernel(
-    device,
     got,
-    act_one,
-    act_two,
-    slope_one,
-    slope_two,
-    stack,
+    inverse_b,
+    inverse_b0,
+    untwist,
+    untwist_rim,
+    inverse_a,
+    inverse_rim,
     w_mid,
     w_out,
     duals,
     place_mid,
     place_in,
     place_out,
-    spread,
-    row_forward,
-    row_inverse,
-    short_forward,
-    short_inverse,
-    spin,
-    inverse_b,
-    inverse_b0,
-    inverse_a,
-    inverse_rim,
-    untwist,
-    untwist_rim,
+    stack,
+    act_one_home,
+    act_two_home,
+    slope_one_home,
+    slope_two_home,
     sent,
+    act_one,
+    act_two,
+    slope_one,
+    slope_two,
     dual_stack,
     sum_mid,
     sum_in,
     sum_out,
+    semaphores,
 ):
-    both = spectral(got[:, 2].reshape(256, 128), device[0], row_forward, short_forward[...], spin)
-    sent[:, 0] = row_back(both, row_inverse, short_inverse[...], spin).reshape(D, 2, 128)
-    real, imag = column_inverse_first(got[:, 0].reshape(256, 128), inverse_b, inverse_b0, untwist, 64, R)
-    own = exact(dot_nt, inverse_a, jnp.concatenate([real, imag], axis=1))
-    rim = got[:, 1].reshape(256, 128)
+    held = (act_one, act_two, slope_one, slope_two)
+    homes = (act_one_home, act_two_home, slope_one_home, slope_two_home)
+    for index in range(NY // TILE):
+        for k in range(4):
+            at = pl.ds(index * TILE, TILE)
+            pltpu.make_async_copy(homes[k].at[:, at], held[k].at[:, at], semaphores.at[k, index]).start()
+    real, imag = column_inverse_first(got[:, 1].reshape(256, 128), inverse_b, inverse_b0, untwist, 64, R)
+    own = exact(dot_nt, inverse_a, side_by_side([real, imag]))
+    rim = got[:, 2].reshape(256, 128)
     real, imag = column_inverse_first(rim[:, :64], inverse_b, inverse_b0, untwist_rim, 32, 2)
-    rim = exact(dot_nt, inverse_rim, jnp.concatenate([real, imag], axis=1))
+    rim = exact(dot_nt, inverse_rim, side_by_side([real, imag]))
     base = jnp.concatenate([from_blocks(own), from_blocks(rim)], axis=0)
     dual_stack[0:16, :] = pltpu.roll(base, NY - 1, 1).astype(BF)
     dual_stack[16:32, :] = base.astype(BF)
     dual_stack[32:48, :] = pltpu.roll(base, 1, 1).astype(BF)
     spread_out = jnp.concatenate([dot_tn(w_out[...], duals[i]).astype(BF) for i in range(R)], axis=0)
     middle = w_mid[...]
+    stack = stack.ready()
     sum_mid[...] = jnp.zeros_like(sum_mid)
     sum_in[...] = jnp.zeros_like(sum_in)
     sum_out[...] = jnp.zeros_like(sum_out)
 
     def step(index, _):
         at = pl.ds(pl.multiple_of(index * TILE, TILE), TILE)
+        for k in range(4):
+            pltpu.make_async_copy(homes[k].at[:, at], held[k].at[:, at], semaphores.at[k, index]).wait()
         dual = dual_stack[:, at]
         back_two = dot(spread_out, dual)
         delta_two = (back_two * slope_two[:, at].astype(F32)).astype(BF)
@@ -482,34 +513,91 @@
         for i in range(R):
             high, low = halves(source[64 * i : 64 * i + 64, :])
             total = total + (dot(high, place[i]) + dot(low, place[i]))
-    high, low = halves(total)
-    sent[:, 1] = dot(spread[...], jnp.concatenate([high, low], axis=0)).astype(BF).reshape(D, 2, 128)
-
-
-def sum_kernel(got, total):
-    ones = jnp.ones((64, 256), BF)
-    total[...] = dot(ones, got[:, 1].reshape(256, 128))
-
-
-def field_kernel(got, inverse_b, inverse_b0, inverse_a, untwist, field):
+    low = total.astype(BF)
+    for k in range(8):
+        sent[k] = low
+
+
+def partial_sum_kernel(got, sent):
+    total = got[0].astype(F32)
+    for k in range(1, 8):
+        total = total + got[k].astype(F32)
+    low = total.astype(BF)
+    for k in range(16):
+        sent[k] = low
+
+
+def total_kernel(got, grad_mid, grad_in, grad_out):
+    total = got[0].astype(F32)
+    for k in range(1, 16):
+        total = total + got[k].astype(F32)
+    grad_mid[...] = total[:, :64]
+    grad_in[...] = total[:, 64:82]
+    flipped = total.T[82:100]
+    for t in range(9):
+        grad_out[t // 3, t % 3] = flipped[2 * t : 2 * t + 2]
+
+
+def field_kernel(got, inverse_b, inverse_b0, untwist, inverse_a, field):
     real, imag = column_inverse_first(got[:, 0].reshape(256, 128), inverse_b, inverse_b0, untwist, 64, R)
-    x = from_blocks(exact(dot_nt, inverse_a, jnp.concatenate([real, imag], axis=1)))
+    x = from_blocks(exact(dot_nt, inverse_a, side_by_side([real, imag])))
     field[0] = x[:R]
     field[1] = x[R:]
 
 
-def call(kernel, outputs, inputs, scratch=(), scalars=0):
-    vmem = pl.BlockSpec(memory_space=pltpu.VMEM)
-    smem = pl.BlockSpec(memory_space=pltpu.SMEM)
-    single = not isinstance(outputs, list)
-    return pl.pallas_call(
-        kernel,
+class Staged:
+    def __init__(self, copy, ref):
+        self.copy, self.ref, self.waited = copy, ref, False
+
+    def ready(self):
+        if not self.waited:
+            self.copy.wait()
+            self.waited = True
+        return self.ref
+
+    def __getitem__(self, index):
+        return self.ready()[index]
+
+
+def call(kernel, outputs, inputs, scratch=(), scalars=0, staged=0, far=0, far_out=0):
+    count = len(inputs)
+    outputs = outputs if isinstance(outputs, list) else [outputs]
+    spec = lambda space: pl.BlockSpec(memory_space=space)
+    specs = [spec(pltpu.SMEM)] * scalars
+    specs += [spec(pltpu.VMEM)] * (count - scalars - staged - far)
+    specs += [spec(pltpu.HBM)] * (staged + far)
+    out_specs = [spec(pltpu.VMEM)] * (len(outputs) - far_out) + [spec(pltpu.HBM)] * far_out
+    first = count - staged - far
+
+    def run(*refs):
+        given = list(refs[:count])
+        rest = refs[count + len(outputs) :]
+        if staged:
+            for k in range(staged):
+                target = rest[len(scratch) + k]
+                copy = pltpu.make_async_copy(given[first + k], target, rest[-1].at[k])
+                copy.start()
+                given[first + k] = Staged(copy, target)
+        kernel(*given, *refs[count : count + len(outputs)], *rest[: len(scratch)])
+        for k in range(staged):
+            given[first + k].ready()
+
+    held = [pltpu.VMEM(x.shape, x.dtype) for x in inputs[first : first + staged]]
+    pinned = [pltpu.with_memory_space_constraint(jnp.asarray(x), pltpu.HBM) for x in inputs[first:]]
+    inputs = [*inputs[:first], *pinned]
+    far_first = len(outputs) - far_out
+    outputs = outputs[:far_first] + [pltpu.HBM(x.shape, x.dtype) for x in outputs[far_first:]]
+    if staged:
+        held.append(pltpu.SemaphoreType.DMA((staged,)))
+    result = pl.pallas_call(
+        run,
         out_shape=outputs,
-        in_specs=[smem] * scalars + [vmem] * (len(inputs) - scalars),
-        out_specs=vmem if single else [vmem] * len(outputs),
-        scratch_shapes=list(scratch),
+        in_specs=specs,
+        out_specs=out_specs,
+        scratch_shapes=list(scratch) + held,
         compiler_params=pltpu.CompilerParams(vmem_limit_bytes=VMEM_LIMIT),
     )(*inputs)
+    return result if len(outputs) > 1 else result[0]
 
 
 def exchange(x, groups=None):
@@ -533,72 +621,83 @@
     after = lax.ppermute(low[:, :2].reshape(4, NY), "rows", down)
 
     forward = [columns[k] for k in ("forward_a", "forward_b", "forward_b0", "twist")]
-    dual_sent = call(dual_kernel, shape((D, 2, 128), BF), [cotangent, *forward])
-    dual_got = exchange(dual_sent)
+    dual_sent = call(dual_kernel, shape((D, 2, 128), BF), [cotangent, *forward], staged=5)
 
     big = shape((R * HID, NY), BF)
-    field_sent, act_one, act_two, slope_one, slope_two, stack = call(
+    own_tiles = [pltpu.VMEM((R * HID, NY), BF)] * 4
+    first_sent, act_one, act_two, slope_one, slope_two, stack = call(
         network_kernel,
-        [shape((D, 2, 128), BF), big, big, big, big, shape((48, NY), BF)],
-        [velocity, before, after, flat_in, w_mid, flat_out, net["taps"], net["outs"], *forward],
-        [pltpu.VMEM((6 * HID, TILE), BF), pltpu.VMEM((24, NY), F32)],
+        [shape((D, 2, 2, 128), BF), big, big, big, big, shape((48, NY), BF)],
+        [dual_sent, before, after, velocity, flat_in, w_mid, flat_out, net["taps"], net["outs"], *forward],
+        own_tiles
+        + [
+            pltpu.VMEM((48, NY), BF),
+            pltpu.VMEM((6 * HID, TILE), BF),
+            pltpu.VMEM((24, NY), F32),
+            pltpu.SemaphoreType.DMA((5, NY // TILE)),
+        ],
+        staged=10,
+        far_out=5,
     )
-    middle = [rows[k] for k in ("row_forward", "row_inverse", "short_forward", "short_inverse")]
+    first_got = exchange(first_sent)
     second_sent = call(
         middle_kernel,
         shape((D, 3, 2, 128), BF),
-        [device, dual_got, field_sent, *middle, rows["short_rim"], rows["spin"], rows["spin_rim"]],
+        [
+            device,
+            first_got,
+            *[rows[k] for k in ("row_forward", "spin", "short_forward", "short_inverse", "short_rim", "spin_rim")],
+            rows["row_inverse"],
+        ],
         scalars=1,
+        staged=7,
     )
     second_got = exchange(second_sent)
-    third_sent = call(
+    back = [columns[k] for k in ("inverse_b", "inverse_b0", "untwist")]
+    partial = call(
         backward_kernel,
-        shape((D, 2, 2, 128), BF),
+        shape((8, 64, 128), BF),
         [
-            device,
             second_got,
+            *back,
+            columns["untwist_rim"],
+            table_pair(columns["inverse_a"] * scale),
+            table_pair(columns["inverse_rim"] * scale),
+            w_mid,
+            flat_out,
+            *[net[k] for k in ("duals", "place_mid", "place_in", "place_out")],
+            stack,
             act_one,
             act_two,
             slope_one,
             slope_two,
-            stack,
-            w_mid,
-            flat_out,
-            net["duals"],
-            net["place_mid"],
-            net["place_in"],
-            net["place_out"],
-            net["spread"],
-            *middle,
-            rows["spin"],
-            columns["inverse_b"],
-            columns["inverse_b0"],
-            table_pair(columns["inverse_a"] * scale),
-            table_pair(columns["inverse_rim"] * scale),
-            columns["untwist"],
-            columns["untwist_rim"],
         ],
-        [
+        own_tiles
+        + [
             pltpu.VMEM((48, NY), BF),
             pltpu.VMEM((HID, HID), F32),
             pltpu.VMEM((R * HID, 48), F32),
             pltpu.VMEM((R * HID, 48), F32),
+            pltpu.SemaphoreType.DMA((4, NY // TILE)),
         ],
-        scalars=1,
+        staged=13,
+        far=4,
     )
-    third_got = exchange(third_sent)
-    total = call(sum_kernel, shape((64, 128), F32), [third_got])
-    groups = [[2 * h + core for h in range(64)] for core in range(2)]
-    grads = exchange(total.reshape(64, 1, 128), groups).reshape(64, 128)
+    along_z = [[16 * z + r for z in range(8)] for r in range(16)]
+    across_z = [[16 * z + r for r in range(16)] for z in range(8)]
+    partial = call(partial_sum_kernel, shape((16, 64, 128), BF), [exchange(partial, along_z)])
     new_velocity = call(
         field_kernel,
         shape((CH, R, NY), F32),
-        [third_got, columns["inverse_b"], columns["inverse_b0"], table_pair(columns["inverse_a"]), columns["untwist"]],
+        [second_got, *back, table_pair(columns["inverse_a"])],
+        staged=4,
     )
-    grad_mid = grads[:, :64]
-    grad_in = grads[:, 64:82].reshape(HID, 3, 3, 2)
-    grad_out = grads[:, 82:100].T.reshape(3, 3, 2, HID)
-    return new_velocity, grad_in, grad_mid, grad_out
+    grad_mid, grad_in, grad_out = call(
+        total_kernel,
+        [shape((HID, HID), F32), shape((HID, 18), F32), shape((3, 3, 2, HID), F32)],
+        [exchange(partial, across_z)],
+    )
+    return new_velocity, grad_in.reshape(HID, 3, 3, 2), grad_mid, grad_out
 
 
 def solution(mesh):

time: 152 us -> 109 us (0.72); the launches traced: 150 us -> 109 us
  local copies, waits for them, and re-layouts: 35.2 us -> 3.49 us
  blocking collectives: 47.2 us -> 30.1 us
  waiting for transfers between devices: 10.3 us -> 19.2 us
  Pallas kernels: 30.9 us -> 28 us
  starting transfers between devices: 24.9 us -> 26.5 us
    unnamed x91 -> x0, local copies, waits for them, and re-layouts: 30.9 us -> none
    all_to_all x2, blocking collectives: 47.2 us -> 30.1 us  [exchange(): lax.all_to_all(x, 'rows', split_axis=0, concat_axis=0, tiled=True, axis_i...]
    all_to_all x2, waiting for transfers between devices: 8.41 us -> 19.1 us  [exchange(): lax.all_to_all(x, 'rows', split_axis=0, concat_axis=0, tiled=True, axis_i...]
    pallas_call x6 -> x7, Pallas kernels: 30.9 us -> 28 us  [call(): pl.pallas_call(run, out_shape=outputs, in_specs=specs, out_specs=out_spec...]
    ppermute x1, waiting for transfers between devices: 1.94 us -> 0.06 us  [body(): after = lax.ppermute(low[:, :2].reshape(4, NY), 'rows', down)]
  transfers between devices with their start and end apart: 4 -> 4, of which waited for: 2 -> 3; matrix products, arithmetic and copies ran while one was open for 2% -> 3% of each run, Pallas kernels for 9% -> 4%
where the time goes in v2:
time: 109 us
  blocking collectives  30.1 us (28%)
  Pallas kernels  28 us (26%)
  starting transfers between devices  26.5 us (24%)
  waiting for transfers between devices  19.2 us (18%)
  local copies, waits for them, and re-layouts  3.49 us (3%)
    all_to_all x2, blocking collectives, exchange(): lax.all_to_all(x, 'rows', split_axis=0, concat_axis=0, tiled=True, axis_i...  30.1 us
    pallas_call x7, Pallas kernels, call(): pl.pallas_call(run, out_shape=outputs, in_specs=specs, out_specs=out_spec...  28 us
    all_to_all x2, starting transfers between devices, exchange(): lax.all_to_all(x, 'rows', split_axis=0, concat_axis=0, tiled=True, axis_i...  22.2 us
    all_to_all x2, waiting for transfers between devices, exchange(): lax.all_to_all(x, 'rows', split_axis=0, concat_axis=0, tiled=True, axis_i...  19.1 us
    ppermute x1, starting transfers between devices, body(): before = lax.ppermute(low[:, R - 2:].reshape(4, NY), 'rows', up)  4.21 us
  transfers between devices with their start and end apart: 4, of which 3 were waited for; matrix products, arithmetic and copies ran while one was open for 3% of the time, Pallas kernels for 4%

profile of v2, /device:TPU:1, one launch (start us, length us, event | category | flops | bytes accessed | tf_op | source)
XLA Modules:
  0.0 109.0 jit_solution(17059329343310236968)
XLA Ops:
  0.6 0.9 convert_element_type.3
  1.6 4.2 %collective-permute-start = (bf16[4,4096]{1,0:T(4,128)(2,1)S(1)}, bf16[4,4096]{1,0:T(4,128)(2,1)S(1)}, u32[]{:S(2)}, u32[]{:S(2)}) collective-permute-start(bf16[4,4096]{1,0:T(4,128)(2,1)S(1)} %reshape.27), channel_id=1, source_target_pairs={{0,2},{2,4},{4,6},{6,8},{8,10},{10,12},{12,14},{14,16},{16,18},{18... | collective-permute-start | bytes 98312 | tf_op jit(solution)/shard_map/ppermute | solution.py:620
  5.9 0.1 collective-permute-start.1
  6.0 1.3 %reshape.30.refs_6_.refs_8_ = bf16[18,64]{1,0:T(8,128)(2,1)} reshape(bf16[3,3,2,64]{3,2,1,0:T(2,128)(2,1)} %param.33) | data formatting | bytes 4608 | tf_op jit(solution)/shard_map/reshape | solution.py:614
  7.3 0.7 reshape.29
  8.0 0.7 copy.35.refs_4_
  8.7 2.0 %shard_map.300.refs_0_ = bf16[128,2,128]{2,1,0:T(2,128)(2,1)S(1)} custom-call(f32[2,4,4096]{2,1,0:T(4,128)} %refs_0_.1, bf16[2,256,256]{2,1,0:T(8,128)(2,1)} %constant.54.clone.refs_1_.refs_9_, bf16[2,256,256]{2,1,0:T(8,128)(2,1)} %constant.55.clone.refs_2_.refs_10_, bf16[2,256,256]{2,1,0:T(8,128)(2,1)} %constant.56.clone.refs_3_.refs_11_, ...), custom_call_target="tpu_custom_call" | custom-call | tf_op jit(solution)/shard_map/pallas_call | solution.py:592
  10.7 0.0 collective-permute-done.refs_1_
  10.7 0.1 collective-permute-done.1.refs_2_
  10.8 10.9 %shard_map.301 = (bf16[128,2,2,128]{3,2,1,0:T(2,128)(2,1)}, bf16[256,4096]{1,0:T(8,128)(2,1)}, bf16[256,4096]{1,0:T(8,128)(2,1)}, bf16[256,4096]{1,0:T(8,128)(2,...) custom-call(bf16[128,2,128]{2,1,0:T(2,128)(2,1)S(1)} %shard_map.300.refs_0_, ...), custom_call_target="tpu_custom_call" | custom-call | tf_op jit(solution)/shard_map/pallas_call | solution.py:592
  21.7 16.2 %all-to-all-start = ((bf16[128,2,2,128]{3,2,1,0:T(2,128)(2,1)}), bf16[128,2,2,128]{3,2,1,0:T(2,128)(2,1)S(1)}, u32[]{:S(2)}, u32[]{:S(2)}) async-start(bf16[128,2,2,128]{3,2,1,0:T(2,128)(2,1)} %get-tuple-element.13), calls=%async_computation | async-start | bytes 262144 | tf_op jit(solution)/shard_map/all_to_all | solution.py:604
  37.9 13.0 %all-to-all-done.refs_1_ = bf16[128,2,2,128]{3,2,1,0:T(2,128)(2,1)S(1)} async-done(((bf16[128,2,2,128]{3,2,1,0:T(2,128)(2,1)}), bf16[128,2,2,128]{3,2,1,0:T(2,128)(2,1)S(1)}, u32[]{:S(2)}, u32[]{:S(2)}) %all-to-all-start) | async-done | bytes 131104 | tf_op jit(solution)/shard_map/all_to_all | solution.py:604
  50.8 2.7 %shard_map.302 = bf16[128,3,2,128]{3,2,1,0:T(2,128)(2,1)S(1)} custom-call(s32[1]{0:T(128)} %bitcast.refs_0_, bf16[128,2,2,128]{3,2,1,0:T(2,128)(2,1)S(1)} %all-to-all-done.refs_1_, bf16[2,256,256]{2,1,0:T(8,128)(2,1)} %constant.60.clone.refs_2_, f32[2,128,128]{2,1,0:T(8,128)} %constant.61.clone.refs_3_, bf16[256,256]{1,0:T(8,128)(2,1)} %constant.62.clone.refs_4_, ...), custom_call_target="tpu_custom_call" | custom-call | tf_op jit(solution)/shard_map/pallas_call | solution.py:592
  53.5 19.8 %all_to_all.20.refs_0_ = bf16[128,3,2,128]{3,2,1,0:T(2,128)(2,1)S(1)} all-to-all(bf16[128,3,2,128]{3,2,1,0:T(2,128)(2,1)S(1)} %shard_map.302), channel_id=1, replica_groups=mesh['rows'=128,'batch'=2] {'rows'}, dimensions={0} | all-to-all | bytes 393216 | tf_op jit(solution)/shard_map/all_to_all | solution.py:604
  73.3 8.4 %shard_map.304 = bf16[8,64,128]{2,1,0:T(8,128)(2,1)S(1)} custom-call(bf16[128,3,2,128]{3,2,1,0:T(2,128)(2,1)S(1)} %all_to_all.20.refs_0_, bf16[2,256,256]{2,1,0:T(8,128)(2,1)} %constant.67.clone.refs_1_, bf16[2,256,256]{2,1,0:T(8,128)(2,1)} %constant.68.clone.refs_2_, f32[2,128,128]{2,1,0:T(8,128)} %constant.69.clone.refs_3_, ...), custom_call_target="tpu_custom_call" | custom-call | tf_op jit(solution)/shard_map/pallas_call | solution.py:592
  81.7 10.3 %all_to_all.21.refs_0_ = bf16[8,64,128]{2,1,0:T(8,128)(2,1)S(1)} all-to-all(bf16[8,64,128]{2,1,0:T(8,128)(2,1)S(1)} %shard_map.304), channel_id=1, replica_groups={{0,32,64,96,128,160,192,224},{2,34,66,98,130,162,194,226},{4,36,68,100,..., dimensions={0} | all-to-all | bytes 262144 | tf_op jit(solution)/shard_map/all_to_all | solution.py:604
  92.1 0.7 shard_map.305
  92.8 6.0 %all-to-all-start.3 = ((bf16[16,64,128]{2,1,0:T(8,128)(2,1)}), bf16[16,64,128]{2,1,0:T(8,128)(2,1)S(1)}, u32[]{:S(2)}, u32[]{:S(2)}) async-start(bf16[16,64,128]{2,1,0:T(8,128)(2,1)} %shard_map.305), calls=%async_computation.3 | async-start | bytes 524288 | tf_op jit(solution)/shard_map/all_to_all | solution.py:604
  98.8 2.5 %shard_map.303 = f32[2,4,4096]{2,1,0:T(4,128)} custom-call(bf16[128,3,2,128]{3,2,1,0:T(2,128)(2,1)S(1)} %all_to_all.20.refs_0_, bf16[2,256,256]{2,1,0:T(8,128)(2,1)} %constant.67.clone.refs_1_, bf16[2,256,256]{2,1,0:T(8,128)(2,1)} %constant.68.clone.refs_2_, f32[2,128,128]{2,1,0:T(8,128)} %constant.69.clone.refs_3_, bf16[2,256,256]{2,1,0:T(8,128)(2,1)} %constant.77.clone.refs_4_), custom_call_target="tpu_custom_call" | custom-call | tf_op jit(solution)/shard_map/pallas_call | solution.py:592
  101.4 6.2 %all-to-all-done.3.refs_0_ = bf16[16,64,128]{2,1,0:T(8,128)(2,1)S(1)} async-done(((bf16[16,64,128]{2,1,0:T(8,128)(2,1)}), bf16[16,64,128]{2,1,0:T(8,128)(2,1)S(1)}, u32[]{:S(2)}, u32[]{:S(2)}) %all-to-all-start.3) | async-done | bytes 262176 | tf_op jit(solution)/shard_map/all_to_all | solution.py:604
  107.5 0.7 shard_map.306
  108.3 0.1 copy.36
  108.4 0.6 reshape.31
  (3 shorter events, 0.1 us)
Async XLA Ops:
  1.6 9.1 %collective-permute-start = (bf16[4,4096]{1,0:T(4,128)(2,1)S(1)}, bf16[4,4096]{1,0:T(4,128)(2,1)S(1)}, u32[]{:S(2)}, u32[]{:S(2)}) collective-permute-start(bf16[4,4096]{1,0:T(4,128)(2,1)S(1)} %reshape.27), channel_id=1, source_target_pairs={{0,2},{2,4},{4,6},{6,8},{8,10},{10,12},{12,14},{14,16},{16,18},{18... | collective-permute-start | bytes 98312 | tf_op jit(solution)/shard_map/ppermute | solution.py:620
  5.9 4.9 %collective-permute-start.1 = (bf16[4,4096]{1,0:T(4,128)(2,1)S(1)}, bf16[4,4096]{1,0:T(4,128)(2,1)S(1)}, u32[]{:S(2)}, u32[]{:S(2)}) collective-permute-start(bf16[4,4096]{1,0:T(4,128)(2,1)S(1)} %reshape.28), channel_id=1, source_target_pairs={{2,0},{4,2},{6,4},{8,6},{10,8},{12,10},{14,12},{16,14},{18,16},{20... | collective-permute-start | bytes 98312 | tf_op jit(solution)/shard_map/ppermute | solution.py:621
  21.7 29.2 %all-to-all-start = ((bf16[128,2,2,128]{3,2,1,0:T(2,128)(2,1)}), bf16[128,2,2,128]{3,2,1,0:T(2,128)(2,1)S(1)}, u32[]{:S(2)}, u32[]{:S(2)}) async-start(bf16[128,2,2,128]{3,2,1,0:T(2,128)(2,1)} %get-tuple-element.13), calls=%async_computation | async-start | bytes 262144 | tf_op jit(solution)/shard_map/all_to_all | solution.py:604
  92.8 14.7 %all-to-all-start.3 = ((bf16[16,64,128]{2,1,0:T(8,128)(2,1)}), bf16[16,64,128]{2,1,0:T(8,128)(2,1)S(1)}, u32[]{:S(2)}, u32[]{:S(2)}) async-start(bf16[16,64,128]{2,1,0:T(8,128)(2,1)} %shard_map.305), calls=%async_computation.3 | async-start | bytes 524288 | tf_op jit(solution)/shard_map/all_to_all | solution.py:604

commit v3 on v2

--- a/solution.py
+++ b/solution.py
@@ -16,6 +16,7 @@
 BF = jnp.bfloat16
 F32 = jnp.float32
 TILE = 1024
+BACK_TILE = 2048
 VMEM_LIMIT = 24 * 1024 * 1024
 
 R = 4
@@ -26,6 +27,8 @@
 C = OUTER // 2
 CH = 2
 HID = 64
+OWN = R * HID
+STEP_ROWS = (-2, -1, 0, 1)
 
 
 def table_pair(matrix):
@@ -95,10 +98,10 @@
     return {
         "forward_a": table_pair(forward_a),
         "forward_b": table_pair(matrix.reshape(256, 256)),
-        "forward_b0": table_pair(zero.reshape(256, 256)),
+        "forward_b0": table_pair(zero.reshape(256, 256))[0],
         "twist": twist,
         "inverse_b": table_pair(back.reshape(256, 256)),
-        "inverse_b0": table_pair(back_zero.reshape(256, 256)),
+        "inverse_b0": table_pair(back_zero.reshape(256, 256))[0],
         "inverse_a": inverse_a,
         "inverse_rim": inverse_rim,
         "untwist": np.ascontiguousarray(twist.transpose(0, 2, 1)),
@@ -154,59 +157,50 @@
         "short_inverse": short(own, 1.0).reshape(256, 256).astype(ml_dtypes.bfloat16),
         "short_rim": rim_block.reshape(256, 256).astype(ml_dtypes.bfloat16),
         "spin": lanes(own),
-        "spin_rim": lanes(rim),
+        "spin_step": lanes(np.array(STEP_ROWS)),
+        "spin_rim": lanes(rim - 2),
     }
 
 
 def velocity_row(ch, row):
-    if 0 <= row < R:
-        return ch * R + row
-    return 8 + ch * 2 + row + 2 if row < 0 else 12 + ch * 2 + row - R
+    return ch * R + row if row >= 0 else 8 + ch * R + row + R
 
 
 def dual_row(ch, row):
-    if 0 <= row < R:
-        return ch * R + row
-    return 8 + ch * 2 + (0 if row < 0 else 1)
+    if row in STEP_ROWS:
+        return ch * R + row + 2
+    return 8 + ch * 2 + (0 if row < -2 else 1)
 
 
 def network_tables():
+    order = (*STEP_ROWS, -3, 2)
     taps = np.zeros((6, 18, 48))
-    for i in range(-1, 5):
+    for at, i in enumerate(order):
         for a in range(-1, 2):
             for b in range(-1, 2):
                 for ch in range(CH):
                     t = (3 * (a + 1) + b + 1) * 2 + ch
-                    taps[i + 1, t, (b + 1) * 16 + velocity_row(ch, i + a)] = 1
+                    taps[at, t, (b + 1) * 16 + velocity_row(ch, i + a)] = 1
     outs = np.zeros((6, 24, 18))
-    for k in range(-1, 5):
+    for at, k in enumerate(order):
         for a in range(-1, 2):
             i = k - a
-            if 0 <= i < R:
+            if i in STEP_ROWS:
                 for b in range(-1, 2):
                     for o in range(CH):
-                        outs[k + 1, (b + 1) * 8 + o * R + i, (3 * (a + 1) + b + 1) * 2 + o] = 1
+                        outs[at, (b + 1) * 8 + o * R + i + 2, (3 * (a + 1) + b + 1) * 2 + o] = 1
     duals = np.zeros((R, 18, 48))
-    for i in range(R):
+    for at, i in enumerate(STEP_ROWS):
         for a in range(-1, 2):
             for b in range(-1, 2):
                 for o in range(CH):
                     t = (3 * (a + 1) + b + 1) * 2 + o
-                    duals[i, t, (b + 1) * 16 + dual_row(o, i - a)] = 1
-    place_mid = np.zeros((64, 128))
-    place_mid[:, :64] = np.eye(64)
-    place_in = np.zeros((R, 48, 128))
-    place_in[:, :, 64:82] = taps[1:5].transpose(0, 2, 1)
-    place_out = np.zeros((R, 48, 128))
-    place_out[:, :, 82:100] = duals.transpose(0, 2, 1)
+                    duals[at, t, (b + 1) * 16 + dual_row(o, i - a)] = 1
     low = lambda t: t.astype(ml_dtypes.bfloat16)
     return {
         "taps": low(taps),
         "outs": low(outs),
         "duals": low(duals),
-        "place_mid": low(place_mid),
-        "place_in": low(place_in),
-        "place_out": low(place_out),
     }
 
 
@@ -251,14 +245,14 @@
     cosine, sine = twist[0], twist[1]
     both = jnp.concatenate([real * cosine + imag * sine, imag * cosine - real * sine], axis=1)
     general = exact(dot_nt, forward_b, both)
-    zero = exact(dot_nt, forward_b0, both)
+    zero = dot_nt(forward_b0[...], both.astype(BF))
     lane = lax.broadcasted_iota(jnp.int32, general.shape, 1)
     return jnp.where(lane % 64 < R, zero, general).astype(BF)
 
 
 def column_inverse_first(x, inverse_b, inverse_b0, untwist, period, width):
     general = pair_low(dot, inverse_b, x)
-    zero = pair_low(dot, inverse_b0, x)
+    zero = dot(inverse_b0[...], x)
     lane = lax.broadcasted_iota(jnp.int32, general.shape, 1)
     y = jnp.where(lane % period < width, zero, general)
     real, imag = y[:128], y[128:]
@@ -284,11 +278,32 @@
     some = square > 0
     inverse = 1.0 / jnp.where(some, square, 1.0)
     same = jnp.where(some, jnp.where(lane < 64, col_square, row_square) * inverse, 1.0)
-    return same, -(wave_row * wave_col) * inverse
+    sign = jnp.where(lane % 2 == 0, 1.0, -1.0)
+    return sign * same, -sign * (wave_row * wave_col) * inverse
 
 
 def side_by_side(parts):
     return jnp.concatenate(parts, axis=1)
+
+
+def staggered(count, *stages):
+    values = {}
+    for step in range(count + len(stages) - 1):
+        for lag in reversed(range(len(stages))):
+            index = step - lag
+            if 0 <= index < count:
+                values[index] = stages[lag](index, values.get(index))
+
+
+def flat_taps(weights):
+    rows = [weights[t // 3, t % 3].astype(F32) for t in range(9)]
+    return jnp.concatenate(rows, axis=0).astype(BF)
+
+
+def diagonal(block, count):
+    empty = jnp.zeros_like(block)
+    rows = [side_by_side([block if i == k else empty for k in range(count)]) for i in range(count)]
+    return jnp.concatenate(rows, axis=0)
 
 
 def gelu_parts(pre):
@@ -302,25 +317,25 @@
     return gate + value * (1.0 - gate) * (2 * GELU_SCALE + (6 * GELU_SCALE * GELU_CUBIC) * square)
 
 
-def dual_kernel(field, forward_a, forward_b, forward_b0, twist, sent):
+def dual_kernel(field, forward_a, forward_b, forward_b0, twist, *refs):
+    sent = refs[-1]
     x = jnp.concatenate([field[0], field[1]], axis=0)
     sent[...] = column_forward(x, forward_a, forward_b, forward_b0, twist).reshape(D, 2, 128)
 
 
 def network_kernel(
     dual_sent,
-    before,
-    after,
+    above,
+    forward_a,
+    forward_b,
+    forward_b0,
+    twist,
     velocity,
     w_in,
     w_mid,
     w_out,
     taps,
     outs,
-    forward_a,
-    forward_b,
-    forward_b0,
-    twist,
     sent,
     act_one_out,
     act_two_out,
@@ -332,7 +347,6 @@
     slope_one,
     slope_two,
     stack,
-    act_all,
     partial,
     semaphores,
 ):
@@ -340,59 +354,62 @@
     held = (act_one, act_two, slope_one, slope_two)
     homes = (act_one_out, act_two_out, slope_one_out, slope_two_out)
     whole = pltpu.make_async_copy(stack, stack_out, semaphores.at[4, 0])
-    own = jnp.concatenate([velocity[0], velocity[1]], axis=0)
-    low_before = before[...].astype(F32)
-    low_after = after[...].astype(F32)
-    base = jnp.concatenate([own, low_before, low_after], axis=0)
+    low_above = [above[c].astype(F32) for c in range(CH)]
+    base = jnp.concatenate([velocity[0], velocity[1], *low_above], axis=0)
     stack[0:16, :] = pltpu.roll(base, 1, 1).astype(BF)
     stack[16:32, :] = base.astype(BF)
     stack[32:48, :] = pltpu.roll(base, NY - 1, 1).astype(BF)
     whole.start()
-    velocity, w_out = velocity.ready(), w_out.ready()
-    first = jnp.concatenate([dot(w_in[...], taps[i]).astype(BF) for i in range(6)], axis=0)
-    third = jnp.concatenate([dot(outs[i], w_out[...]).astype(BF) for i in range(6)], axis=1)
-    middle = w_mid[...]
-
-    def step(index, _):
-        at = pl.ds(pl.multiple_of(index * TILE, TILE), TILE)
-        pre = dot(first, stack[:, at])
-        for i in range(6):
-            keep = 1 <= i <= R
-            rows = pl.ds(64 * (i - 1), 64)
-            square, gate, value = gelu_parts(pre[64 * i : 64 * i + 64])
-            low = value.astype(BF)
-            if keep:
-                act_one[rows, at] = low
-                slope_one[rows, at] = slope_of(square, gate, value).astype(BF)
-            square, gate, value = gelu_parts(dot(middle, low))
-            low = value.astype(BF)
-            act_all[pl.ds(64 * i, 64), :] = low
-            if keep:
-                act_two[rows, at] = low
-                slope_two[rows, at] = slope_of(square, gate, value).astype(BF)
-        partial[:, at] = dot(third, act_all[...])
+    flat_in, flat_out = flat_taps(w_in), flat_taps(w_out)
+    first = jnp.concatenate([dot_tn(flat_in, taps[i]).astype(BF) for i in range(6)], axis=0)
+    third = side_by_side([dot(outs[i], flat_out).astype(BF) for i in range(6)])
+    middle = diagonal(w_mid[...], R)
+
+    def columns(index):
+        return slice(index * TILE, index * TILE + TILE)
+
+    def layer_one(index, _):
+        return dot(first, stack[:, columns(index)])
+
+    def gelu_one(index, pre):
+        at = columns(index)
+        square, gate, value = gelu_parts(pre[:OWN])
+        low = value.astype(BF)
+        act_one[:, at] = low
+        slope_one[:, at] = slope_of(square, gate, value).astype(BF)
+        return low, gelu_parts(pre[OWN:])[2].astype(BF)
+
+    def layer_two(index, low):
+        return dot(middle, low[0]), dot(middle[:128, :128], low[1])
+
+    def gelu_two(index, pre):
+        at = columns(index)
+        square, gate, value = gelu_parts(pre[0])
+        low = value.astype(BF)
+        act_two[:, at] = low
+        slope_two[:, at] = slope_of(square, gate, value).astype(BF)
         for k in range(4):
             pltpu.make_async_copy(held[k].at[:, at], homes[k].at[:, at], semaphores.at[k, index]).start()
-        return 0
-
-    lax.fori_loop(0, NY // TILE, step, 0)
+        return jnp.concatenate([low, gelu_parts(pre[1])[2].astype(BF)], axis=0)
+
+    def layer_three(index, low):
+        partial[:, columns(index)] = dot(third, low)
+
+    staggered(NY // TILE, layer_one, gelu_one, layer_two, gelu_two, layer_three)
     correction = (
         pltpu.roll(partial[0:8, :], 1, 1) + partial[8:16, :] + pltpu.roll(partial[16:24, :], NY - 1, 1)
     )
-    extended = [
-        jnp.concatenate([low_before[2 * c + 1 : 2 * c + 2], velocity[c], low_after[2 * c : 2 * c + 1]], axis=0)
-        for c in range(CH)
-    ]
-    across = velocity[1]
+    near = [jnp.concatenate([low_above[c][1:], velocity[c][:3]], axis=0) for c in range(CH)]
+    rows = [field[1:5] for field in near]
     pieces = []
     for c in range(CH):
-        flux = extended[0] * extended[c]
-        side = across * velocity[c]
+        flux = near[0] * near[c]
+        side = rows[1] * rows[c]
         pieces.append(
             (flux[2:] - flux[:-2]) + (pltpu.roll(side, NY - 1, 1) - pltpu.roll(side, 1, 1))
         )
     advect = 0.5 * jnp.concatenate(pieces, axis=0)
-    provisional = own + STEP_SIZE * (correction - advect)
+    provisional = jnp.concatenate(rows, axis=0) + STEP_SIZE * (correction - advect)
     sent[:, 0] = column_forward(provisional, forward_a, forward_b, forward_b0, twist).reshape(D, 2, 128)
     whole.wait()
     for k in range(4):
@@ -402,13 +419,14 @@
 
 
 def middle_kernel(
-    device, got, row_forward, spin, short_forward, short_inverse, short_rim, spin_rim, row_inverse, sent
+    device, got, row_forward, spin, spin_step, short_forward, short_inverse, short_rim, spin_rim, row_inverse, sent
 ):
     same, cross = multiplier(device[0])
     v = pair_low(dot, row_forward, side_by_side([got[:, k].reshape(256, 128) for k in range(2)]))
-    cosine, sine = spin[0], spin[1]
+    plain = (spin[0], spin[1])
+    step = (spin_step[0], spin_step[1])
     fields = []
-    for k in range(2):
+    for k, (cosine, sine) in enumerate((step, plain)):
         real, imag = v[:128, 128 * k : 128 * k + 128], v[128:, 128 * k : 128 * k + 128]
         fields.append(side_by_side([real * cosine + imag * sine, imag * cosine - real * sine]))
     high, low = halves(jnp.concatenate(fields, axis=0))
@@ -425,8 +443,8 @@
     rim = dot(high[128:], short_rim[...]) + dot(low[128:], short_rim[...])
     parts = []
     for part, (cosine, sine) in (
-        (full[:128], (cosine, sine)),
-        (full[128:], (cosine, sine)),
+        (full[:128], plain),
+        (full[128:], step),
         (rim, (spin_rim[0], spin_rim[1])),
     ):
         real, imag = part[:, :128], part[:, 128:]
@@ -447,9 +465,7 @@
     w_mid,
     w_out,
     duals,
-    place_mid,
-    place_in,
-    place_out,
+    taps,
     stack,
     act_one_home,
     act_two_home,
@@ -466,11 +482,12 @@
     sum_out,
     semaphores,
 ):
-    held = (act_one, act_two, slope_one, slope_two)
-    homes = (act_one_home, act_two_home, slope_one_home, slope_two_home)
-    for index in range(NY // TILE):
+    held = (slope_two, act_one, act_two, slope_one)
+    homes = (slope_two_home, act_one_home, act_two_home, slope_one_home)
+    count = NY // BACK_TILE
+    for index in range(count):
         for k in range(4):
-            at = pl.ds(index * TILE, TILE)
+            at = pl.ds(index * BACK_TILE, BACK_TILE)
             pltpu.make_async_copy(homes[k].at[:, at], held[k].at[:, at], semaphores.at[k, index]).start()
     real, imag = column_inverse_first(got[:, 1].reshape(256, 128), inverse_b, inverse_b0, untwist, 64, R)
     own = exact(dot_nt, inverse_a, side_by_side([real, imag]))
@@ -481,61 +498,61 @@
     dual_stack[0:16, :] = pltpu.roll(base, NY - 1, 1).astype(BF)
     dual_stack[16:32, :] = base.astype(BF)
     dual_stack[32:48, :] = pltpu.roll(base, 1, 1).astype(BF)
-    spread_out = jnp.concatenate([dot_tn(w_out[...], duals[i]).astype(BF) for i in range(R)], axis=0)
-    middle = w_mid[...]
-    stack = stack.ready()
+    flat_out = flat_taps(w_out)
+    spread_out = jnp.concatenate([dot_tn(flat_out, duals[i]).astype(BF) for i in range(R)], axis=0)
+    middle = diagonal(w_mid[...].T, R)
     sum_mid[...] = jnp.zeros_like(sum_mid)
     sum_in[...] = jnp.zeros_like(sum_in)
     sum_out[...] = jnp.zeros_like(sum_out)
 
     def step(index, _):
-        at = pl.ds(pl.multiple_of(index * TILE, TILE), TILE)
+        at = pl.ds(pl.multiple_of(index * BACK_TILE, BACK_TILE), BACK_TILE)
         for k in range(4):
             pltpu.make_async_copy(homes[k].at[:, at], held[k].at[:, at], semaphores.at[k, index]).wait()
         dual = dual_stack[:, at]
         back_two = dot(spread_out, dual)
         delta_two = (back_two * slope_two[:, at].astype(F32)).astype(BF)
-        hidden = act_one[:, at]
-        wide = lambda t: jnp.concatenate([t[64 * i : 64 * i + 64] for i in range(R)], axis=1)
-        wide_two = wide(delta_two)
-        sum_mid[...] += dot_nt(wide_two, wide(hidden))
-        back_one = dot_tn(middle, wide_two)
-        tall = jnp.concatenate([back_one[:, TILE * i : TILE * i + TILE] for i in range(R)], axis=0)
-        delta_one = (tall * slope_one[:, at].astype(F32)).astype(BF)
+        sum_mid[...] += dot_nt(delta_two, act_one[:, at])
+        delta_one = (dot(middle, delta_two) * slope_one[:, at].astype(F32)).astype(BF)
         sum_in[...] += dot_nt(delta_one, stack[:, at])
         sum_out[...] += dot_nt(act_two[:, at], dual)
         return 0
 
-    lax.fori_loop(0, NY // TILE, step, 0)
-    high, low = halves(sum_mid[...])
-    total = dot(high, place_mid[...]) + dot(low, place_mid[...])
-    for source, place in ((sum_in, place_in), (sum_out, place_out)):
+    lax.fori_loop(0, count, step, 0, unroll=2)
+    mid = sum(sum_mid[64 * i : 64 * i + 64, 64 * i : 64 * i + 64] for i in range(R))
+    flips = []
+    for source, choose in ((sum_in, taps), (sum_out, duals)):
+        flip = jnp.zeros((18, HID), F32)
         for i in range(R):
             high, low = halves(source[64 * i : 64 * i + 64, :])
-            total = total + (dot(high, place[i]) + dot(low, place[i]))
-    low = total.astype(BF)
+            flip = flip + (dot_nt(choose[i], high) + dot_nt(choose[i], low))
+        flips.append(flip)
+    packed = jnp.concatenate([side_by_side([mid[:32], mid[32:]]), side_by_side(flips)], axis=0)
+    low = packed.astype(BF).reshape(25, 2, 128)
     for k in range(8):
         sent[k] = low
 
 
+def added(got, count):
+    total = got[0].astype(F32)
+    for k in range(1, count):
+        total = total + got[k].astype(F32)
+    return total
+
+
 def partial_sum_kernel(got, sent):
-    total = got[0].astype(F32)
-    for k in range(1, 8):
-        total = total + got[k].astype(F32)
-    low = total.astype(BF)
+    low = added(got, 8).astype(BF)
     for k in range(16):
         sent[k] = low
 
 
 def total_kernel(got, grad_mid, grad_in, grad_out):
-    total = got[0].astype(F32)
-    for k in range(1, 16):
-        total = total + got[k].astype(F32)
-    grad_mid[...] = total[:, :64]
-    grad_in[...] = total[:, 64:82]
-    flipped = total.T[82:100]
+    total = added(got, 16).reshape(50, 128)
+    grad_mid[:32] = total[:32, :64]
+    grad_mid[32:] = total[:32, 64:]
     for t in range(9):
-        grad_out[t // 3, t % 3] = flipped[2 * t : 2 * t + 2]
+        grad_out[t // 3, t % 3] = total[32 + 2 * t : 34 + 2 * t, 64:]
+    grad_in[...] = total[32:, :64].T
 
 
 def field_kernel(got, inverse_b, inverse_b0, untwist, inverse_a, field):
@@ -559,7 +576,7 @@
         return self.ready()[index]
 
 
-def call(kernel, outputs, inputs, scratch=(), scalars=0, staged=0, far=0, far_out=0):
+def call(kernel, outputs, inputs, scratch=(), scalars=0, staged=0, kept=0, far=0, far_out=0):
     count = len(inputs)
     outputs = outputs if isinstance(outputs, list) else [outputs]
     spec = lambda space: pl.BlockSpec(memory_space=space)
@@ -567,26 +584,32 @@
     specs += [spec(pltpu.VMEM)] * (count - scalars - staged - far)
     specs += [spec(pltpu.HBM)] * (staged + far)
     out_specs = [spec(pltpu.VMEM)] * (len(outputs) - far_out) + [spec(pltpu.HBM)] * far_out
+    out_specs += [spec(pltpu.VMEM)] * kept
     first = count - staged - far
+    dropped = staged - kept
 
     def run(*refs):
         given = list(refs[:count])
-        rest = refs[count + len(outputs) :]
+        own = len(outputs) - kept
+        targets = refs[count + own : count + own + kept]
+        rest = refs[count + own + kept :]
         if staged:
             for k in range(staged):
-                target = rest[len(scratch) + k]
+                target = rest[len(scratch) + k] if k < dropped else targets[k - dropped]
                 copy = pltpu.make_async_copy(given[first + k], target, rest[-1].at[k])
                 copy.start()
                 given[first + k] = Staged(copy, target)
-        kernel(*given, *refs[count : count + len(outputs)], *rest[: len(scratch)])
+        kernel(*given, *refs[count : count + own], *rest[: len(scratch)])
         for k in range(staged):
             given[first + k].ready()
 
-    held = [pltpu.VMEM(x.shape, x.dtype) for x in inputs[first : first + staged]]
+    held = [pltpu.VMEM(x.shape, x.dtype) for x in inputs[first : first + dropped]]
+    kept_out = [pltpu.VMEM(x.shape, x.dtype) for x in inputs[first + dropped : first + staged]]
     pinned = [pltpu.with_memory_space_constraint(jnp.asarray(x), pltpu.HBM) for x in inputs[first:]]
     inputs = [*inputs[:first], *pinned]
     far_first = len(outputs) - far_out
     outputs = outputs[:far_first] + [pltpu.HBM(x.shape, x.dtype) for x in outputs[far_first:]]
+    outputs += kept_out
     if staged:
         held.append(pltpu.SemaphoreType.DMA((staged,)))
     result = pl.pallas_call(
@@ -600,6 +623,28 @@
     return result if len(outputs) > 1 else result[0]
 
 
+def prefetch(arrays, after):
+    count = len(arrays)
+
+    def run(*refs):
+        targets, semaphores = refs[count + 1 : 2 * count + 1], refs[-1]
+        copies = [pltpu.make_async_copy(refs[k], targets[k], semaphores.at[k]) for k in range(count)]
+        for copy in copies:
+            copy.start()
+        for copy in copies:
+            copy.wait()
+
+    arrays = [jnp.asarray(x) for x in arrays]
+    return pl.pallas_call(
+        run,
+        out_shape=[pltpu.VMEM(x.shape, x.dtype) for x in arrays],
+        in_specs=[pl.BlockSpec(memory_space=pltpu.HBM)] * count + [pl.BlockSpec(memory_space=pl.ANY)],
+        out_specs=[pl.BlockSpec(memory_space=pltpu.VMEM)] * count,
+        scratch_shapes=[pltpu.SemaphoreType.DMA((count,))],
+        compiler_params=pltpu.CompilerParams(vmem_limit_bytes=VMEM_LIMIT),
+    )(*[pltpu.with_memory_space_constraint(x, pltpu.HBM) for x in arrays], after)
+
+
 def exchange(x, groups=None):
     return lax.all_to_all(x, "rows", split_axis=0, concat_axis=0, tiled=True, axis_index_groups=groups)
 
@@ -610,82 +655,70 @@
     net = network_tables()
     scale = STEP_SIZE / math.sqrt(NX * NY)
     shape = jax.ShapeDtypeStruct
-    flat_in = w_in.reshape(HID, 18)
-    flat_out = w_out.reshape(18, HID)
+    w_in = jnp.transpose(w_in, (1, 2, 3, 0))
     device = lax.axis_index("rows").reshape(1)
-    size = D
-    up = [(i, (i + 1) % size) for i in range(size)]
-    down = [(j, i) for i, j in up]
-    low = velocity.astype(BF)
-    before = lax.ppermute(low[:, R - 2 :].reshape(4, NY), "rows", up)
-    after = lax.ppermute(low[:, :2].reshape(4, NY), "rows", down)
+    down = [(i, (i + 1) % D) for i in range(D)]
+    above = lax.ppermute(velocity.astype(BF), "rows", down)
 
     forward = [columns[k] for k in ("forward_a", "forward_b", "forward_b0", "twist")]
-    dual_sent = call(dual_kernel, shape((D, 2, 128), BF), [cotangent, *forward], staged=5)
+    ahead = [*forward, velocity, w_in, w_mid, w_out, net["taps"], net["outs"]]
+    dual_sent, *ahead = call(
+        dual_kernel, shape((D, 2, 128), BF), [cotangent, *ahead], staged=1 + len(ahead), kept=len(ahead)
+    )
 
     big = shape((R * HID, NY), BF)
     own_tiles = [pltpu.VMEM((R * HID, NY), BF)] * 4
     first_sent, act_one, act_two, slope_one, slope_two, stack = call(
         network_kernel,
         [shape((D, 2, 2, 128), BF), big, big, big, big, shape((48, NY), BF)],
-        [dual_sent, before, after, velocity, flat_in, w_mid, flat_out, net["taps"], net["outs"], *forward],
+        [dual_sent, above, *ahead],
         own_tiles
         + [
             pltpu.VMEM((48, NY), BF),
-            pltpu.VMEM((6 * HID, TILE), BF),
             pltpu.VMEM((24, NY), F32),
             pltpu.SemaphoreType.DMA((5, NY // TILE)),
         ],
-        staged=10,
         far_out=5,
     )
     first_got = exchange(first_sent)
+    names = ("row_forward", "spin", "spin_step", "short_forward", "short_inverse", "short_rim", "spin_rim")
+    tables = prefetch([*[rows[k] for k in names], rows["row_inverse"]], first_sent)
     second_sent = call(
-        middle_kernel,
-        shape((D, 3, 2, 128), BF),
-        [
-            device,
-            first_got,
-            *[rows[k] for k in ("row_forward", "spin", "short_forward", "short_inverse", "short_rim", "spin_rim")],
-            rows["row_inverse"],
-        ],
-        scalars=1,
-        staged=7,
+        middle_kernel, shape((D, 3, 2, 128), BF), [device, first_got, *tables], scalars=1
     )
     second_got = exchange(second_sent)
     back = [columns[k] for k in ("inverse_b", "inverse_b0", "untwist")]
-    partial = call(
-        backward_kernel,
-        shape((8, 64, 128), BF),
+    tables = prefetch(
         [
-            second_got,
             *back,
             columns["untwist_rim"],
             table_pair(columns["inverse_a"] * scale),
             table_pair(columns["inverse_rim"] * scale),
             w_mid,
-            flat_out,
-            *[net[k] for k in ("duals", "place_mid", "place_in", "place_out")],
+            w_out,
+            net["duals"],
+            net["taps"],
             stack,
-            act_one,
-            act_two,
-            slope_one,
-            slope_two,
         ],
+        second_sent,
+    )
+    partial = call(
+        backward_kernel,
+        shape((8, 25, 2, 128), BF),
+        [second_got, *tables, act_one, act_two, slope_one, slope_two],
         own_tiles
         + [
             pltpu.VMEM((48, NY), BF),
-            pltpu.VMEM((HID, HID), F32),
+            pltpu.VMEM((OWN, OWN), F32),
             pltpu.VMEM((R * HID, 48), F32),
             pltpu.VMEM((R * HID, 48), F32),
-            pltpu.SemaphoreType.DMA((4, NY // TILE)),
+            pltpu.SemaphoreType.DMA((4, NY // BACK_TILE)),
         ],
-        staged=13,
         far=4,
     )
     along_z = [[16 * z + r for z in range(8)] for r in range(16)]
     across_z = [[16 * z + r for r in range(16)] for z in range(8)]
-    partial = call(partial_sum_kernel, shape((16, 64, 128), BF), [exchange(partial, along_z)])
+    partial = call(partial_sum_kernel, shape((16, 25, 2, 128), BF), [exchange(partial, along_z)])
     new_velocity = call(
         field_kernel,
         shape((CH, R, NY), F32),

time: 109 us -> 99.9 us (0.917)
  blocking collectives: 30.1 us -> 10 us
  waiting for transfers between devices: 19.2 us -> 30.1 us
  starting transfers between devices: 26.5 us -> 32 us
  Pallas kernels: 28 us -> 25 us
  local copies, waits for them, and re-layouts: 3.49 us -> 0.7 us
    all_to_all x2 -> x1, blocking collectives: 30.1 us -> 10 us  [exchange(): lax.all_to_all(x, 'rows', split_axis=0, concat_axis=0, tiled=True, axis_i...]
    all_to_all x2 -> x3, waiting for transfers between devices: 19.1 us -> 30.1 us  [exchange(): lax.all_to_all(x, 'rows', split_axis=0, concat_axis=0, tiled=True, axis_i...]
    pallas_call x7, Pallas kernels: 28 us -> 22.1 us  [call(): pl.pallas_call(run, out_shape=outputs, in_specs=specs, out_specs=out_spec...]
    all_to_all x2 -> x3, starting transfers between devices: 22.2 us -> 27.8 us  [exchange(): lax.all_to_all(x, 'rows', split_axis=0, concat_axis=0, tiled=True, axis_i...]
    pallas_call x0 -> x2, Pallas kernels: none -> 2.91 us  [prefetch(): pl.pallas_call(run, out_shape=[pltpu.VMEM(x.shape, x.dtype) for x in arra...]
    reshape x5 -> x0, local copies, waits for them, and re-layouts: 2.75 us -> none  [the longest x2 1.41 us: body(): flat_in = w_in.reshape(HID, 18)]
    ppermute x2 -> x1, starting transfers between devices: 4.29 us -> 4.21 us  [body(): above = lax.ppermute(velocity.astype(BF), 'rows', down)]
  transfers between devices with their start and end apart: 4 -> 4, of which waited for: 3 -> 3; matrix products, arithmetic and copies ran while one was open for 3% -> 0% of each run, Pallas kernels for 4% -> 7%
where the time goes in v3:
time: 99.9 us; the launch traced here: 99.4 us
  starting transfers between devices  32 us (32%)
  waiting for transfers between devices  30.1 us (30%)
  Pallas kernels  25 us (25%)
  blocking collectives  10 us (10%)
    all_to_all x3, waiting for transfers between devices, exchange(): lax.all_to_all(x, 'rows', split_axis=0, concat_axis=0, tiled=True, axis_i...  30.1 us
    all_to_all x3, starting transfers between devices, exchange(): lax.all_to_all(x, 'rows', split_axis=0, concat_axis=0, tiled=True, axis_i...  27.8 us
    pallas_call x7, Pallas kernels, call(): pl.pallas_call(run, out_shape=outputs, in_specs=specs, out_specs=out_spec...  22.1 us
    all_to_all x1, blocking collectives, exchange(): lax.all_to_all(x, 'rows', split_axis=0, concat_axis=0, tiled=True, axis_i...  10 us
    ppermute x1, starting transfers between devices, body(): above = lax.ppermute(velocity.astype(BF), 'rows', down)  4.21 us
    pallas_call x2, Pallas kernels, prefetch(): pl.pallas_call(run, out_shape=[pltpu.VMEM(x.shape, x.dtype) for x in arra...  2.91 us
  transfers between devices with their start and end apart: 4, of which 3 were waited for; matrix products, arithmetic and copies ran while one was open for 0% of the time, Pallas kernels for 7%

profile of v3, /device:TPU:1, one launch (start us, length us, event | category | flops | bytes accessed | tf_op | source)
XLA Modules:
  0.0 99.4 jit_solution(7837155908293639895)
XLA Ops:
  0.6 0.9 convert_element_type.3
  1.6 4.2 %collective-permute-start = (bf16[2,4,4096]{2,1,0:T(4,128)(2,1)S(1)}, bf16[2,4,4096]{2,1,0:T(4,128)(2,1)S(1)}, u32[]{:S(2)}, u32[]{:S(2)}) collective-permute-start(bf16[2,4,4096]{2,1,0:T(4,128)(2,1)S(1)} %convert_element_type.3), channel_id=1, source_target_pairs={{0,2},{2,4},{4,6},{6,8},{8,10},{10,12},{12,14},{14,16},{16,18},{18... | collective-permute-start | bytes 196616 | tf_op jit(solution)/shard_map/ppermute | solution.py:661
  5.8 2.0 %shard_map.282 = (bf16[128,2,128]{2,1,0:T(2,128)(2,1)S(1)}, bf16[2,256,256]{2,1,0:T(8,128)(2,1)S(1)}, bf16[2,256,256]{2,1,0:T(8,128)(2,1)S(1)}, bf16[256,256]{1,...) custom-call(f32[2,4,4096]{2,1,0:T(4,128)} %refs_0_.3, ...), custom_call_target="tpu_custom_call" | custom-call | tf_op jit(solution)/shard_map/pallas_call | solution.py:615
  7.8 0.0 collective-permute-done.refs_1_
  7.8 8.2 %shard_map.283 = (bf16[128,2,2,128]{3,2,1,0:T(2,128)(2,1)}, bf16[256,4096]{1,0:T(8,128)(2,1)}, bf16[256,4096]{1,0:T(8,128)(2,1)}, bf16[256,4096]{1,0:T(8,128)(2,...) custom-call(bf16[128,2,128]{2,1,0:T(2,128)(2,1)S(1)} %get-tuple-element.43.refs_0_, ...), custom_call_target="tpu_custom_call" | custom-call | tf_op jit(solution)/shard_map/pallas_call | solution.py:615
  16.1 15.4 %all-to-all-start = ((bf16[128,2,2,128]{3,2,1,0:T(2,128)(2,1)}), bf16[128,2,2,128]{3,2,1,0:T(2,128)(2,1)S(1)}, u32[]{:S(2)}, u32[]{:S(2)}) async-start(bf16[128,2,2,128]{3,2,1,0:T(2,128)(2,1)} %get-tuple-element.54.refs_8_), calls=%async_computation | async-start | bytes 262144 | tf_op jit(solution)/shard_map/all_to_all | solution.py:649
  31.5 1.4 %shard_map.284 = (bf16[2,256,256]{2,1,0:T(8,128)(2,1)S(1)}, f32[2,128,128]{2,1,0:T(8,128)S(1)}, f32[2,128,128]{2,1,0:T(8,128)S(1)}, bf16[256,256]{1,0:T(8,128)(2...) custom-call(bf16[2,256,256]{2,1,0:T(8,128)(2,1)} %constant.56.clone., ...), custom_call_target="tpu_custom_call" | custom-call | tf_op jit(solution)/shard_map/pallas_call | solution.py:638
  32.9 11.6 %all-to-all-done.refs_1_ = bf16[128,2,2,128]{3,2,1,0:T(2,128)(2,1)S(1)} async-done(((bf16[128,2,2,128]{3,2,1,0:T(2,128)(2,1)}), bf16[128,2,2,128]{3,2,1,0:T(2,128)(2,1)S(1)}, u32[]{:S(2)}, u32[]{:S(2)}) %all-to-all-start) | async-done | bytes 131104 | tf_op jit(solution)/shard_map/all_to_all | solution.py:649
  44.4 1.9 %shard_map.285.refs_11_ = bf16[128,3,2,128]{3,2,1,0:T(2,128)(2,1)} custom-call(s32[1]{0:T(128)} %bitcast.refs_0_, bf16[128,2,2,128]{3,2,1,0:T(2,128)(2,1)S(1)} %all-to-all-done.refs_1_, bf16[2,256,256]{2,1,0:T(8,128)(2,1)S(1)} %get-tuple-element.55.refs_2_, f32[2,128,128]{2,1,0:T(8,128)S(1)} %get-tuple-element.56.refs_3_, ...), custom_call_target="tpu_custom_call" | custom-call | tf_op jit(solution)/shard_map/pallas_call | solution.py:615
  46.3 6.5 %all-to-all-start.1 = ((bf16[128,3,2,128]{3,2,1,0:T(2,128)(2,1)}), bf16[128,3,2,128]{3,2,1,0:T(2,128)(2,1)S(1)}, u32[]{:S(2)}, u32[]{:S(2)}) async-start(bf16[128,3,2,128]{3,2,1,0:T(2,128)(2,1)} %shard_map.285.refs_11_), calls=%async_computation.1 | async-start | bytes 393216 | tf_op jit(solution)/shard_map/all_to_all | solution.py:649
  52.8 1.5 %shard_map.287 = (bf16[2,256,256]{2,1,0:T(8,128)(2,1)S(1)}, bf16[256,256]{1,0:T(8,128)(2,1)S(1)}, f32[2,128,128]{2,1,0:T(8,128)S(1)}, f32[2,128,64]{2,1,0:T(8,12...) custom-call(bf16[2,256,256]{2,1,0:T(8,128)(2,1)} %constant.64.clone., ...), custom_call_target="tpu_custom_call" | custom-call | tf_op jit(solution)/shard_map/pallas_call | solution.py:638
  54.3 12.6 %all-to-all-done.1.refs_0_ = bf16[128,3,2,128]{3,2,1,0:T(2,128)(2,1)S(1)} async-done(((bf16[128,3,2,128]{3,2,1,0:T(2,128)(2,1)}), bf16[128,3,2,128]{3,2,1,0:T(2,128)(2,1)S(1)}, u32[]{:S(2)}, u32[]{:S(2)}) %all-to-all-start.1) | async-done | bytes 196640 | tf_op jit(solution)/shard_map/all_to_all | solution.py:649
  66.9 6.0 %shard_map.288 = bf16[8,25,2,128]{3,2,1,0:T(2,128)(2,1)S(1)} custom-call(bf16[128,3,2,128]{3,2,1,0:T(2,128)(2,1)S(1)} %all-to-all-done.1.refs_0_, bf16[2,256,256]{2,1,0:T(8,128)(2,1)S(1)} %get-tuple-element.64.refs_1_, bf16[256,256]{1,0:T(8,128)(2,1)S(1)} %get-tuple-element.65.refs_2_, f32[2,128,128]{2,1,0:T(8,128)S(1)} %get-tuple-element.66.refs_3_, ...), custom_call_target="tpu_custom_call" | custom-call | tf_op jit(solution)/shard_map/pallas_call | solution.py:615
  72.9 10.0 %all_to_all.20.refs_0_ = bf16[8,25,2,128]{3,2,1,0:T(2,128)(2,1)S(1)} all-to-all(bf16[8,25,2,128]{3,2,1,0:T(2,128)(2,1)S(1)} %shard_map.288), channel_id=1, replica_groups={{0,32,64,96,128,160,192,224},{2,34,66,98,130,162,194,226},{4,36,68,100,..., dimensions={0} | all-to-all | bytes 204800 | tf_op jit(solution)/shard_map/all_to_all | solution.py:649
  82.9 0.8 shard_map.289
  83.7 5.9 %all-to-all-start.3 = ((bf16[16,25,2,128]{3,2,1,0:T(2,128)(2,1)}), bf16[16,25,2,128]{3,2,1,0:T(2,128)(2,1)S(1)}, u32[]{:S(2)}, u32[]{:S(2)}) async-start(bf16[16,25,2,128]{3,2,1,0:T(2,128)(2,1)} %shard_map.289), calls=%async_computation.3 | async-start | bytes 409600 | tf_op jit(solution)/shard_map/all_to_all | solution.py:649
  89.6 2.4 %shard_map.286 = f32[2,4,4096]{2,1,0:T(4,128)} custom-call(bf16[128,3,2,128]{3,2,1,0:T(2,128)(2,1)S(1)} %all-to-all-done.1.refs_0_, bf16[2,256,256]{2,1,0:T(8,128)(2,1)} %constant.64.clone.refs_1_.refs_0_, bf16[256,256]{1,0:T(8,128)(2,1)} %constant.65.clone.refs_2_.refs_1_, f32[2,128,128]{2,1,0:T(8,128)} %constant.66.clone.refs_3_.refs_2_, ...), custom_call_target="tpu_custom_call" | custom-call | tf_op jit(solution)/shard_map/pallas_call | solution.py:615
  92.1 5.9 %all-to-all-done.3.refs_0_ = bf16[16,25,2,128]{3,2,1,0:T(2,128)(2,1)S(1)} async-done(((bf16[16,25,2,128]{3,2,1,0:T(2,128)(2,1)}), bf16[16,25,2,128]{3,2,1,0:T(2,128)(2,1)S(1)}, u32[]{:S(2)}, u32[]{:S(2)}) %all-to-all-start.3) | async-done | bytes 204832 | tf_op jit(solution)/shard_map/all_to_all | solution.py:649
  97.9 0.8 shard_map.290
  98.7 0.1 copy.32
  98.8 0.6 reshape.15
Async XLA Ops:
  1.6 6.3 %collective-permute-start = (bf16[2,4,4096]{2,1,0:T(4,128)(2,1)S(1)}, bf16[2,4,4096]{2,1,0:T(4,128)(2,1)S(1)}, u32[]{:S(2)}, u32[]{:S(2)}) collective-permute-start(bf16[2,4,4096]{2,1,0:T(4,128)(2,1)S(1)} %convert_element_type.3), channel_id=1, source_target_pairs={{0,2},{2,4},{4,6},{6,8},{8,10},{10,12},{12,14},{14,16},{16,18},{18... | collective-permute-start | bytes 196616 | tf_op jit(solution)/shard_map/ppermute | solution.py:661
  16.1 28.4 %all-to-all-start = ((bf16[128,2,2,128]{3,2,1,0:T(2,128)(2,1)}), bf16[128,2,2,128]{3,2,1,0:T(2,128)(2,1)S(1)}, u32[]{:S(2)}, u32[]{:S(2)}) async-start(bf16[128,2,2,128]{3,2,1,0:T(2,128)(2,1)} %get-tuple-element.54.refs_8_), calls=%async_computation | async-start | bytes 262144 | tf_op jit(solution)/shard_map/all_to_all | solution.py:649
  46.3 20.6 %all-to-all-start.1 = ((bf16[128,3,2,128]{3,2,1,0:T(2,128)(2,1)}), bf16[128,3,2,128]{3,2,1,0:T(2,128)(2,1)S(1)}, u32[]{:S(2)}, u32[]{:S(2)}) async-start(bf16[128,3,2,128]{3,2,1,0:T(2,128)(2,1)} %shard_map.285.refs_11_), calls=%async_computation.1 | async-start | bytes 393216 | tf_op jit(solution)/shard_map/all_to_all | solution.py:649
  83.7 14.2 %all-to-all-start.3 = ((bf16[16,25,2,128]{3,2,1,0:T(2,128)(2,1)}), bf16[16,25,2,128]{3,2,1,0:T(2,128)(2,1)S(1)}, u32[]{:S(2)}, u32[]{:S(2)}) async-start(bf16[16,25,2,128]{3,2,1,0:T(2,128)(2,1)} %shard_map.289), calls=%async_computation.3 | async-start | bytes 409600 | tf_op jit(solution)/shard_map/all_to_all | solution.py:649

commit v4 on v3

--- a/solution.py
+++ b/solution.py
@@ -17,7 +17,7 @@
 F32 = jnp.float32
 TILE = 1024
 BACK_TILE = 2048
-VMEM_LIMIT = 24 * 1024 * 1024
+VMEM_LIMIT = 32 * 1024 * 1024
 
 R = 4
 D = 128
@@ -29,6 +29,8 @@
 HID = 64
 OWN = R * HID
 STEP_ROWS = (-2, -1, 0, 1)
+LATE_ROWS = (-2, -1, 0, -3)
+EARLY_ROWS = (1, 2)
 
 
 def table_pair(matrix):
@@ -173,7 +175,7 @@
 
 
 def network_tables():
-    order = (*STEP_ROWS, -3, 2)
+    order = (*LATE_ROWS, *EARLY_ROWS)
     taps = np.zeros((6, 18, 48))
     for at, i in enumerate(order):
         for a in range(-1, 2):
@@ -197,8 +199,11 @@
                     t = (3 * (a + 1) + b + 1) * 2 + o
                     duals[at, t, (b + 1) * 16 + dual_row(o, i - a)] = 1
     low = lambda t: t.astype(ml_dtypes.bfloat16)
+    inner = taps.reshape(6, 18, 3, 16)[4:, :, :, :8].reshape(2, 18, 24)
     return {
         "taps": low(taps),
+        "taps_inner": low(inner),
+        "taps_step": low(taps[[0, 1, 2, 4]]),
         "outs": low(outs),
         "duals": low(duals),
     }
@@ -250,11 +255,11 @@
     return jnp.where(lane % 64 < R, zero, general).astype(BF)
 
 
-def column_inverse_first(x, inverse_b, inverse_b0, untwist, period, width):
+def column_inverse_first(x, inverse_b, inverse_b0, untwist):
     general = pair_low(dot, inverse_b, x)
     zero = dot(inverse_b0[...], x)
     lane = lax.broadcasted_iota(jnp.int32, general.shape, 1)
-    y = jnp.where(lane % period < width, zero, general)
+    y = jnp.where(lane % 64 < R, zero, general)
     real, imag = y[:128], y[128:]
     cosine, sine = untwist[0], untwist[1]
     return real * cosine - imag * sine, imag * cosine + real * sine
@@ -317,14 +322,57 @@
     return gate + value * (1.0 - gate) * (2 * GELU_SCALE + (6 * GELU_SCALE * GELU_CUBIC) * square)
 
 
-def dual_kernel(field, forward_a, forward_b, forward_b0, twist, *refs):
-    sent = refs[-1]
+def early_kernel(
+    field,
+    forward_a,
+    forward_b,
+    forward_b0,
+    twist,
+    velocity,
+    w_in,
+    w_mid,
+    w_out,
+    taps,
+    outs,
+    taps_inner,
+    sent,
+    early_one,
+    early_two,
+    inner,
+):
     x = jnp.concatenate([field[0], field[1]], axis=0)
     sent[...] = column_forward(x, forward_a, forward_b, forward_b0, twist).reshape(D, 2, 128)
+    base = jnp.concatenate([velocity[0], velocity[1]], axis=0)
+    shifts = [pltpu.roll(base, 1, 1), base, pltpu.roll(base, NY - 1, 1)]
+    inner[...] = jnp.concatenate(shifts, axis=0).astype(BF)
+    flat_in = flat_taps(w_in.ready())
+    first = jnp.concatenate([dot_tn(flat_in, taps_inner[i]).astype(BF) for i in range(2)], axis=0)
+    middle = diagonal(w_mid[...], 2)
+
+    def columns(index):
+        return slice(index * TILE, index * TILE + TILE)
+
+    def layer_one(index, _):
+        return dot(first, inner[:, columns(index)])
+
+    def gelu_one(index, pre):
+        low = gelu_parts(pre)[2].astype(BF)
+        early_one[:, columns(index)] = low[:HID]
+        return low
+
+    def layer_two(index, low):
+        return dot(middle, low)
+
+    def gelu_two(index, pre):
+        early_two[:, columns(index)] = gelu_parts(pre)[2].astype(BF)
+
+    staggered(NY // TILE, layer_one, gelu_one, layer_two, gelu_two)
 
 
 def network_kernel(
     dual_sent,
+    early_one,
+    early_two,
     above,
     forward_a,
     forward_b,
@@ -336,32 +384,33 @@
     w_out,
     taps,
     outs,
+    _,
     sent,
+    stack,
     act_one_out,
     act_two_out,
-    slope_one_out,
-    slope_two_out,
-    stack_out,
     act_one,
     act_two,
-    slope_one,
-    slope_two,
-    stack,
     partial,
     semaphores,
 ):
     sent[:, 1] = dual_sent[...]
-    held = (act_one, act_two, slope_one, slope_two)
-    homes = (act_one_out, act_two_out, slope_one_out, slope_two_out)
-    whole = pltpu.make_async_copy(stack, stack_out, semaphores.at[4, 0])
-    low_above = [above[c].astype(F32) for c in range(CH)]
-    base = jnp.concatenate([velocity[0], velocity[1], *low_above], axis=0)
+    mine = 3 * HID
+    ready = [
+        pltpu.make_async_copy(early_one, act_one_out.at[mine:], semaphores.at[2, 0]),
+        pltpu.make_async_copy(early_two.at[:HID], act_two_out.at[mine:], semaphores.at[2, 1]),
+    ]
+    for copy in ready:
+        copy.start()
+    held = (act_one, act_two)
+    homes = (act_one_out, act_two_out)
+    upper = [above[c] for c in range(CH)]
+    base = jnp.concatenate([velocity[0], velocity[1], *upper], axis=0)
     stack[0:16, :] = pltpu.roll(base, 1, 1).astype(BF)
     stack[16:32, :] = base.astype(BF)
     stack[32:48, :] = pltpu.roll(base, NY - 1, 1).astype(BF)
-    whole.start()
     flat_in, flat_out = flat_taps(w_in), flat_taps(w_out)
-    first = jnp.concatenate([dot_tn(flat_in, taps[i]).astype(BF) for i in range(6)], axis=0)
+    first = jnp.concatenate([dot_tn(flat_in, taps[i]).astype(BF) for i in range(4)], axis=0)
     third = side_by_side([dot(outs[i], flat_out).astype(BF) for i in range(6)])
     middle = diagonal(w_mid[...], R)
 
@@ -372,34 +421,32 @@
         return dot(first, stack[:, columns(index)])
 
     def gelu_one(index, pre):
-        at = columns(index)
-        square, gate, value = gelu_parts(pre[:OWN])
-        low = value.astype(BF)
-        act_one[:, at] = low
-        slope_one[:, at] = slope_of(square, gate, value).astype(BF)
-        return low, gelu_parts(pre[OWN:])[2].astype(BF)
+        low = gelu_parts(pre)[2].astype(BF)
+        act_one[:, columns(index)] = low[:mine]
+        return low
 
     def layer_two(index, low):
-        return dot(middle, low[0]), dot(middle[:128, :128], low[1])
+        return dot(middle, low)
 
     def gelu_two(index, pre):
         at = columns(index)
-        square, gate, value = gelu_parts(pre[0])
-        low = value.astype(BF)
-        act_two[:, at] = low
-        slope_two[:, at] = slope_of(square, gate, value).astype(BF)
-        for k in range(4):
-            pltpu.make_async_copy(held[k].at[:, at], homes[k].at[:, at], semaphores.at[k, index]).start()
-        return jnp.concatenate([low, gelu_parts(pre[1])[2].astype(BF)], axis=0)
+        low = gelu_parts(pre)[2].astype(BF)
+        act_two[:, at] = low[:mine]
+        for k in range(2):
+            pltpu.make_async_copy(
+                held[k].at[:, at], homes[k].at[:mine, at], semaphores.at[k, index]
+            ).start()
+        return low
 
     def layer_three(index, low):
-        partial[:, columns(index)] = dot(third, low)
+        at = columns(index)
+        partial[:, at] = dot(third[:, :OWN], low) + dot(third[:, OWN:], early_two[:, at])
 
     staggered(NY // TILE, layer_one, gelu_one, layer_two, gelu_two, layer_three)
     correction = (
         pltpu.roll(partial[0:8, :], 1, 1) + partial[8:16, :] + pltpu.roll(partial[16:24, :], NY - 1, 1)
     )
-    near = [jnp.concatenate([low_above[c][1:], velocity[c][:3]], axis=0) for c in range(CH)]
+    near = [jnp.concatenate([upper[c][1:], velocity[c][:3]], axis=0) for c in range(CH)]
     rows = [field[1:5] for field in near]
     pieces = []
     for c in range(CH):
@@ -411,11 +458,12 @@
     advect = 0.5 * jnp.concatenate(pieces, axis=0)
     provisional = jnp.concatenate(rows, axis=0) + STEP_SIZE * (correction - advect)
     sent[:, 0] = column_forward(provisional, forward_a, forward_b, forward_b0, twist).reshape(D, 2, 128)
-    whole.wait()
-    for k in range(4):
+    for copy in ready:
+        copy.wait()
+    for k in range(2):
         for index in range(NY // TILE):
             at = pl.ds(index * TILE, TILE)
-            pltpu.make_async_copy(held[k].at[:, at], homes[k].at[:, at], semaphores.at[k, index]).wait()
+            pltpu.make_async_copy(held[k].at[:, at], homes[k].at[:mine, at], semaphores.at[k, index]).wait()
 
 
 def middle_kernel(
@@ -459,7 +507,6 @@
     inverse_b,
     inverse_b0,
     untwist,
-    untwist_rim,
     inverse_a,
     inverse_rim,
     w_mid,
@@ -485,15 +532,24 @@
     held = (slope_two, act_one, act_two, slope_one)
     homes = (slope_two_home, act_one_home, act_two_home, slope_one_home)
     count = NY // BACK_TILE
-    for index in range(count):
+
+    def fetch(index):
+        at = pl.ds(pl.multiple_of(index * BACK_TILE, BACK_TILE), BACK_TILE)
         for k in range(4):
-            at = pl.ds(index * BACK_TILE, BACK_TILE)
             pltpu.make_async_copy(homes[k].at[:, at], held[k].at[:, at], semaphores.at[k, index]).start()
-    real, imag = column_inverse_first(got[:, 1].reshape(256, 128), inverse_b, inverse_b0, untwist, 64, R)
-    own = exact(dot_nt, inverse_a, side_by_side([real, imag]))
-    rim = got[:, 2].reshape(256, 128)
-    real, imag = column_inverse_first(rim[:, :64], inverse_b, inverse_b0, untwist_rim, 32, 2)
-    rim = exact(dot_nt, inverse_rim, side_by_side([real, imag]))
+
+    fetch(0)
+    both = side_by_side([got[:, 1].reshape(256, 128), got[:, 2].reshape(256, 128)])
+    general = pair_low(dot, inverse_b, both)
+    zero = dot(inverse_b0[...], both)
+    lane = lax.broadcasted_iota(jnp.int32, general.shape, 1)
+    beyond = jnp.where(lane < 128, lane % 64 - R, lane % 32 - 2)
+    y = jnp.where(beyond < 0, zero, general)
+    real, imag = y[:128], y[128:]
+    cosine, sine = untwist[0], untwist[1]
+    real, imag = real * cosine - imag * sine, imag * cosine + real * sine
+    own = exact(dot_nt, inverse_a, side_by_side([real[:, :128], imag[:, :128]]))
+    rim = exact(dot_nt, inverse_rim, side_by_side([real[:, 128:192], imag[:, 128:192]]))
     base = jnp.concatenate([from_blocks(own), from_blocks(rim)], axis=0)
     dual_stack[0:16, :] = pltpu.roll(base, NY - 1, 1).astype(BF)
     dual_stack[16:32, :] = base.astype(BF)
@@ -507,15 +563,22 @@
 
     def step(index, _):
         at = pl.ds(pl.multiple_of(index * BACK_TILE, BACK_TILE), BACK_TILE)
-        for k in range(4):
+        @pl.when(index + 1 < count)
+        def _():
+            fetch(index + 1)
+
+        def arrived(k):
             pltpu.make_async_copy(homes[k].at[:, at], held[k].at[:, at], semaphores.at[k, index]).wait()
+            return held[k][:, at]
+
         dual = dual_stack[:, at]
         back_two = dot(spread_out, dual)
-        delta_two = (back_two * slope_two[:, at].astype(F32)).astype(BF)
-        sum_mid[...] += dot_nt(delta_two, act_one[:, at])
-        delta_one = (dot(middle, delta_two) * slope_one[:, at].astype(F32)).astype(BF)
+        delta_two = (back_two * arrived(0)).astype(BF)
+        sum_mid[...] += dot_nt(delta_two, arrived(1))
+        back_one = dot(middle, delta_two)
+        sum_out[...] += dot_nt(arrived(2), dual)
+        delta_one = (back_one * arrived(3)).astype(BF)
         sum_in[...] += dot_nt(delta_one, stack[:, at])
-        sum_out[...] += dot_nt(act_two[:, at], dual)
         return 0
 
     lax.fori_loop(0, count, step, 0, unroll=2)
@@ -551,12 +614,13 @@
     grad_mid[:32] = total[:32, :64]
     grad_mid[32:] = total[:32, 64:]
     for t in range(9):
-        grad_out[t // 3, t % 3] = total[32 + 2 * t : 34 + 2 * t, 64:]
-    grad_in[...] = total[32:, :64].T
+        pair = total[32 + 2 * t : 34 + 2 * t]
+        grad_in[t // 3, t % 3] = pair[:, :64]
+        grad_out[t // 3, t % 3] = pair[:, 64:]
 
 
 def field_kernel(got, inverse_b, inverse_b0, untwist, inverse_a, field):
-    real, imag = column_inverse_first(got[:, 0].reshape(256, 128), inverse_b, inverse_b0, untwist, 64, R)
+    real, imag = column_inverse_first(got[:, 0].reshape(256, 128), inverse_b, inverse_b0, untwist)
     x = from_blocks(exact(dot_nt, inverse_a, side_by_side([real, imag])))
     field[0] = x[:R]
     field[1] = x[R:]
@@ -623,26 +687,58 @@
     return result if len(outputs) > 1 else result[0]
 
 
-def prefetch(arrays, after):
-    count = len(arrays)
+def slope_one_kernel(stack, w_in, taps):
+    flat_in = flat_taps(w_in)
+    first = jnp.concatenate([dot_tn(flat_in, taps[i]).astype(BF) for i in range(R)], axis=0)
+    return lambda at: slope_of(*gelu_parts(dot(first, stack[:, at])))
+
+
+def slope_two_kernel(act_one, w_mid):
+    middle = diagonal(w_mid[...], R)
+    return lambda at: slope_of(*gelu_parts(dot(middle, act_one[:, at])))
+
+
+def prefetch(arrays, after, maker, inputs, near=()):
+    count, given = len(arrays), len(inputs)
 
     def run(*refs):
-        targets, semaphores = refs[count + 1 : 2 * count + 1], refs[-1]
-        copies = [pltpu.make_async_copy(refs[k], targets[k], semaphores.at[k]) for k in range(count)]
-        for copy in copies:
-            copy.start()
-        for copy in copies:
+        sources, close, refs = refs[: count + given], refs[count + given + 1 :][: len(near)], refs[count + given + 1 + len(near) :]
+        targets, slope_out, refs = refs[:count], refs[count], refs[count + 1 :]
+        held, slope, semaphores, out_semaphores = refs[:given], *refs[given:]
+        copies = []
+        for k in list(range(count, count + given)) + list(range(count)):
+            target = targets[k] if k < count else held[k - count]
+            copies.append(pltpu.make_async_copy(sources[k], target, semaphores.at[k]))
+            copies[-1].start()
+        for copy in copies[:given]:
             copy.wait()
-
-    arrays = [jnp.asarray(x) for x in arrays]
-    return pl.pallas_call(
+        slopes = maker(*close, *held)
+        stores = []
+        for index in range(NY // TILE):
+            at = slice(index * TILE, index * TILE + TILE)
+            slope[:, at] = slopes(at)
+            stores.append(pltpu.make_async_copy(slope.at[:, at], slope_out.at[:, at], out_semaphores.at[index]))
+            stores[-1].start()
+        for copy in copies[given:] + stores:
+            copy.wait()
+
+    arrays = [jnp.asarray(x) for x in [*arrays, *inputs]]
+    *tables, slope = pl.pallas_call(
         run,
-        out_shape=[pltpu.VMEM(x.shape, x.dtype) for x in arrays],
-        in_specs=[pl.BlockSpec(memory_space=pltpu.HBM)] * count + [pl.BlockSpec(memory_space=pl.ANY)],
-        out_specs=[pl.BlockSpec(memory_space=pltpu.VMEM)] * count,
-        scratch_shapes=[pltpu.SemaphoreType.DMA((count,))],
+        out_shape=[pltpu.VMEM(x.shape, x.dtype) for x in arrays[:count]] + [pltpu.HBM((OWN, NY), F32)],
+        in_specs=[pl.BlockSpec(memory_space=pltpu.HBM)] * (count + given)
+        + [pl.BlockSpec(memory_space=pl.ANY)]
+        + [pl.BlockSpec(memory_space=pltpu.VMEM)] * len(near),
+        out_specs=[pl.BlockSpec(memory_space=pltpu.VMEM)] * count + [pl.BlockSpec(memory_space=pltpu.HBM)],
+        scratch_shapes=[pltpu.VMEM(x.shape, x.dtype) for x in arrays[count:]]
+        + [
+            pltpu.VMEM((OWN, NY), F32),
+            pltpu.SemaphoreType.DMA((count + given,)),
+            pltpu.SemaphoreType.DMA((NY // TILE,)),
+        ],
         compiler_params=pltpu.CompilerParams(vmem_limit_bytes=VMEM_LIMIT),
-    )(*[pltpu.with_memory_space_constraint(x, pltpu.HBM) for x in arrays], after)
+    )(*[pltpu.with_memory_space_constraint(x, pltpu.HBM) for x in arrays], after, *near)
+    return tables, slope
 
 
 def exchange(x, groups=None):
@@ -658,60 +754,73 @@
     w_in = jnp.transpose(w_in, (1, 2, 3, 0))
     device = lax.axis_index("rows").reshape(1)
     down = [(i, (i + 1) % D) for i in range(D)]
-    above = lax.ppermute(velocity.astype(BF), "rows", down)
+    above = lax.ppermute(velocity, "rows", down)
 
     forward = [columns[k] for k in ("forward_a", "forward_b", "forward_b0", "twist")]
-    ahead = [*forward, velocity, w_in, w_mid, w_out, net["taps"], net["outs"]]
-    dual_sent, *ahead = call(
-        dual_kernel, shape((D, 2, 128), BF), [cotangent, *ahead], staged=1 + len(ahead), kept=len(ahead)
-    )
-
-    big = shape((R * HID, NY), BF)
-    own_tiles = [pltpu.VMEM((R * HID, NY), BF)] * 4
-    first_sent, act_one, act_two, slope_one, slope_two, stack = call(
+    ahead = [*forward, velocity, w_in, w_mid, w_out, net["taps"], net["outs"], net["taps_inner"]]
+    dual_sent, early_one, early_two, *ahead = call(
+        early_kernel,
+        [shape((D, 2, 128), BF), pltpu.VMEM((HID, NY), BF), pltpu.VMEM((2 * HID, NY), BF)],
+        [cotangent, *ahead],
+        [pltpu.VMEM((24, NY), BF)],
+        staged=1 + len(ahead),
+        kept=len(ahead),
+    )
+
+    big = shape((OWN, NY), BF)
+    first_sent, stack, act_one, act_two = call(
         network_kernel,
-        [shape((D, 2, 2, 128), BF), big, big, big, big, shape((48, NY), BF)],
-        [dual_sent, above, *ahead],
-        own_tiles
-        + [
-            pltpu.VMEM((48, NY), BF),
+        [shape((D, 2, 2, 128), BF), pltpu.VMEM((48, NY), BF), big, big],
+        [dual_sent, early_one, early_two, above, *ahead],
+        [
+            pltpu.VMEM((3 * HID, NY), BF),
+            pltpu.VMEM((3 * HID, NY), BF),
             pltpu.VMEM((24, NY), F32),
-            pltpu.SemaphoreType.DMA((5, NY // TILE)),
+            pltpu.SemaphoreType.DMA((3, NY // TILE)),
         ],
-        far_out=5,
+        far_out=2,
     )
     first_got = exchange(first_sent)
     names = ("row_forward", "spin", "spin_step", "short_forward", "short_inverse", "short_rim", "spin_rim")
-    tables = prefetch([*[rows[k] for k in names], rows["row_inverse"]], first_sent)
+    tables, slope_one = prefetch(
+        [*[rows[k] for k in names], rows["row_inverse"]],
+        first_sent,
+        slope_one_kernel,
+        [w_in, net["taps_step"]],
+        [stack],
+    )
     second_sent = call(
         middle_kernel, shape((D, 3, 2, 128), BF), [device, first_got, *tables], scalars=1
     )
     second_got = exchange(second_sent)
     back = [columns[k] for k in ("inverse_b", "inverse_b0", "untwist")]
-    tables = prefetch(
+    empty = np.zeros((2, 128, 64), np.float32)
+    untwists = np.concatenate([columns["untwist"], columns["untwist_rim"], empty], axis=2)
+    tables, slope_two = prefetch(
         [
-            *back,
-            columns["untwist_rim"],
+            *back[:2],
+            untwists,
             table_pair(columns["inverse_a"] * scale),
             table_pair(columns["inverse_rim"] * scale),
             w_mid,
             w_out,
             net["duals"],
-            net["taps"],
-            stack,
+            net["taps_step"],
         ],
         second_sent,
+        slope_two_kernel,
+        [act_one, w_mid],
     )
     partial = call(
         backward_kernel,
         shape((8, 25, 2, 128), BF),
-        [second_got, *tables, act_one, act_two, slope_one, slope_two],
-        own_tiles
-        + [
+        [second_got, *tables, stack, act_one, act_two, slope_one, slope_two],
+        [
+            *[pltpu.VMEM((OWN, NY), t) for t in (BF, BF, F32, F32)],
             pltpu.VMEM((48, NY), BF),
             pltpu.VMEM((OWN, OWN), F32),
-            pltpu.VMEM((R * HID, 48), F32),
-            pltpu.VMEM((R * HID, 48), F32),
+            pltpu.VMEM((OWN, 48), F32),
+            pltpu.VMEM((OWN, 48), F32),
             pltpu.SemaphoreType.DMA((4, NY // BACK_TILE)),
         ],
         far=4,
@@ -727,10 +836,10 @@
     )
     grad_mid, grad_in, grad_out = call(
         total_kernel,
-        [shape((HID, HID), F32), shape((HID, 18), F32), shape((3, 3, 2, HID), F32)],
+        [shape((HID, HID), F32), shape((3, 3, 2, HID), F32), shape((3, 3, 2, HID), F32)],
         [exchange(partial, across_z)],
     )
-    return new_velocity, grad_in.reshape(HID, 3, 3, 2), grad_mid, grad_out
+    return new_velocity, jnp.transpose(grad_in, (3, 0, 1, 2)), grad_mid, grad_out
 
 
 def solution(mesh):

time: 99.9 us -> 96.2 us (0.963)
  waiting for transfers between devices: 30.1 us -> 23.5 us
  Pallas kernels: 25 us -> 30.1 us
    all_to_all x3, waiting for transfers between devices: 30.1 us -> 23.5 us  [exchange(): lax.all_to_all(x, 'rows', split_axis=0, concat_axis=0, tiled=True, axis_i...]
    pallas_call x2, Pallas kernels: 2.91 us -> 9.26 us  [prefetch(): pl.pallas_call(run, out_shape=[pltpu.VMEM(x.shape, x.dtype) for x in arra...]
    pallas_call x7, Pallas kernels: 22.1 us -> 20.8 us  [call(): pl.pallas_call(run, out_shape=outputs, in_specs=specs, out_specs=out_spec...]
  transfers between devices with their start and end apart: 4 -> 4, of which waited for: 3 -> 3; matrix products, arithmetic and copies ran while one was open for 0% -> 0% of each run, Pallas kernels for 7% -> 16%
where the time goes in v4:
time: 96.2 us; the launch traced here: 95.8 us
  starting transfers between devices  31.3 us (33%)
  Pallas kernels  30.1 us (31%)
  waiting for transfers between devices  23.5 us (24%)
  blocking collectives  10.2 us (11%)
    all_to_all x3, starting transfers between devices, exchange(): lax.all_to_all(x, 'rows', split_axis=0, concat_axis=0, tiled=True, axis_i...  27.1 us
    all_to_all x3, waiting for transfers between devices, exchange(): lax.all_to_all(x, 'rows', split_axis=0, concat_axis=0, tiled=True, axis_i...  23.5 us
    pallas_call x7, Pallas kernels, call(): pl.pallas_call(run, out_shape=outputs, in_specs=specs, out_specs=out_spec...  20.8 us
    all_to_all x1, blocking collectives, exchange(): lax.all_to_all(x, 'rows', split_axis=0, concat_axis=0, tiled=True, axis_i...  10.2 us
    pallas_call x2, Pallas kernels, prefetch(): pl.pallas_call(run, out_shape=[pltpu.VMEM(x.shape, x.dtype) for x in arra...  9.26 us
    ppermute x1, starting transfers between devices, body(): above = lax.ppermute(velocity, 'rows', down)  4.21 us
  transfers between devices with their start and end apart: 4, of which 3 were waited for; matrix products, arithmetic and copies ran while one was open for 0% of the time, Pallas kernels for 16%

profile of v4, /device:TPU:1, one launch (start us, length us, event | category | flops | bytes accessed | tf_op | source)
XLA Modules:
  0.0 95.8 jit_solution(7944784635504051365)
XLA Ops:
  0.6 4.2 %collective-permute-start = (f32[2,4,4096]{2,1,0:T(4,128)}, f32[2,4,4096]{2,1,0:T(4,128)S(1)}, u32[]{:S(2)}, u32[]{:S(2)}) collective-permute-start(f32[2,4,4096]{2,1,0:T(4,128)} %refs_5_.3), channel_id=1, source_target_pairs={{0,2},{2,4},{4,6},{6,8},{8,10},{10,12},{12,14},{14,16},{16,18},{18... | collective-permute-start | bytes 393224 | tf_op jit(solution)/shard_map/ppermute | solution.py:757
  4.8 3.8 %shard_map.300 = (bf16[128,2,128]{2,1,0:T(2,128)(2,1)S(1)}, bf16[64,4096]{1,0:T(8,128)(2,1)S(1)}, bf16[128,4096]{1,0:T(8,128)(2,1)S(1)}, bf16[2,256,256]{2,1,0:T...) custom-call(f32[2,4,4096]{2,1,0:T(4,128)} %refs_0_.3, ...), custom_call_target="tpu_custom_call" | custom-call | tf_op jit(solution)/shard_map/pallas_call | solution.py:679
  8.6 0.0 collective-permute-done.refs_3_
  8.6 4.7 %shard_map.301 = (bf16[128,2,2,128]{3,2,1,0:T(2,128)(2,1)}, bf16[48,4096]{1,0:T(8,128)(2,1)S(1)}, bf16[256,4096]{1,0:T(8,128)(2,1)}, bf16[256,4096]{1,0:T(8,128)(2,1)}) custom-call(bf16[128,2,128]{2,1,0:T(2,128)(2,1)S(1)} %get-tuple-element.44.refs_0_, bf16[64,4096]{1,0:T(8,128)(2,1)S(1)} %get-tuple-element.45.refs_1_, ...), custom_call_target="tpu_custom_call" | custom-call | tf_op jit(solution)/shard_map/pallas_call | solution.py:679
  13.3 14.6 %all-to-all-start = ((bf16[128,2,2,128]{3,2,1,0:T(2,128)(2,1)}), bf16[128,2,2,128]{3,2,1,0:T(2,128)(2,1)S(1)}, u32[]{:S(2)}, u32[]{:S(2)}) async-start(bf16[128,2,2,128]{3,2,1,0:T(2,128)(2,1)} %get-tuple-element.58.refs_10_), calls=%async_computation | async-start | bytes 262144 | tf_op jit(solution)/shard_map/all_to_all | solution.py:745
  27.9 4.2 %shard_map.302 = (bf16[2,256,256]{2,1,0:T(8,128)(2,1)S(1)}, f32[2,128,128]{2,1,0:T(8,128)S(1)}, f32[2,128,128]{2,1,0:T(8,128)S(1)}, bf16[256,256]{1,0:T(8,128)(2...) custom-call(bf16[2,256,256]{2,1,0:T(8,128)(2,1)} %constant.61.clone., ...), custom_call_target="tpu_custom_call" | custom-call | tf_op jit(solution)/shard_map/pallas_call | solution.py:726
  32.2 8.7 %all-to-all-done.refs_1_ = bf16[128,2,2,128]{3,2,1,0:T(2,128)(2,1)S(1)} async-done(((bf16[128,2,2,128]{3,2,1,0:T(2,128)(2,1)}), bf16[128,2,2,128]{3,2,1,0:T(2,128)(2,1)S(1)}, u32[]{:S(2)}, u32[]{:S(2)}) %all-to-all-start) | async-done | bytes 131104 | tf_op jit(solution)/shard_map/all_to_all | solution.py:745
  40.9 1.9 %shard_map.303.refs_11_ = bf16[128,3,2,128]{3,2,1,0:T(2,128)(2,1)} custom-call(s32[1]{0:T(128)} %bitcast.refs_0_, bf16[128,2,2,128]{3,2,1,0:T(2,128)(2,1)S(1)} %all-to-all-done.refs_1_, bf16[2,256,256]{2,1,0:T(8,128)(2,1)S(1)} %get-tuple-element.60.refs_2_, f32[2,128,128]{2,1,0:T(8,128)S(1)} %get-tuple-element.61.refs_3_, ...), custom_call_target="tpu_custom_call" | custom-call | tf_op jit(solution)/shard_map/pallas_call | solution.py:679
  42.8 6.4 %all-to-all-start.1 = ((bf16[128,3,2,128]{3,2,1,0:T(2,128)(2,1)}), bf16[128,3,2,128]{3,2,1,0:T(2,128)(2,1)S(1)}, u32[]{:S(2)}, u32[]{:S(2)}) async-start(bf16[128,3,2,128]{3,2,1,0:T(2,128)(2,1)} %shard_map.303.refs_11_), calls=%async_computation.1 | async-start | bytes 393216 | tf_op jit(solution)/shard_map/all_to_all | solution.py:745
  49.2 5.0 %shard_map.305 = (bf16[2,256,256]{2,1,0:T(8,128)(2,1)S(1)}, bf16[256,256]{1,0:T(8,128)(2,1)S(1)}, f32[2,128,256]{2,1,0:T(8,128)S(1)}, bf16[2,256,256]{2,1,0:T(8,...) custom-call(bf16[2,256,256]{2,1,0:T(8,128)(2,1)} %constant.70.clone., ...), custom_call_target="tpu_custom_call" | custom-call | tf_op jit(solution)/shard_map/pallas_call | solution.py:726
  54.2 8.9 %all-to-all-done.1.refs_0_ = bf16[128,3,2,128]{3,2,1,0:T(2,128)(2,1)S(1)} async-done(((bf16[128,3,2,128]{3,2,1,0:T(2,128)(2,1)}), bf16[128,3,2,128]{3,2,1,0:T(2,128)(2,1)S(1)}, u32[]{:S(2)}, u32[]{:S(2)}) %all-to-all-start.1) | async-done | bytes 196640 | tf_op jit(solution)/shard_map/all_to_all | solution.py:745
  63.1 6.5 %shard_map.306 = bf16[8,25,2,128]{3,2,1,0:T(2,128)(2,1)S(1)} custom-call(bf16[128,3,2,128]{3,2,1,0:T(2,128)(2,1)S(1)} %all-to-all-done.1.refs_0_, bf16[2,256,256]{2,1,0:T(8,128)(2,1)S(1)} %get-tuple-element.69.refs_1_, bf16[256,256]{1,0:T(8,128)(2,1)S(1)} %get-tuple-element.70.refs_2_, f32[2,128,256]{2,1,0:T(8,128)S(1)} %get-tuple-element.71.refs_3_, ...), custom_call_target="tpu_custom_call" | custom-call | tf_op jit(solution)/shard_map/pallas_call | solution.py:679
  69.7 10.2 %all_to_all.20.refs_0_ = bf16[8,25,2,128]{3,2,1,0:T(2,128)(2,1)S(1)} all-to-all(bf16[8,25,2,128]{3,2,1,0:T(2,128)(2,1)S(1)} %shard_map.306), channel_id=1, replica_groups={{0,32,64,96,128,160,192,224},{2,34,66,98,130,162,194,226},{4,36,68,100,..., dimensions={0} | all-to-all | bytes 204800 | tf_op jit(solution)/shard_map/all_to_all | solution.py:745
  79.9 0.8 shard_map.307
  80.7 6.0 %all-to-all-start.3 = ((bf16[16,25,2,128]{3,2,1,0:T(2,128)(2,1)}), bf16[16,25,2,128]{3,2,1,0:T(2,128)(2,1)S(1)}, u32[]{:S(2)}, u32[]{:S(2)}) async-start(bf16[16,25,2,128]{3,2,1,0:T(2,128)(2,1)} %shard_map.307), calls=%async_computation.3 | async-start | bytes 409600 | tf_op jit(solution)/shard_map/all_to_all | solution.py:745
  86.7 2.4 %shard_map.304 = f32[2,4,4096]{2,1,0:T(4,128)} custom-call(bf16[128,3,2,128]{3,2,1,0:T(2,128)(2,1)S(1)} %all-to-all-done.1.refs_0_, bf16[2,256,256]{2,1,0:T(8,128)(2,1)} %constant.70.clone.refs_1_.refs_0_, bf16[256,256]{1,0:T(8,128)(2,1)} %constant.71.clone.refs_2_.refs_1_, f32[2,128,128]{2,1,0:T(8,128)} %constant.76.clone.refs_3_, ...), custom_call_target="tpu_custom_call" | custom-call | tf_op jit(solution)/shard_map/pallas_call | solution.py:679
  89.1 5.9 %all-to-all-done.3.refs_0_ = bf16[16,25,2,128]{3,2,1,0:T(2,128)(2,1)S(1)} async-done(((bf16[16,25,2,128]{3,2,1,0:T(2,128)(2,1)}), bf16[16,25,2,128]{3,2,1,0:T(2,128)(2,1)S(1)}, u32[]{:S(2)}, u32[]{:S(2)}) %all-to-all-start.3) | async-done | bytes 204832 | tf_op jit(solution)/shard_map/all_to_all | solution.py:745
  95.0 0.8 shard_map.308
Async XLA Ops:
  0.6 8.0 %collective-permute-start = (f32[2,4,4096]{2,1,0:T(4,128)}, f32[2,4,4096]{2,1,0:T(4,128)S(1)}, u32[]{:S(2)}, u32[]{:S(2)}) collective-permute-start(f32[2,4,4096]{2,1,0:T(4,128)} %refs_5_.3), channel_id=1, source_target_pairs={{0,2},{2,4},{4,6},{6,8},{8,10},{10,12},{12,14},{14,16},{16,18},{18... | collective-permute-start | bytes 393224 | tf_op jit(solution)/shard_map/ppermute | solution.py:757
  13.3 27.6 %all-to-all-start = ((bf16[128,2,2,128]{3,2,1,0:T(2,128)(2,1)}), bf16[128,2,2,128]{3,2,1,0:T(2,128)(2,1)S(1)}, u32[]{:S(2)}, u32[]{:S(2)}) async-start(bf16[128,2,2,128]{3,2,1,0:T(2,128)(2,1)} %get-tuple-element.58.refs_10_), calls=%async_computation | async-start | bytes 262144 | tf_op jit(solution)/shard_map/all_to_all | solution.py:745
  42.8 20.4 %all-to-all-start.1 = ((bf16[128,3,2,128]{3,2,1,0:T(2,128)(2,1)}), bf16[128,3,2,128]{3,2,1,0:T(2,128)(2,1)S(1)}, u32[]{:S(2)}, u32[]{:S(2)}) async-start(bf16[128,3,2,128]{3,2,1,0:T(2,128)(2,1)} %shard_map.303.refs_11_), calls=%async_computation.1 | async-start | bytes 393216 | tf_op jit(solution)/shard_map/all_to_all | solution.py:745
  80.7 14.3 %all-to-all-start.3 = ((bf16[16,25,2,128]{3,2,1,0:T(2,128)(2,1)}), bf16[16,25,2,128]{3,2,1,0:T(2,128)(2,1)S(1)}, u32[]{:S(2)}, u32[]{:S(2)}) async-start(bf16[16,25,2,128]{3,2,1,0:T(2,128)(2,1)} %shard_map.307), calls=%async_computation.3 | async-start | bytes 409600 | tf_op jit(solution)/shard_map/all_to_all | solution.py:745

commit v5 on v4

--- a/solution.py
+++ b/solution.py
@@ -17,6 +17,7 @@
 F32 = jnp.float32
 TILE = 1024
 BACK_TILE = 2048
+SUM_BITS = 0b0001111
 VMEM_LIMIT = 32 * 1024 * 1024
 
 R = 4
@@ -324,20 +325,23 @@
 
 def early_kernel(
     field,
-    forward_a,
-    forward_b,
-    forward_b0,
-    twist,
-    velocity,
     w_in,
     w_mid,
     w_out,
     taps,
     outs,
     taps_inner,
+    forward_a,
+    forward_b,
+    forward_b0,
+    twist,
+    velocity,
     sent,
     early_one,
     early_two,
+    first_all,
+    third,
+    middle_all,
     inner,
 ):
     x = jnp.concatenate([field[0], field[1]], axis=0)
@@ -348,6 +352,11 @@
     flat_in = flat_taps(w_in.ready())
     first = jnp.concatenate([dot_tn(flat_in, taps_inner[i]).astype(BF) for i in range(2)], axis=0)
     middle = diagonal(w_mid[...], 2)
+    for i in range(6):
+        first_all[HID * i : HID * i + HID] = dot_tn(flat_in, taps[i]).astype(BF)
+    flat_out = flat_taps(w_out.ready())
+    third[...] = side_by_side([dot(outs[i], flat_out).astype(BF) for i in range(6)])
+    middle_all[...] = diagonal(w_mid[...], R)
 
     def columns(index):
         return slice(index * TILE, index * TILE + TILE)
@@ -373,18 +382,15 @@
     dual_sent,
     early_one,
     early_two,
+    first_all,
+    third,
+    middle_all,
     above,
     forward_a,
     forward_b,
     forward_b0,
     twist,
     velocity,
-    w_in,
-    w_mid,
-    w_out,
-    taps,
-    outs,
-    _,
     sent,
     stack,
     act_one_out,
@@ -409,10 +415,7 @@
     stack[0:16, :] = pltpu.roll(base, 1, 1).astype(BF)
     stack[16:32, :] = base.astype(BF)
     stack[32:48, :] = pltpu.roll(base, NY - 1, 1).astype(BF)
-    flat_in, flat_out = flat_taps(w_in), flat_taps(w_out)
-    first = jnp.concatenate([dot_tn(flat_in, taps[i]).astype(BF) for i in range(4)], axis=0)
-    third = side_by_side([dot(outs[i], flat_out).astype(BF) for i in range(6)])
-    middle = diagonal(w_mid[...], R)
+    first, middle = first_all[:OWN], middle_all[...]
 
     def columns(index):
         return slice(index * TILE, index * TILE + TILE)
@@ -592,25 +595,25 @@
         flips.append(flip)
     packed = jnp.concatenate([side_by_side([mid[:32], mid[32:]]), side_by_side(flips)], axis=0)
     low = packed.astype(BF).reshape(25, 2, 128)
-    for k in range(8):
+    for k in range(sent.shape[0]):
         sent[k] = low
 
 
-def added(got, count):
+def added(got):
     total = got[0].astype(F32)
-    for k in range(1, count):
+    for k in range(1, got.shape[0]):
         total = total + got[k].astype(F32)
     return total
 
 
 def partial_sum_kernel(got, sent):
-    low = added(got, 8).astype(BF)
-    for k in range(16):
+    low = added(got).astype(BF)
+    for k in range(sent.shape[0]):
         sent[k] = low
 
 
 def total_kernel(got, grad_mid, grad_in, grad_out):
-    total = added(got, 16).reshape(50, 128)
+    total = added(got).reshape(50, 128)
     grad_mid[:32] = total[:32, :64]
     grad_mid[32:] = total[:32, 64:]
     for t in range(9):
@@ -687,14 +690,13 @@
     return result if len(outputs) > 1 else result[0]
 
 
-def slope_one_kernel(stack, w_in, taps):
-    flat_in = flat_taps(w_in)
-    first = jnp.concatenate([dot_tn(flat_in, taps[i]).astype(BF) for i in range(R)], axis=0)
+def slope_one_kernel(stack, first_all):
+    first = jnp.concatenate([first_all[: 3 * HID], first_all[4 * HID : 5 * HID]], axis=0)
     return lambda at: slope_of(*gelu_parts(dot(first, stack[:, at])))
 
 
-def slope_two_kernel(act_one, w_mid):
-    middle = diagonal(w_mid[...], R)
+def slope_two_kernel(middle_all, act_one):
+    middle = middle_all[...]
     return lambda at: slope_of(*gelu_parts(dot(middle, act_one[:, at])))
 
 
@@ -741,6 +743,10 @@
     return tables, slope
 
 
+def groups_of(mask):
+    return [[i for i in range(D) if i & ~mask == j] for j in range(D) if not j & mask]
+
+
 def exchange(x, groups=None):
     return lax.all_to_all(x, "rows", split_axis=0, concat_axis=0, tiled=True, axis_index_groups=groups)
 
@@ -757,21 +763,30 @@
     above = lax.ppermute(velocity, "rows", down)
 
     forward = [columns[k] for k in ("forward_a", "forward_b", "forward_b0", "twist")]
-    ahead = [*forward, velocity, w_in, w_mid, w_out, net["taps"], net["outs"], net["taps_inner"]]
-    dual_sent, early_one, early_two, *ahead = call(
+    weights = [w_in, w_mid, w_out, net["taps"], net["outs"], net["taps_inner"]]
+    dual_sent, *prepared = call(
         early_kernel,
-        [shape((D, 2, 128), BF), pltpu.VMEM((HID, NY), BF), pltpu.VMEM((2 * HID, NY), BF)],
-        [cotangent, *ahead],
+        [
+            shape((D, 2, 128), BF),
+            pltpu.VMEM((HID, NY), BF),
+            pltpu.VMEM((2 * HID, NY), BF),
+            pltpu.VMEM((6 * HID, 48), BF),
+            pltpu.VMEM((24, 6 * HID), BF),
+            pltpu.VMEM((OWN, OWN), BF),
+        ],
+        [cotangent, *weights, *forward, velocity],
         [pltpu.VMEM((24, NY), BF)],
-        staged=1 + len(ahead),
-        kept=len(ahead),
-    )
+        staged=12,
+        kept=5,
+    )
+    early, tables = prepared[:5], prepared[5:]
+    first_all, middle_all = early[2], early[4]
 
     big = shape((OWN, NY), BF)
     first_sent, stack, act_one, act_two = call(
         network_kernel,
         [shape((D, 2, 2, 128), BF), pltpu.VMEM((48, NY), BF), big, big],
-        [dual_sent, early_one, early_two, above, *ahead],
+        [dual_sent, *early, above, *tables],
         [
             pltpu.VMEM((3 * HID, NY), BF),
             pltpu.VMEM((3 * HID, NY), BF),
@@ -786,8 +801,8 @@
         [*[rows[k] for k in names], rows["row_inverse"]],
         first_sent,
         slope_one_kernel,
-        [w_in, net["taps_step"]],
-        [stack],
+        [],
+        [stack, first_all],
     )
     second_sent = call(
         middle_kernel, shape((D, 3, 2, 128), BF), [device, first_got, *tables], scalars=1
@@ -809,11 +824,13 @@
         ],
         second_sent,
         slope_two_kernel,
-        [act_one, w_mid],
-    )
+        [act_one],
+        [middle_all],
+    )
+    one, two = groups_of(SUM_BITS), groups_of(D - 1 - SUM_BITS)
     partial = call(
         backward_kernel,
-        shape((8, 25, 2, 128), BF),
+        shape((len(one[0]), 25, 2, 128), BF),
         [second_got, *tables, stack, act_one, act_two, slope_one, slope_two],
         [
             *[pltpu.VMEM((OWN, NY), t) for t in (BF, BF, F32, F32)],
@@ -825,9 +842,7 @@
         ],
         far=4,
     )
-    along_z = [[16 * z + r for z in range(8)] for r in range(16)]
-    across_z = [[16 * z + r for r in range(16)] for z in range(8)]
-    partial = call(partial_sum_kernel, shape((16, 25, 2, 128), BF), [exchange(partial, along_z)])
+    partial = call(partial_sum_kernel, shape((len(two[0]), 25, 2, 128), BF), [exchange(partial, one)])
     new_velocity = call(
         field_kernel,
         shape((CH, R, NY), F32),
@@ -837,7 +852,7 @@
     grad_mid, grad_in, grad_out = call(
         total_kernel,
         [shape((HID, HID), F32), shape((3, 3, 2, HID), F32), shape((3, 3, 2, HID), F32)],
-        [exchange(partial, across_z)],
+        [exchange(partial, two)],
     )
     return new_velocity, jnp.transpose(grad_in, (3, 0, 1, 2)), grad_mid, grad_out
 

time: 96.2 us -> 94.7 us (0.984)
  starting transfers between devices: 31.3 us -> 28.2 us
  blocking collectives: 10.2 us -> 12.5 us
    all_to_all x3, starting transfers between devices: 27.1 us -> 24 us  [exchange(): lax.all_to_all(x, 'rows', split_axis=0, concat_axis=0, tiled=True, axis_i...]
    all_to_all x1, blocking collectives: 10.2 us -> 12.5 us  [exchange(): lax.all_to_all(x, 'rows', split_axis=0, concat_axis=0, tiled=True, axis_i...]
where the time goes in v5:
time: 94.7 us; the launch traced here: 94.3 us
  Pallas kernels  29.8 us (31%)
  starting transfers between devices  28.2 us (30%)
  waiting for transfers between devices  23.1 us (24%)
  blocking collectives  12.5 us (13%)
    all_to_all x3, starting transfers between devices, exchange(): lax.all_to_all(x, 'rows', split_axis=0, concat_axis=0, tiled=True, axis_i...  24 us
    all_to_all x3, waiting for transfers between devices, exchange(): lax.all_to_all(x, 'rows', split_axis=0, concat_axis=0, tiled=True, axis_i...  23.1 us
    pallas_call x7, Pallas kernels, call(): pl.pallas_call(run, out_shape=outputs, in_specs=specs, out_specs=out_spec...  21.1 us
    all_to_all x1, blocking collectives, exchange(): lax.all_to_all(x, 'rows', split_axis=0, concat_axis=0, tiled=True, axis_i...  12.5 us
    pallas_call x2, Pallas kernels, prefetch(): pl.pallas_call(run, out_shape=[pltpu.VMEM(x.shape, x.dtype) for x in arra...  8.69 us
    ppermute x1, starting transfers between devices, body(): above = lax.ppermute(velocity, 'rows', down)  4.21 us
  transfers between devices with their start and end apart: 4, of which 3 were waited for; matrix products, arithmetic and copies ran while one was open for 0% of the time, Pallas kernels for 16%

profile of v5, /device:TPU:1, one launch (start us, length us, event | category | flops | bytes accessed | tf_op | source)
XLA Modules:
  0.0 94.3 jit_solution(4845726963934371193)
XLA Ops:
  0.6 4.2 %collective-permute-start = (f32[2,4,4096]{2,1,0:T(4,128)}, f32[2,4,4096]{2,1,0:T(4,128)S(1)}, u32[]{:S(2)}, u32[]{:S(2)}) collective-permute-start(f32[2,4,4096]{2,1,0:T(4,128)} %refs_11_.1), channel_id=1, source_target_pairs={{0,2},{2,4},{4,6},{6,8},{8,10},{10,12},{12,14},{14,16},{16,18},{18... | collective-permute-start | bytes 393224 | tf_op jit(solution)/shard_map/ppermute | solution.py:763
  4.8 4.2 %shard_map.300 = (bf16[128,2,128]{2,1,0:T(2,128)(2,1)S(1)}, bf16[64,4096]{1,0:T(8,128)(2,1)S(1)}, bf16[128,4096]{1,0:T(8,128)(2,1)S(1)}, bf16[384,48]{1,0:T(8,12...) custom-call(f32[2,4,4096]{2,1,0:T(4,128)} %refs_0_.3, ...), custom_call_target="tpu_custom_call" | custom-call | tf_op jit(solution)/shard_map/pallas_call | solution.py:682
  9.1 0.0 collective-permute-done.refs_6_
  9.1 4.6 %shard_map.301 = (bf16[128,2,2,128]{3,2,1,0:T(2,128)(2,1)}, bf16[48,4096]{1,0:T(8,128)(2,1)S(1)}, bf16[256,4096]{1,0:T(8,128)(2,1)}, bf16[256,4096]{1,0:T(8,128)(2,1)}) custom-call(bf16[128,2,128]{2,1,0:T(2,128)(2,1)S(1)} %get-tuple-element.41.refs_0_, bf16[64,4096]{1,0:T(8,128)(2,1)S(1)} %get-tuple-element.42.refs_1_, ...), custom_call_target="tpu_custom_call" | custom-call | tf_op jit(solution)/shard_map/pallas_call | solution.py:682
  13.7 14.2 %all-to-all-start = ((bf16[128,2,2,128]{3,2,1,0:T(2,128)(2,1)}), bf16[128,2,2,128]{3,2,1,0:T(2,128)(2,1)S(1)}, u32[]{:S(2)}, u32[]{:S(2)}) async-start(bf16[128,2,2,128]{3,2,1,0:T(2,128)(2,1)} %get-tuple-element.52.refs_8_), calls=%async_computation | async-start | bytes 262144 | tf_op jit(solution)/shard_map/all_to_all | solution.py:751
  27.9 3.7 %shard_map.302 = (bf16[2,256,256]{2,1,0:T(8,128)(2,1)S(1)}, f32[2,128,128]{2,1,0:T(8,128)S(1)}, f32[2,128,128]{2,1,0:T(8,128)S(1)}, bf16[256,256]{1,0:T(8,128)(2...) custom-call(bf16[2,256,256]{2,1,0:T(8,128)(2,1)} %constant.61.clone., ...), custom_call_target="tpu_custom_call" | custom-call | tf_op jit(solution)/shard_map/pallas_call | solution.py:728
  31.6 9.3 %all-to-all-done.refs_1_ = bf16[128,2,2,128]{3,2,1,0:T(2,128)(2,1)S(1)} async-done(((bf16[128,2,2,128]{3,2,1,0:T(2,128)(2,1)}), bf16[128,2,2,128]{3,2,1,0:T(2,128)(2,1)S(1)}, u32[]{:S(2)}, u32[]{:S(2)}) %all-to-all-start) | async-done | bytes 131104 | tf_op jit(solution)/shard_map/all_to_all | solution.py:751
  40.8 1.9 %shard_map.303.refs_10_ = bf16[128,3,2,128]{3,2,1,0:T(2,128)(2,1)} custom-call(s32[1]{0:T(128)} %bitcast.refs_0_, bf16[128,2,2,128]{3,2,1,0:T(2,128)(2,1)S(1)} %all-to-all-done.refs_1_, bf16[2,256,256]{2,1,0:T(8,128)(2,1)S(1)} %get-tuple-element.54.refs_2_, f32[2,128,128]{2,1,0:T(8,128)S(1)} %get-tuple-element.55.refs_3_, ...), custom_call_target="tpu_custom_call" | custom-call | tf_op jit(solution)/shard_map/pallas_call | solution.py:682
  42.7 6.4 %all-to-all-start.1 = ((bf16[128,3,2,128]{3,2,1,0:T(2,128)(2,1)}), bf16[128,3,2,128]{3,2,1,0:T(2,128)(2,1)S(1)}, u32[]{:S(2)}, u32[]{:S(2)}) async-start(bf16[128,3,2,128]{3,2,1,0:T(2,128)(2,1)} %shard_map.303.refs_10_), calls=%async_computation.1 | async-start | bytes 393216 | tf_op jit(solution)/shard_map/all_to_all | solution.py:751
  49.1 5.0 %shard_map.305 = (bf16[2,256,256]{2,1,0:T(8,128)(2,1)S(1)}, bf16[256,256]{1,0:T(8,128)(2,1)S(1)}, f32[2,128,256]{2,1,0:T(8,128)S(1)}, bf16[2,256,256]{2,1,0:T(8,...) custom-call(bf16[2,256,256]{2,1,0:T(8,128)(2,1)} %constant.69.clone., ...), custom_call_target="tpu_custom_call" | custom-call | tf_op jit(solution)/shard_map/pallas_call | solution.py:728
  54.1 8.9 %all-to-all-done.1.refs_0_ = bf16[128,3,2,128]{3,2,1,0:T(2,128)(2,1)S(1)} async-done(((bf16[128,3,2,128]{3,2,1,0:T(2,128)(2,1)}), bf16[128,3,2,128]{3,2,1,0:T(2,128)(2,1)S(1)}, u32[]{:S(2)}, u32[]{:S(2)}) %all-to-all-start.1) | async-done | bytes 196640 | tf_op jit(solution)/shard_map/all_to_all | solution.py:751
  63.0 6.6 %shard_map.306 = bf16[16,25,2,128]{3,2,1,0:T(2,128)(2,1)S(1)} custom-call(bf16[128,3,2,128]{3,2,1,0:T(2,128)(2,1)S(1)} %all-to-all-done.1.refs_0_, bf16[2,256,256]{2,1,0:T(8,128)(2,1)S(1)} %get-tuple-element.63.refs_1_, bf16[256,256]{1,0:T(8,128)(2,1)S(1)} %get-tuple-element.64.refs_2_, f32[2,128,256]{2,1,0:T(8,128)S(1)} %get-tuple-element.65.refs_3_, ...), custom_call_target="tpu_custom_call" | custom-call | tf_op jit(solution)/shard_map/pallas_call | solution.py:682
  69.6 12.5 %all_to_all.20.refs_0_ = bf16[16,25,2,128]{3,2,1,0:T(2,128)(2,1)S(1)} all-to-all(bf16[16,25,2,128]{3,2,1,0:T(2,128)(2,1)S(1)} %shard_map.306), channel_id=1, replica_groups={{0,2,4,6,8,10,12,14,16,18,20,22,24,26,28,30},{32,34,36,38,40,42,44,46,4..., dimensions={0} | all-to-all | bytes 409600 | tf_op jit(solution)/shard_map/all_to_all | solution.py:751
  82.1 0.8 shard_map.307
  82.8 3.4 %all-to-all-start.3 = ((bf16[8,25,2,128]{3,2,1,0:T(2,128)(2,1)}), bf16[8,25,2,128]{3,2,1,0:T(2,128)(2,1)S(1)}, u32[]{:S(2)}, u32[]{:S(2)}) async-start(bf16[8,25,2,128]{3,2,1,0:T(2,128)(2,1)} %shard_map.307), calls=%async_computation.3 | async-start | bytes 204800 | tf_op jit(solution)/shard_map/all_to_all | solution.py:751
  86.2 2.4 %shard_map.304 = f32[2,4,4096]{2,1,0:T(4,128)} custom-call(bf16[128,3,2,128]{3,2,1,0:T(2,128)(2,1)S(1)} %all-to-all-done.1.refs_0_, bf16[2,256,256]{2,1,0:T(8,128)(2,1)} %constant.69.clone.refs_1_.refs_0_, bf16[256,256]{1,0:T(8,128)(2,1)} %constant.70.clone.refs_2_.refs_1_, f32[2,128,128]{2,1,0:T(8,128)} %constant.76.clone.refs_3_, ...), custom_call_target="tpu_custom_call" | custom-call | tf_op jit(solution)/shard_map/pallas_call | solution.py:682
  88.6 5.0 %all-to-all-done.3.refs_0_ = bf16[8,25,2,128]{3,2,1,0:T(2,128)(2,1)S(1)} async-done(((bf16[8,25,2,128]{3,2,1,0:T(2,128)(2,1)}), bf16[8,25,2,128]{3,2,1,0:T(2,128)(2,1)S(1)}, u32[]{:S(2)}, u32[]{:S(2)}) %all-to-all-start.3) | async-done | bytes 102432 | tf_op jit(solution)/shard_map/all_to_all | solution.py:751
  93.6 0.7 shard_map.308
Async XLA Ops:
  0.6 8.4 %collective-permute-start = (f32[2,4,4096]{2,1,0:T(4,128)}, f32[2,4,4096]{2,1,0:T(4,128)S(1)}, u32[]{:S(2)}, u32[]{:S(2)}) collective-permute-start(f32[2,4,4096]{2,1,0:T(4,128)} %refs_11_.1), channel_id=1, source_target_pairs={{0,2},{2,4},{4,6},{6,8},{8,10},{10,12},{12,14},{14,16},{16,18},{18... | collective-permute-start | bytes 393224 | tf_op jit(solution)/shard_map/ppermute | solution.py:763
  13.7 27.1 %all-to-all-start = ((bf16[128,2,2,128]{3,2,1,0:T(2,128)(2,1)}), bf16[128,2,2,128]{3,2,1,0:T(2,128)(2,1)S(1)}, u32[]{:S(2)}, u32[]{:S(2)}) async-start(bf16[128,2,2,128]{3,2,1,0:T(2,128)(2,1)} %get-tuple-element.52.refs_8_), calls=%async_computation | async-start | bytes 262144 | tf_op jit(solution)/shard_map/all_to_all | solution.py:751
  42.7 20.4 %all-to-all-start.1 = ((bf16[128,3,2,128]{3,2,1,0:T(2,128)(2,1)}), bf16[128,3,2,128]{3,2,1,0:T(2,128)(2,1)S(1)}, u32[]{:S(2)}, u32[]{:S(2)}) async-start(bf16[128,3,2,128]{3,2,1,0:T(2,128)(2,1)} %shard_map.303.refs_10_), calls=%async_computation.1 | async-start | bytes 393216 | tf_op jit(solution)/shard_map/all_to_all | solution.py:751
  82.8 10.8 %all-to-all-start.3 = ((bf16[8,25,2,128]{3,2,1,0:T(2,128)(2,1)}), bf16[8,25,2,128]{3,2,1,0:T(2,128)(2,1)S(1)}, u32[]{:S(2)}, u32[]{:S(2)}) async-start(bf16[8,25,2,128]{3,2,1,0:T(2,128)(2,1)} %shard_map.307), calls=%async_computation.3 | async-start | bytes 204800 | tf_op jit(solution)/shard_map/all_to_all | solution.py:751

commit v6 on v5

--- a/solution.py
+++ b/solution.py
@@ -337,7 +337,6 @@
     twist,
     velocity,
     sent,
-    early_one,
     early_two,
     first_all,
     third,
@@ -365,9 +364,7 @@
         return dot(first, inner[:, columns(index)])
 
     def gelu_one(index, pre):
-        low = gelu_parts(pre)[2].astype(BF)
-        early_one[:, columns(index)] = low[:HID]
-        return low
+        return gelu_parts(pre)[2].astype(BF)
 
     def layer_two(index, low):
         return dot(middle, low)
@@ -380,7 +377,6 @@
 
 def network_kernel(
     dual_sent,
-    early_one,
     early_two,
     first_all,
     third,
@@ -393,23 +389,9 @@
     velocity,
     sent,
     stack,
-    act_one_out,
-    act_two_out,
-    act_one,
-    act_two,
     partial,
-    semaphores,
 ):
     sent[:, 1] = dual_sent[...]
-    mine = 3 * HID
-    ready = [
-        pltpu.make_async_copy(early_one, act_one_out.at[mine:], semaphores.at[2, 0]),
-        pltpu.make_async_copy(early_two.at[:HID], act_two_out.at[mine:], semaphores.at[2, 1]),
-    ]
-    for copy in ready:
-        copy.start()
-    held = (act_one, act_two)
-    homes = (act_one_out, act_two_out)
     upper = [above[c] for c in range(CH)]
     base = jnp.concatenate([velocity[0], velocity[1], *upper], axis=0)
     stack[0:16, :] = pltpu.roll(base, 1, 1).astype(BF)
@@ -423,29 +405,17 @@
     def layer_one(index, _):
         return dot(first, stack[:, columns(index)])
 
-    def gelu_one(index, pre):
-        low = gelu_parts(pre)[2].astype(BF)
-        act_one[:, columns(index)] = low[:mine]
-        return low
+    def gelu(index, pre):
+        return gelu_parts(pre)[2].astype(BF)
 
     def layer_two(index, low):
         return dot(middle, low)
-
-    def gelu_two(index, pre):
-        at = columns(index)
-        low = gelu_parts(pre)[2].astype(BF)
-        act_two[:, at] = low[:mine]
-        for k in range(2):
-            pltpu.make_async_copy(
-                held[k].at[:, at], homes[k].at[:mine, at], semaphores.at[k, index]
-            ).start()
-        return low
 
     def layer_three(index, low):
         at = columns(index)
         partial[:, at] = dot(third[:, :OWN], low) + dot(third[:, OWN:], early_two[:, at])
 
-    staggered(NY // TILE, layer_one, gelu_one, layer_two, gelu_two, layer_three)
+    staggered(NY // TILE, layer_one, gelu, layer_two, gelu, layer_three)
     correction = (
         pltpu.roll(partial[0:8, :], 1, 1) + partial[8:16, :] + pltpu.roll(partial[16:24, :], NY - 1, 1)
     )
@@ -461,12 +431,6 @@
     advect = 0.5 * jnp.concatenate(pieces, axis=0)
     provisional = jnp.concatenate(rows, axis=0) + STEP_SIZE * (correction - advect)
     sent[:, 0] = column_forward(provisional, forward_a, forward_b, forward_b0, twist).reshape(D, 2, 128)
-    for copy in ready:
-        copy.wait()
-    for k in range(2):
-        for index in range(NY // TILE):
-            at = pl.ds(index * TILE, TILE)
-            pltpu.make_async_copy(held[k].at[:, at], homes[k].at[:mine, at], semaphores.at[k, index]).wait()
 
 
 def middle_kernel(
@@ -690,57 +654,71 @@
     return result if len(outputs) > 1 else result[0]
 
 
-def slope_one_kernel(stack, first_all):
+def layer_one_kernel(stack, first_all):
     first = jnp.concatenate([first_all[: 3 * HID], first_all[4 * HID : 5 * HID]], axis=0)
-    return lambda at: slope_of(*gelu_parts(dot(first, stack[:, at])))
-
-
-def slope_two_kernel(middle_all, act_one):
+    return lambda at: dot(first, stack[:, at])
+
+
+def layer_two_kernel(middle_all, act_one):
     middle = middle_all[...]
-    return lambda at: slope_of(*gelu_parts(dot(middle, act_one[:, at])))
-
-
-def prefetch(arrays, after, maker, inputs, near=()):
-    count, given = len(arrays), len(inputs)
+    return lambda at: dot(middle, act_one[:, at])
+
+
+def prefetch(arrays, after, maker, near, wide=()):
+    count, given, tiles = len(arrays), len(wide), NY // TILE
 
     def run(*refs):
-        sources, close, refs = refs[: count + given], refs[count + given + 1 :][: len(near)], refs[count + given + 1 + len(near) :]
-        targets, slope_out, refs = refs[:count], refs[count], refs[count + 1 :]
-        held, slope, semaphores, out_semaphores = refs[:given], *refs[given:]
-        copies = []
-        for k in list(range(count, count + given)) + list(range(count)):
-            target = targets[k] if k < count else held[k - count]
-            copies.append(pltpu.make_async_copy(sources[k], target, semaphores.at[k]))
-            copies[-1].start()
-        for copy in copies[:given]:
+        sources, refs = refs[: count + given], refs[count + given + 1 :]
+        close, refs = refs[: len(near)], refs[len(near) :]
+        targets, homes, refs = refs[:count], refs[count : count + 2], refs[count + 2 :]
+        held, results, refs = refs[:given], refs[given : given + 2], refs[given + 2 :]
+        semaphores, in_semaphores, out_semaphores = refs
+        columns = [slice(index * TILE, index * TILE + TILE) for index in range(tiles)]
+        pieces = [
+            [
+                pltpu.make_async_copy(sources[count + k].at[:, at], held[k].at[:, at], in_semaphores.at[k, index])
+                for k in range(given)
+            ]
+            for index, at in enumerate(columns)
+        ]
+        copies = [pltpu.make_async_copy(sources[k], targets[k], semaphores.at[k]) for k in range(count)]
+        for copy in sum(pieces, []) + copies:
+            copy.start()
+        layer = maker(*close, *held)
+        for index, at in enumerate(columns):
+            for copy in pieces[index]:
+                copy.wait()
+            square, gate, value = gelu_parts(layer(at))
+            results[0][:, at] = value.astype(BF)
+            results[1][:, at] = slope_of(square, gate, value)
+            for k in range(2):
+                copies.append(
+                    pltpu.make_async_copy(results[k].at[:, at], homes[k].at[:, at], out_semaphores.at[k, index])
+                )
+                copies[-1].start()
+        for copy in copies:
             copy.wait()
-        slopes = maker(*close, *held)
-        stores = []
-        for index in range(NY // TILE):
-            at = slice(index * TILE, index * TILE + TILE)
-            slope[:, at] = slopes(at)
-            stores.append(pltpu.make_async_copy(slope.at[:, at], slope_out.at[:, at], out_semaphores.at[index]))
-            stores[-1].start()
-        for copy in copies[given:] + stores:
-            copy.wait()
-
-    arrays = [jnp.asarray(x) for x in [*arrays, *inputs]]
-    *tables, slope = pl.pallas_call(
+
+    arrays = [jnp.asarray(x) for x in [*arrays, *wide]]
+    *tables, act, slope = pl.pallas_call(
         run,
-        out_shape=[pltpu.VMEM(x.shape, x.dtype) for x in arrays[:count]] + [pltpu.HBM((OWN, NY), F32)],
+        out_shape=[pltpu.VMEM(x.shape, x.dtype) for x in arrays[:count]]
+        + [pltpu.HBM((OWN, NY), BF), pltpu.HBM((OWN, NY), F32)],
         in_specs=[pl.BlockSpec(memory_space=pltpu.HBM)] * (count + given)
         + [pl.BlockSpec(memory_space=pl.ANY)]
         + [pl.BlockSpec(memory_space=pltpu.VMEM)] * len(near),
-        out_specs=[pl.BlockSpec(memory_space=pltpu.VMEM)] * count + [pl.BlockSpec(memory_space=pltpu.HBM)],
+        out_specs=[pl.BlockSpec(memory_space=pltpu.VMEM)] * count + [pl.BlockSpec(memory_space=pltpu.HBM)] * 2,
         scratch_shapes=[pltpu.VMEM(x.shape, x.dtype) for x in arrays[count:]]
         + [
+            pltpu.VMEM((OWN, NY), BF),
             pltpu.VMEM((OWN, NY), F32),
-            pltpu.SemaphoreType.DMA((count + given,)),
-            pltpu.SemaphoreType.DMA((NY // TILE,)),
+            pltpu.SemaphoreType.DMA((count,)),
+            pltpu.SemaphoreType.DMA((max(given, 1), tiles)),
+            pltpu.SemaphoreType.DMA((2, tiles)),
         ],
         compiler_params=pltpu.CompilerParams(vmem_limit_bytes=VMEM_LIMIT),
     )(*[pltpu.with_memory_space_constraint(x, pltpu.HBM) for x in arrays], after, *near)
-    return tables, slope
+    return tables, act, slope
 
 
 def groups_of(mask):
@@ -768,7 +746,6 @@
         early_kernel,
         [
             shape((D, 2, 128), BF),
-            pltpu.VMEM((HID, NY), BF),
             pltpu.VMEM((2 * HID, NY), BF),
             pltpu.VMEM((6 * HID, 48), BF),
             pltpu.VMEM((24, 6 * HID), BF),
@@ -779,29 +756,21 @@
         staged=12,
         kept=5,
     )
-    early, tables = prepared[:5], prepared[5:]
-    first_all, middle_all = early[2], early[4]
-
-    big = shape((OWN, NY), BF)
-    first_sent, stack, act_one, act_two = call(
+    early, tables = prepared[:4], prepared[4:]
+    first_all, middle_all = early[1], early[3]
+
+    first_sent, stack = call(
         network_kernel,
-        [shape((D, 2, 2, 128), BF), pltpu.VMEM((48, NY), BF), big, big],
+        [shape((D, 2, 2, 128), BF), pltpu.VMEM((48, NY), BF)],
         [dual_sent, *early, above, *tables],
-        [
-            pltpu.VMEM((3 * HID, NY), BF),
-            pltpu.VMEM((3 * HID, NY), BF),
-            pltpu.VMEM((24, NY), F32),
-            pltpu.SemaphoreType.DMA((3, NY // TILE)),
-        ],
-        far_out=2,
+        [pltpu.VMEM((24, NY), F32)],
     )
     first_got = exchange(first_sent)
     names = ("row_forward", "spin", "spin_step", "short_forward", "short_inverse", "short_rim", "spin_rim")
-    tables, slope_one = prefetch(
+    tables, act_one, slope_one = prefetch(
         [*[rows[k] for k in names], rows["row_inverse"]],
         first_sent,
-        slope_one_kernel,
-        [],
+        layer_one_kernel,
         [stack, first_all],
     )
     second_sent = call(
@@ -811,7 +780,7 @@
     back = [columns[k] for k in ("inverse_b", "inverse_b0", "untwist")]
     empty = np.zeros((2, 128, 64), np.float32)
     untwists = np.concatenate([columns["untwist"], columns["untwist_rim"], empty], axis=2)
-    tables, slope_two = prefetch(
+    tables, act_two, slope_two = prefetch(
         [
             *back[:2],
             untwists,
@@ -823,9 +792,9 @@
             net["taps_step"],
         ],
         second_sent,
-        slope_two_kernel,
+        layer_two_kernel,
+        [middle_all],
         [act_one],
-        [middle_all],
     )
     one, two = groups_of(SUM_BITS), groups_of(D - 1 - SUM_BITS)
     partial = call(

time: 94.7 us -> 94.5 us (level)
  transfers between devices with their start and end apart: 4 -> 4, of which waited for: 3 -> 3; matrix products, arithmetic and copies ran while one was open for 0% -> 0% of each run, Pallas kernels for 16% -> 17%
where the time goes in v6:
time: 94.5 us; the launch traced here: 94 us
  Pallas kernels  30.3 us (32%)
  starting transfers between devices  28.2 us (30%)
  waiting for transfers between devices  22.4 us (24%)
  blocking collectives  12.5 us (13%)
    all_to_all x3, starting transfers between devices, exchange(): lax.all_to_all(x, 'rows', split_axis=0, concat_axis=0, tiled=True, axis_i...  24 us
    all_to_all x3, waiting for transfers between devices, exchange(): lax.all_to_all(x, 'rows', split_axis=0, concat_axis=0, tiled=True, axis_i...  22.4 us
    pallas_call x7, Pallas kernels, call(): pl.pallas_call(run, out_shape=outputs, in_specs=specs, out_specs=out_spec...  20.9 us
    all_to_all x1, blocking collectives, exchange(): lax.all_to_all(x, 'rows', split_axis=0, concat_axis=0, tiled=True, axis_i...  12.5 us
    pallas_call x2, Pallas kernels, prefetch(): pl.pallas_call(run, out_shape=[pltpu.VMEM(x.shape, x.dtype) for x in arra...  9.4 us
    ppermute x1, starting transfers between devices, body(): above = lax.ppermute(velocity, 'rows', down)  4.21 us
  transfers between devices with their start and end apart: 4, of which 3 were waited for; matrix products, arithmetic and copies ran while one was open for 0% of the time, Pallas kernels for 17%

profile of v6, /device:TPU:1, one launch (start us, length us, event | category | flops | bytes accessed | tf_op | source)
XLA Modules:
  0.0 94.0 jit_solution(13528006431048575955)
XLA Ops:
  0.6 4.2 %collective-permute-start = (f32[2,4,4096]{2,1,0:T(4,128)}, f32[2,4,4096]{2,1,0:T(4,128)S(1)}, u32[]{:S(2)}, u32[]{:S(2)}) collective-permute-start(f32[2,4,4096]{2,1,0:T(4,128)} %refs_11_.1), channel_id=1, source_target_pairs={{0,2},{2,4},{4,6},{6,8},{8,10},{10,12},{12,14},{14,16},{16,18},{18... | collective-permute-start | bytes 393224 | tf_op jit(solution)/shard_map/ppermute | solution.py:741
  4.8 4.2 %shard_map.300 = (bf16[128,2,128]{2,1,0:T(2,128)(2,1)S(1)}, bf16[128,4096]{1,0:T(8,128)(2,1)S(1)}, bf16[384,48]{1,0:T(8,128)(2,1)S(1)}, bf16[24,384]{1,0:T(8,128...) custom-call(f32[2,4,4096]{2,1,0:T(4,128)} %refs_0_.3, ...), custom_call_target="tpu_custom_call" | custom-call | tf_op jit(solution)/shard_map/pallas_call | solution.py:646
  9.0 0.0 collective-permute-done.refs_5_
  9.1 4.4 %shard_map.301 = (bf16[128,2,2,128]{3,2,1,0:T(2,128)(2,1)}, bf16[48,4096]{1,0:T(8,128)(2,1)S(1)}) custom-call(bf16[128,2,128]{2,1,0:T(2,128)(2,1)S(1)} %get-tuple-element.40.refs_0_, bf16[128,4096]{1,0:T(8,128)(2,1)S(1)} %get-tuple-element.41.refs_1_, bf16[384,48]{1,0:T(8,128)(2,1)S(1)} %get-tuple-element.42.refs_2_.refs_10_, ...), custom_call_target="tpu_custom_call" | custom-call | tf_op jit(solution)/shard_map/pallas_call | solution.py:646
  13.4 14.1 %all-to-all-start = ((bf16[128,2,2,128]{3,2,1,0:T(2,128)(2,1)}), bf16[128,2,2,128]{3,2,1,0:T(2,128)(2,1)S(1)}, u32[]{:S(2)}, u32[]{:S(2)}) async-start(bf16[128,2,2,128]{3,2,1,0:T(2,128)(2,1)} %get-tuple-element.50.refs_8_), calls=%async_computation | async-start | bytes 262144 | tf_op jit(solution)/shard_map/all_to_all | solution.py:729
  27.6 3.9 %shard_map.302 = (bf16[2,256,256]{2,1,0:T(8,128)(2,1)S(1)}, f32[2,128,128]{2,1,0:T(8,128)S(1)}, f32[2,128,128]{2,1,0:T(8,128)S(1)}, bf16[256,256]{1,0:T(8,128)(2...) custom-call(bf16[2,256,256]{2,1,0:T(8,128)(2,1)} %constant.61.clone., ...), custom_call_target="tpu_custom_call" | custom-call | tf_op jit(solution)/shard_map/pallas_call | solution.py:703
  31.5 9.1 %all-to-all-done.refs_1_ = bf16[128,2,2,128]{3,2,1,0:T(2,128)(2,1)S(1)} async-done(((bf16[128,2,2,128]{3,2,1,0:T(2,128)(2,1)}), bf16[128,2,2,128]{3,2,1,0:T(2,128)(2,1)S(1)}, u32[]{:S(2)}, u32[]{:S(2)}) %all-to-all-start) | async-done | bytes 131104 | tf_op jit(solution)/shard_map/all_to_all | solution.py:729
  40.5 1.9 %shard_map.303.refs_10_ = bf16[128,3,2,128]{3,2,1,0:T(2,128)(2,1)} custom-call(s32[1]{0:T(128)} %bitcast.refs_0_, bf16[128,2,2,128]{3,2,1,0:T(2,128)(2,1)S(1)} %all-to-all-done.refs_1_, bf16[2,256,256]{2,1,0:T(8,128)(2,1)S(1)} %get-tuple-element.52.refs_2_, f32[2,128,128]{2,1,0:T(8,128)S(1)} %get-tuple-element.53.refs_3_, ...), custom_call_target="tpu_custom_call" | custom-call | tf_op jit(solution)/shard_map/pallas_call | solution.py:646
  42.4 6.4 %all-to-all-start.1 = ((bf16[128,3,2,128]{3,2,1,0:T(2,128)(2,1)}), bf16[128,3,2,128]{3,2,1,0:T(2,128)(2,1)S(1)}, u32[]{:S(2)}, u32[]{:S(2)}) async-start(bf16[128,3,2,128]{3,2,1,0:T(2,128)(2,1)} %shard_map.303.refs_10_), calls=%async_computation.1 | async-start | bytes 393216 | tf_op jit(solution)/shard_map/all_to_all | solution.py:729
  48.8 5.5 %shard_map.305 = (bf16[2,256,256]{2,1,0:T(8,128)(2,1)S(1)}, bf16[256,256]{1,0:T(8,128)(2,1)S(1)}, f32[2,128,256]{2,1,0:T(8,128)S(1)}, bf16[2,256,256]{2,1,0:T(8,...) custom-call(bf16[2,256,256]{2,1,0:T(8,128)(2,1)} %constant.69.clone., ...), custom_call_target="tpu_custom_call" | custom-call | tf_op jit(solution)/shard_map/pallas_call | solution.py:703
  54.4 8.4 %all-to-all-done.1.refs_0_ = bf16[128,3,2,128]{3,2,1,0:T(2,128)(2,1)S(1)} async-done(((bf16[128,3,2,128]{3,2,1,0:T(2,128)(2,1)}), bf16[128,3,2,128]{3,2,1,0:T(2,128)(2,1)S(1)}, u32[]{:S(2)}, u32[]{:S(2)}) %all-to-all-start.1) | async-done | bytes 196640 | tf_op jit(solution)/shard_map/all_to_all | solution.py:729
  62.7 6.6 %shard_map.306 = bf16[16,25,2,128]{3,2,1,0:T(2,128)(2,1)S(1)} custom-call(bf16[128,3,2,128]{3,2,1,0:T(2,128)(2,1)S(1)} %all-to-all-done.1.refs_0_, bf16[2,256,256]{2,1,0:T(8,128)(2,1)S(1)} %get-tuple-element.61.refs_1_, bf16[256,256]{1,0:T(8,128)(2,1)S(1)} %get-tuple-element.62.refs_2_, f32[2,128,256]{2,1,0:T(8,128)S(1)} %get-tuple-element.63.refs_3_, ...), custom_call_target="tpu_custom_call" | custom-call | tf_op jit(solution)/shard_map/pallas_call | solution.py:646
  69.3 12.5 %all_to_all.20.refs_0_ = bf16[16,25,2,128]{3,2,1,0:T(2,128)(2,1)S(1)} all-to-all(bf16[16,25,2,128]{3,2,1,0:T(2,128)(2,1)S(1)} %shard_map.306), channel_id=1, replica_groups={{0,2,4,6,8,10,12,14,16,18,20,22,24,26,28,30},{32,34,36,38,40,42,44,46,4..., dimensions={0} | all-to-all | bytes 409600 | tf_op jit(solution)/shard_map/all_to_all | solution.py:729
  81.8 0.8 shard_map.307
  82.5 3.4 %all-to-all-start.3 = ((bf16[8,25,2,128]{3,2,1,0:T(2,128)(2,1)}), bf16[8,25,2,128]{3,2,1,0:T(2,128)(2,1)S(1)}, u32[]{:S(2)}, u32[]{:S(2)}) async-start(bf16[8,25,2,128]{3,2,1,0:T(2,128)(2,1)} %shard_map.307), calls=%async_computation.3 | async-start | bytes 204800 | tf_op jit(solution)/shard_map/all_to_all | solution.py:729
  85.9 2.4 %shard_map.304 = f32[2,4,4096]{2,1,0:T(4,128)} custom-call(bf16[128,3,2,128]{3,2,1,0:T(2,128)(2,1)S(1)} %all-to-all-done.1.refs_0_, bf16[2,256,256]{2,1,0:T(8,128)(2,1)} %constant.69.clone.refs_1_.refs_0_, bf16[256,256]{1,0:T(8,128)(2,1)} %constant.70.clone.refs_2_.refs_1_, f32[2,128,128]{2,1,0:T(8,128)} %constant.76.clone.refs_3_, ...), custom_call_target="tpu_custom_call" | custom-call | tf_op jit(solution)/shard_map/pallas_call | solution.py:646
  88.3 5.0 %all-to-all-done.3.refs_0_ = bf16[8,25,2,128]{3,2,1,0:T(2,128)(2,1)S(1)} async-done(((bf16[8,25,2,128]{3,2,1,0:T(2,128)(2,1)}), bf16[8,25,2,128]{3,2,1,0:T(2,128)(2,1)S(1)}, u32[]{:S(2)}, u32[]{:S(2)}) %all-to-all-start.3) | async-done | bytes 102432 | tf_op jit(solution)/shard_map/all_to_all | solution.py:729
  93.3 0.7 shard_map.308
Async XLA Ops:
  0.6 8.4 %collective-permute-start = (f32[2,4,4096]{2,1,0:T(4,128)}, f32[2,4,4096]{2,1,0:T(4,128)S(1)}, u32[]{:S(2)}, u32[]{:S(2)}) collective-permute-start(f32[2,4,4096]{2,1,0:T(4,128)} %refs_11_.1), channel_id=1, source_target_pairs={{0,2},{2,4},{4,6},{6,8},{8,10},{10,12},{12,14},{14,16},{16,18},{18... | collective-permute-start | bytes 393224 | tf_op jit(solution)/shard_map/ppermute | solution.py:741
  13.4 27.1 %all-to-all-start = ((bf16[128,2,2,128]{3,2,1,0:T(2,128)(2,1)}), bf16[128,2,2,128]{3,2,1,0:T(2,128)(2,1)S(1)}, u32[]{:S(2)}, u32[]{:S(2)}) async-start(bf16[128,2,2,128]{3,2,1,0:T(2,128)(2,1)} %get-tuple-element.50.refs_8_), calls=%async_computation | async-start | bytes 262144 | tf_op jit(solution)/shard_map/all_to_all | solution.py:729
  42.4 20.4 %all-to-all-start.1 = ((bf16[128,3,2,128]{3,2,1,0:T(2,128)(2,1)}), bf16[128,3,2,128]{3,2,1,0:T(2,128)(2,1)S(1)}, u32[]{:S(2)}, u32[]{:S(2)}) async-start(bf16[128,3,2,128]{3,2,1,0:T(2,128)(2,1)} %shard_map.303.refs_10_), calls=%async_computation.1 | async-start | bytes 393216 | tf_op jit(solution)/shard_map/all_to_all | solution.py:729
  82.5 10.8 %all-to-all-start.3 = ((bf16[8,25,2,128]{3,2,1,0:T(2,128)(2,1)}), bf16[8,25,2,128]{3,2,1,0:T(2,128)(2,1)S(1)}, u32[]{:S(2)}, u32[]{:S(2)}) async-start(bf16[8,25,2,128]{3,2,1,0:T(2,128)(2,1)} %shard_map.307), calls=%async_computation.3 | async-start | bytes 204800 | tf_op jit(solution)/shard_map/all_to_all | solution.py:729

commit v7 on v6

--- a/solution.py
+++ b/solution.py
@@ -233,7 +233,8 @@
 
 
 def pair_low(form, pair, x):
-    return form(pair[0], x) + form(pair[1], x)
+    low = x.astype(BF)
+    return form(pair[0], low) + form(pair[1], low)
 
 
 def to_blocks(x):
@@ -245,12 +246,12 @@
     return jnp.concatenate([x[rows * a : rows * a + rows] for a in range(OUTER)], axis=1)
 
 
-def column_forward(x, forward_a, forward_b, forward_b0, twist):
-    y = exact(dot, forward_a, to_blocks(x))
+def column_forward(x, forward_a, forward_b, forward_b0, twist, product):
+    y = product(dot, forward_a, to_blocks(x))
     real, imag = y[:128], y[128:]
     cosine, sine = twist[0], twist[1]
     both = jnp.concatenate([real * cosine + imag * sine, imag * cosine - real * sine], axis=1)
-    general = exact(dot_nt, forward_b, both)
+    general = product(dot_nt, forward_b, both)
     zero = dot_nt(forward_b0[...], both.astype(BF))
     lane = lax.broadcasted_iota(jnp.int32, general.shape, 1)
     return jnp.where(lane % 64 < R, zero, general).astype(BF)
@@ -344,7 +345,7 @@
     inner,
 ):
     x = jnp.concatenate([field[0], field[1]], axis=0)
-    sent[...] = column_forward(x, forward_a, forward_b, forward_b0, twist).reshape(D, 2, 128)
+    sent[...] = column_forward(x, forward_a, forward_b, forward_b0, twist, exact).reshape(D, 2, 128)
     base = jnp.concatenate([velocity[0], velocity[1]], axis=0)
     shifts = [pltpu.roll(base, 1, 1), base, pltpu.roll(base, NY - 1, 1)]
     inner[...] = jnp.concatenate(shifts, axis=0).astype(BF)
@@ -430,7 +431,7 @@
         )
     advect = 0.5 * jnp.concatenate(pieces, axis=0)
     provisional = jnp.concatenate(rows, axis=0) + STEP_SIZE * (correction - advect)
-    sent[:, 0] = column_forward(provisional, forward_a, forward_b, forward_b0, twist).reshape(D, 2, 128)
+    sent[:, 0] = column_forward(provisional, forward_a, forward_b, forward_b0, twist, pair_low).reshape(D, 2, 128)
 
 
 def middle_kernel(
@@ -464,9 +465,10 @@
     ):
         real, imag = part[:, :128], part[:, 128:]
         parts.append(jnp.concatenate([real * cosine - imag * sine, imag * cosine + real * sine], axis=0))
-    out = exact(dot, row_inverse, side_by_side(parts)).astype(BF)
-    for k in range(3):
-        sent[:, k] = out[:, 128 * k : 128 * k + 128].reshape(D, 2, 128)
+    sent[:, 0] = pair_low(dot, row_inverse, parts[0]).astype(BF).reshape(D, 2, 128)
+    out = exact(dot, row_inverse, side_by_side(parts[1:])).astype(BF)
+    for k in range(2):
+        sent[:, k + 1] = out[:, 128 * k : 128 * k + 128].reshape(D, 2, 128)
 
 
 def backward_kernel(

time: 94.5 us -> 94.4 us (level)
  no operation moved by 1% of the time
where the time goes in v7:
time: 94.4 us; the launch traced here: 93.9 us
  Pallas kernels  30.2 us (32%)
  starting transfers between devices  28.2 us (30%)
  waiting for transfers between devices  22.4 us (24%)
  blocking collectives  12.5 us (13%)
    all_to_all x3, starting transfers between devices, exchange(): lax.all_to_all(x, 'rows', split_axis=0, concat_axis=0, tiled=True, axis_i...  24 us
    all_to_all x3, waiting for transfers between devices, exchange(): lax.all_to_all(x, 'rows', split_axis=0, concat_axis=0, tiled=True, axis_i...  22.4 us
    pallas_call x7, Pallas kernels, call(): pl.pallas_call(run, out_shape=outputs, in_specs=specs, out_specs=out_spec...  20.8 us
    all_to_all x1, blocking collectives, exchange(): lax.all_to_all(x, 'rows', split_axis=0, concat_axis=0, tiled=True, axis_i...  12.5 us
    pallas_call x2, Pallas kernels, prefetch(): pl.pallas_call(run, out_shape=[pltpu.VMEM(x.shape, x.dtype) for x in arra...  9.4 us
    ppermute x1, starting transfers between devices, body(): above = lax.ppermute(velocity, 'rows', down)  4.21 us
  transfers between devices with their start and end apart: 4, of which 3 were waited for; matrix products, arithmetic and copies ran while one was open for 0% of the time, Pallas kernels for 17%

profile of v7, /device:TPU:1, one launch (start us, length us, event | category | flops | bytes accessed | tf_op | source)
XLA Modules:
  0.0 93.9 jit_solution(6910815161170666607)
XLA Ops:
  0.6 4.2 %collective-permute-start = (f32[2,4,4096]{2,1,0:T(4,128)}, f32[2,4,4096]{2,1,0:T(4,128)S(1)}, u32[]{:S(2)}, u32[]{:S(2)}) collective-permute-start(f32[2,4,4096]{2,1,0:T(4,128)} %refs_11_.1), channel_id=1, source_target_pairs={{0,2},{2,4},{4,6},{6,8},{8,10},{10,12},{12,14},{14,16},{16,18},{18... | collective-permute-start | bytes 393224 | tf_op jit(solution)/shard_map/ppermute | solution.py:743
  4.8 4.2 %shard_map.300 = (bf16[128,2,128]{2,1,0:T(2,128)(2,1)S(1)}, bf16[128,4096]{1,0:T(8,128)(2,1)S(1)}, bf16[384,48]{1,0:T(8,128)(2,1)S(1)}, bf16[24,384]{1,0:T(8,128...) custom-call(f32[2,4,4096]{2,1,0:T(4,128)} %refs_0_.3, ...), custom_call_target="tpu_custom_call" | custom-call | tf_op jit(solution)/shard_map/pallas_call | solution.py:648
  9.0 0.0 collective-permute-done.refs_5_
  9.1 4.3 %shard_map.301 = (bf16[128,2,2,128]{3,2,1,0:T(2,128)(2,1)}, bf16[48,4096]{1,0:T(8,128)(2,1)S(1)}) custom-call(bf16[128,2,128]{2,1,0:T(2,128)(2,1)S(1)} %get-tuple-element.40.refs_0_, bf16[128,4096]{1,0:T(8,128)(2,1)S(1)} %get-tuple-element.41.refs_1_, bf16[384,48]{1,0:T(8,128)(2,1)S(1)} %get-tuple-element.42.refs_2_.refs_10_, ...), custom_call_target="tpu_custom_call" | custom-call | tf_op jit(solution)/shard_map/pallas_call | solution.py:648
  13.3 14.1 %all-to-all-start = ((bf16[128,2,2,128]{3,2,1,0:T(2,128)(2,1)}), bf16[128,2,2,128]{3,2,1,0:T(2,128)(2,1)S(1)}, u32[]{:S(2)}, u32[]{:S(2)}) async-start(bf16[128,2,2,128]{3,2,1,0:T(2,128)(2,1)} %get-tuple-element.50.refs_8_), calls=%async_computation | async-start | bytes 262144 | tf_op jit(solution)/shard_map/all_to_all | solution.py:731
  27.5 3.9 %shard_map.302 = (bf16[2,256,256]{2,1,0:T(8,128)(2,1)S(1)}, f32[2,128,128]{2,1,0:T(8,128)S(1)}, f32[2,128,128]{2,1,0:T(8,128)S(1)}, bf16[256,256]{1,0:T(8,128)(2...) custom-call(bf16[2,256,256]{2,1,0:T(8,128)(2,1)} %constant.61.clone., ...), custom_call_target="tpu_custom_call" | custom-call | tf_op jit(solution)/shard_map/pallas_call | solution.py:705
  31.4 9.0 %all-to-all-done.refs_1_ = bf16[128,2,2,128]{3,2,1,0:T(2,128)(2,1)S(1)} async-done(((bf16[128,2,2,128]{3,2,1,0:T(2,128)(2,1)}), bf16[128,2,2,128]{3,2,1,0:T(2,128)(2,1)S(1)}, u32[]{:S(2)}, u32[]{:S(2)}) %all-to-all-start) | async-done | bytes 131104 | tf_op jit(solution)/shard_map/all_to_all | solution.py:731
  40.5 1.8 %shard_map.303.refs_10_ = bf16[128,3,2,128]{3,2,1,0:T(2,128)(2,1)} custom-call(s32[1]{0:T(128)} %bitcast.refs_0_, bf16[128,2,2,128]{3,2,1,0:T(2,128)(2,1)S(1)} %all-to-all-done.refs_1_, bf16[2,256,256]{2,1,0:T(8,128)(2,1)S(1)} %get-tuple-element.52.refs_2_, f32[2,128,128]{2,1,0:T(8,128)S(1)} %get-tuple-element.53.refs_3_, ...), custom_call_target="tpu_custom_call" | custom-call | tf_op jit(solution)/shard_map/pallas_call | solution.py:648
  42.3 6.4 %all-to-all-start.1 = ((bf16[128,3,2,128]{3,2,1,0:T(2,128)(2,1)}), bf16[128,3,2,128]{3,2,1,0:T(2,128)(2,1)S(1)}, u32[]{:S(2)}, u32[]{:S(2)}) async-start(bf16[128,3,2,128]{3,2,1,0:T(2,128)(2,1)} %shard_map.303.refs_10_), calls=%async_computation.1 | async-start | bytes 393216 | tf_op jit(solution)/shard_map/all_to_all | solution.py:731
  48.8 5.5 %shard_map.305 = (bf16[2,256,256]{2,1,0:T(8,128)(2,1)S(1)}, bf16[256,256]{1,0:T(8,128)(2,1)S(1)}, f32[2,128,256]{2,1,0:T(8,128)S(1)}, bf16[2,256,256]{2,1,0:T(8,...) custom-call(bf16[2,256,256]{2,1,0:T(8,128)(2,1)} %constant.69.clone., ...), custom_call_target="tpu_custom_call" | custom-call | tf_op jit(solution)/shard_map/pallas_call | solution.py:705
  54.3 8.4 %all-to-all-done.1.refs_0_ = bf16[128,3,2,128]{3,2,1,0:T(2,128)(2,1)S(1)} async-done(((bf16[128,3,2,128]{3,2,1,0:T(2,128)(2,1)}), bf16[128,3,2,128]{3,2,1,0:T(2,128)(2,1)S(1)}, u32[]{:S(2)}, u32[]{:S(2)}) %all-to-all-start.1) | async-done | bytes 196640 | tf_op jit(solution)/shard_map/all_to_all | solution.py:731
  62.6 6.6 %shard_map.306 = bf16[16,25,2,128]{3,2,1,0:T(2,128)(2,1)S(1)} custom-call(bf16[128,3,2,128]{3,2,1,0:T(2,128)(2,1)S(1)} %all-to-all-done.1.refs_0_, bf16[2,256,256]{2,1,0:T(8,128)(2,1)S(1)} %get-tuple-element.61.refs_1_, bf16[256,256]{1,0:T(8,128)(2,1)S(1)} %get-tuple-element.62.refs_2_, f32[2,128,256]{2,1,0:T(8,128)S(1)} %get-tuple-element.63.refs_3_, ...), custom_call_target="tpu_custom_call" | custom-call | tf_op jit(solution)/shard_map/pallas_call | solution.py:648
  69.2 12.5 %all_to_all.20.refs_0_ = bf16[16,25,2,128]{3,2,1,0:T(2,128)(2,1)S(1)} all-to-all(bf16[16,25,2,128]{3,2,1,0:T(2,128)(2,1)S(1)} %shard_map.306), channel_id=1, replica_groups={{0,2,4,6,8,10,12,14,16,18,20,22,24,26,28,30},{32,34,36,38,40,42,44,46,4..., dimensions={0} | all-to-all | bytes 409600 | tf_op jit(solution)/shard_map/all_to_all | solution.py:731
  81.7 0.8 shard_map.307
  82.4 3.4 %all-to-all-start.3 = ((bf16[8,25,2,128]{3,2,1,0:T(2,128)(2,1)}), bf16[8,25,2,128]{3,2,1,0:T(2,128)(2,1)S(1)}, u32[]{:S(2)}, u32[]{:S(2)}) async-start(bf16[8,25,2,128]{3,2,1,0:T(2,128)(2,1)} %shard_map.307), calls=%async_computation.3 | async-start | bytes 204800 | tf_op jit(solution)/shard_map/all_to_all | solution.py:731
  85.8 2.4 %shard_map.304 = f32[2,4,4096]{2,1,0:T(4,128)} custom-call(bf16[128,3,2,128]{3,2,1,0:T(2,128)(2,1)S(1)} %all-to-all-done.1.refs_0_, bf16[2,256,256]{2,1,0:T(8,128)(2,1)} %constant.69.clone.refs_1_.refs_0_, bf16[256,256]{1,0:T(8,128)(2,1)} %constant.70.clone.refs_2_.refs_1_, f32[2,128,128]{2,1,0:T(8,128)} %constant.76.clone.refs_3_, ...), custom_call_target="tpu_custom_call" | custom-call | tf_op jit(solution)/shard_map/pallas_call | solution.py:648
  88.2 5.0 %all-to-all-done.3.refs_0_ = bf16[8,25,2,128]{3,2,1,0:T(2,128)(2,1)S(1)} async-done(((bf16[8,25,2,128]{3,2,1,0:T(2,128)(2,1)}), bf16[8,25,2,128]{3,2,1,0:T(2,128)(2,1)S(1)}, u32[]{:S(2)}, u32[]{:S(2)}) %all-to-all-start.3) | async-done | bytes 102432 | tf_op jit(solution)/shard_map/all_to_all | solution.py:731
  93.2 0.7 shard_map.308
Async XLA Ops:
  0.6 8.4 %collective-permute-start = (f32[2,4,4096]{2,1,0:T(4,128)}, f32[2,4,4096]{2,1,0:T(4,128)S(1)}, u32[]{:S(2)}, u32[]{:S(2)}) collective-permute-start(f32[2,4,4096]{2,1,0:T(4,128)} %refs_11_.1), channel_id=1, source_target_pairs={{0,2},{2,4},{4,6},{6,8},{8,10},{10,12},{12,14},{14,16},{16,18},{18... | collective-permute-start | bytes 393224 | tf_op jit(solution)/shard_map/ppermute | solution.py:743
  13.3 27.1 %all-to-all-start = ((bf16[128,2,2,128]{3,2,1,0:T(2,128)(2,1)}), bf16[128,2,2,128]{3,2,1,0:T(2,128)(2,1)S(1)}, u32[]{:S(2)}, u32[]{:S(2)}) async-start(bf16[128,2,2,128]{3,2,1,0:T(2,128)(2,1)} %get-tuple-element.50.refs_8_), calls=%async_computation | async-start | bytes 262144 | tf_op jit(solution)/shard_map/all_to_all | solution.py:731
  42.3 20.4 %all-to-all-start.1 = ((bf16[128,3,2,128]{3,2,1,0:T(2,128)(2,1)}), bf16[128,3,2,128]{3,2,1,0:T(2,128)(2,1)S(1)}, u32[]{:S(2)}, u32[]{:S(2)}) async-start(bf16[128,3,2,128]{3,2,1,0:T(2,128)(2,1)} %shard_map.303.refs_10_), calls=%async_computation.1 | async-start | bytes 393216 | tf_op jit(solution)/shard_map/all_to_all | solution.py:731
  82.4 10.8 %all-to-all-start.3 = ((bf16[8,25,2,128]{3,2,1,0:T(2,128)(2,1)}), bf16[8,25,2,128]{3,2,1,0:T(2,128)(2,1)S(1)}, u32[]{:S(2)}, u32[]{:S(2)}) async-start(bf16[8,25,2,128]{3,2,1,0:T(2,128)(2,1)} %shard_map.307), calls=%async_computation.3 | async-start | bytes 204800 | tf_op jit(solution)/shard_map/all_to_all | solution.py:731

commit v8 on v7

--- a/solution.py
+++ b/solution.py
@@ -546,7 +546,7 @@
         sum_mid[...] += dot_nt(delta_two, arrived(1))
         back_one = dot(middle, delta_two)
         sum_out[...] += dot_nt(arrived(2), dual)
-        delta_one = (back_one * arrived(3)).astype(BF)
+        delta_one = (back_one * arrived(3).astype(F32)).astype(BF)
         sum_in[...] += dot_nt(delta_one, stack[:, at])
         return 0
 
@@ -666,7 +666,7 @@
     return lambda at: dot(middle, act_one[:, at])
 
 
-def prefetch(arrays, after, maker, near, wide=()):
+def prefetch(arrays, after, maker, near, wide=(), kept_as=F32):
     count, given, tiles = len(arrays), len(wide), NY // TILE
 
     def run(*refs):
@@ -692,7 +692,7 @@
                 copy.wait()
             square, gate, value = gelu_parts(layer(at))
             results[0][:, at] = value.astype(BF)
-            results[1][:, at] = slope_of(square, gate, value)
+            results[1][:, at] = slope_of(square, gate, value).astype(kept_as)
             for k in range(2):
                 copies.append(
                     pltpu.make_async_copy(results[k].at[:, at], homes[k].at[:, at], out_semaphores.at[k, index])
@@ -705,7 +705,7 @@
     *tables, act, slope = pl.pallas_call(
         run,
         out_shape=[pltpu.VMEM(x.shape, x.dtype) for x in arrays[:count]]
-        + [pltpu.HBM((OWN, NY), BF), pltpu.HBM((OWN, NY), F32)],
+        + [pltpu.HBM((OWN, NY), BF), pltpu.HBM((OWN, NY), kept_as)],
         in_specs=[pl.BlockSpec(memory_space=pltpu.HBM)] * (count + given)
         + [pl.BlockSpec(memory_space=pl.ANY)]
         + [pl.BlockSpec(memory_space=pltpu.VMEM)] * len(near),
@@ -713,7 +713,7 @@
         scratch_shapes=[pltpu.VMEM(x.shape, x.dtype) for x in arrays[count:]]
         + [
             pltpu.VMEM((OWN, NY), BF),
-            pltpu.VMEM((OWN, NY), F32),
+            pltpu.VMEM((OWN, NY), kept_as),
             pltpu.SemaphoreType.DMA((count,)),
             pltpu.SemaphoreType.DMA((max(given, 1), tiles)),
             pltpu.SemaphoreType.DMA((2, tiles)),
@@ -774,6 +774,7 @@
         first_sent,
         layer_one_kernel,
         [stack, first_all],
+        kept_as=BF,
     )
     second_sent = call(
         middle_kernel, shape((D, 3, 2, 128), BF), [device, first_got, *tables], scalars=1
@@ -804,7 +805,7 @@
         shape((len(one[0]), 25, 2, 128), BF),
         [second_got, *tables, stack, act_one, act_two, slope_one, slope_two],
         [
-            *[pltpu.VMEM((OWN, NY), t) for t in (BF, BF, F32, F32)],
+            *[pltpu.VMEM((OWN, NY), t) for t in (BF, BF, BF, F32)],
             pltpu.VMEM((48, NY), BF),
             pltpu.VMEM((OWN, OWN), F32),
             pltpu.VMEM((OWN, 48), F32),

time: 94.4 us -> 94.3 us (level)
  no operation moved by 1% of the time
where the time goes in v8:
time: 94.3 us; the launch traced here: 93.9 us
  Pallas kernels  30.3 us (32%)
  starting transfers between devices  28.2 us (30%)
  waiting for transfers between devices  22.4 us (24%)
  blocking collectives  12.4 us (13%)
    all_to_all x3, starting transfers between devices, exchange(): lax.all_to_all(x, 'rows', split_axis=0, concat_axis=0, tiled=True, axis_i...  24 us
    all_to_all x3, waiting for transfers between devices, exchange(): lax.all_to_all(x, 'rows', split_axis=0, concat_axis=0, tiled=True, axis_i...  22.3 us
    pallas_call x7, Pallas kernels, call(): pl.pallas_call(run, out_shape=outputs, in_specs=specs, out_specs=out_spec...  20.8 us
    all_to_all x1, blocking collectives, exchange(): lax.all_to_all(x, 'rows', split_axis=0, concat_axis=0, tiled=True, axis_i...  12.4 us
    pallas_call x2, Pallas kernels, prefetch(): pl.pallas_call(run, out_shape=[pltpu.VMEM(x.shape, x.dtype) for x in arra...  9.52 us
    ppermute x1, starting transfers between devices, body(): above = lax.ppermute(velocity, 'rows', down)  4.21 us
  transfers between devices with their start and end apart: 4, of which 3 were waited for; matrix products, arithmetic and copies ran while one was open for 0% of the time, Pallas kernels for 17%

profile of v8, /device:TPU:1, one launch (start us, length us, event | category | flops | bytes accessed | tf_op | source)
XLA Modules:
  0.0 93.9 jit_solution(5057715066337296185)
XLA Ops:
  0.6 4.2 %collective-permute-start = (f32[2,4,4096]{2,1,0:T(4,128)}, f32[2,4,4096]{2,1,0:T(4,128)S(1)}, u32[]{:S(2)}, u32[]{:S(2)}) collective-permute-start(f32[2,4,4096]{2,1,0:T(4,128)} %refs_11_.1), channel_id=1, source_target_pairs={{0,2},{2,4},{4,6},{6,8},{8,10},{10,12},{12,14},{14,16},{16,18},{18... | collective-permute-start | bytes 393224 | tf_op jit(solution)/shard_map/ppermute | solution.py:743
  4.8 4.2 %shard_map.300 = (bf16[128,2,128]{2,1,0:T(2,128)(2,1)S(1)}, bf16[128,4096]{1,0:T(8,128)(2,1)S(1)}, bf16[384,48]{1,0:T(8,128)(2,1)S(1)}, bf16[24,384]{1,0:T(8,128...) custom-call(f32[2,4,4096]{2,1,0:T(4,128)} %refs_0_.3, ...), custom_call_target="tpu_custom_call" | custom-call | tf_op jit(solution)/shard_map/pallas_call | solution.py:648
  9.0 0.0 collective-permute-done.refs_5_
  9.1 4.3 %shard_map.301 = (bf16[128,2,2,128]{3,2,1,0:T(2,128)(2,1)}, bf16[48,4096]{1,0:T(8,128)(2,1)S(1)}) custom-call(bf16[128,2,128]{2,1,0:T(2,128)(2,1)S(1)} %get-tuple-element.40.refs_0_, bf16[128,4096]{1,0:T(8,128)(2,1)S(1)} %get-tuple-element.41.refs_1_, bf16[384,48]{1,0:T(8,128)(2,1)S(1)} %get-tuple-element.42.refs_2_.refs_10_, ...), custom_call_target="tpu_custom_call" | custom-call | tf_op jit(solution)/shard_map/pallas_call | solution.py:648
  13.3 14.1 %all-to-all-start = ((bf16[128,2,2,128]{3,2,1,0:T(2,128)(2,1)}), bf16[128,2,2,128]{3,2,1,0:T(2,128)(2,1)S(1)}, u32[]{:S(2)}, u32[]{:S(2)}) async-start(bf16[128,2,2,128]{3,2,1,0:T(2,128)(2,1)} %get-tuple-element.50.refs_8_), calls=%async_computation | async-start | bytes 262144 | tf_op jit(solution)/shard_map/all_to_all | solution.py:731
  27.5 4.1 %shard_map.302 = (bf16[2,256,256]{2,1,0:T(8,128)(2,1)S(1)}, f32[2,128,128]{2,1,0:T(8,128)S(1)}, f32[2,128,128]{2,1,0:T(8,128)S(1)}, bf16[256,256]{1,0:T(8,128)(2...) custom-call(bf16[2,256,256]{2,1,0:T(8,128)(2,1)} %constant.61.clone., ...), custom_call_target="tpu_custom_call" | custom-call | tf_op jit(solution)/shard_map/pallas_call | solution.py:705
  31.6 8.9 %all-to-all-done.refs_1_ = bf16[128,2,2,128]{3,2,1,0:T(2,128)(2,1)S(1)} async-done(((bf16[128,2,2,128]{3,2,1,0:T(2,128)(2,1)}), bf16[128,2,2,128]{3,2,1,0:T(2,128)(2,1)S(1)}, u32[]{:S(2)}, u32[]{:S(2)}) %all-to-all-start) | async-done | bytes 131104 | tf_op jit(solution)/shard_map/all_to_all | solution.py:731
  40.5 1.8 %shard_map.303.refs_10_ = bf16[128,3,2,128]{3,2,1,0:T(2,128)(2,1)} custom-call(s32[1]{0:T(128)} %bitcast.refs_0_, bf16[128,2,2,128]{3,2,1,0:T(2,128)(2,1)S(1)} %all-to-all-done.refs_1_, bf16[2,256,256]{2,1,0:T(8,128)(2,1)S(1)} %get-tuple-element.52.refs_2_, f32[2,128,128]{2,1,0:T(8,128)S(1)} %get-tuple-element.53.refs_3_, ...), custom_call_target="tpu_custom_call" | custom-call | tf_op jit(solution)/shard_map/pallas_call | solution.py:648
  42.3 6.5 %all-to-all-start.1 = ((bf16[128,3,2,128]{3,2,1,0:T(2,128)(2,1)}), bf16[128,3,2,128]{3,2,1,0:T(2,128)(2,1)S(1)}, u32[]{:S(2)}, u32[]{:S(2)}) async-start(bf16[128,3,2,128]{3,2,1,0:T(2,128)(2,1)} %shard_map.303.refs_10_), calls=%async_computation.1 | async-start | bytes 393216 | tf_op jit(solution)/shard_map/all_to_all | solution.py:731
  48.8 5.5 %shard_map.305 = (bf16[2,256,256]{2,1,0:T(8,128)(2,1)S(1)}, bf16[256,256]{1,0:T(8,128)(2,1)S(1)}, f32[2,128,256]{2,1,0:T(8,128)S(1)}, bf16[2,256,256]{2,1,0:T(8,...) custom-call(bf16[2,256,256]{2,1,0:T(8,128)(2,1)} %constant.69.clone., ...), custom_call_target="tpu_custom_call" | custom-call | tf_op jit(solution)/shard_map/pallas_call | solution.py:705
  54.2 8.5 %all-to-all-done.1.refs_0_ = bf16[128,3,2,128]{3,2,1,0:T(2,128)(2,1)S(1)} async-done(((bf16[128,3,2,128]{3,2,1,0:T(2,128)(2,1)}), bf16[128,3,2,128]{3,2,1,0:T(2,128)(2,1)S(1)}, u32[]{:S(2)}, u32[]{:S(2)}) %all-to-all-start.1) | async-done | bytes 196640 | tf_op jit(solution)/shard_map/all_to_all | solution.py:731
  62.7 6.6 %shard_map.306 = bf16[16,25,2,128]{3,2,1,0:T(2,128)(2,1)S(1)} custom-call(bf16[128,3,2,128]{3,2,1,0:T(2,128)(2,1)S(1)} %all-to-all-done.1.refs_0_, bf16[2,256,256]{2,1,0:T(8,128)(2,1)S(1)} %get-tuple-element.61.refs_1_, bf16[256,256]{1,0:T(8,128)(2,1)S(1)} %get-tuple-element.62.refs_2_, f32[2,128,256]{2,1,0:T(8,128)S(1)} %get-tuple-element.63.refs_3_, ...), custom_call_target="tpu_custom_call" | custom-call | tf_op jit(solution)/shard_map/pallas_call | solution.py:648
  69.3 12.4 %all_to_all.20.refs_0_ = bf16[16,25,2,128]{3,2,1,0:T(2,128)(2,1)S(1)} all-to-all(bf16[16,25,2,128]{3,2,1,0:T(2,128)(2,1)S(1)} %shard_map.306), channel_id=1, replica_groups={{0,2,4,6,8,10,12,14,16,18,20,22,24,26,28,30},{32,34,36,38,40,42,44,46,4..., dimensions={0} | all-to-all | bytes 409600 | tf_op jit(solution)/shard_map/all_to_all | solution.py:731
  81.6 0.8 shard_map.307
  82.4 3.4 %all-to-all-start.3 = ((bf16[8,25,2,128]{3,2,1,0:T(2,128)(2,1)}), bf16[8,25,2,128]{3,2,1,0:T(2,128)(2,1)S(1)}, u32[]{:S(2)}, u32[]{:S(2)}) async-start(bf16[8,25,2,128]{3,2,1,0:T(2,128)(2,1)} %shard_map.307), calls=%async_computation.3 | async-start | bytes 204800 | tf_op jit(solution)/shard_map/all_to_all | solution.py:731
  85.8 2.4 %shard_map.304 = f32[2,4,4096]{2,1,0:T(4,128)} custom-call(bf16[128,3,2,128]{3,2,1,0:T(2,128)(2,1)S(1)} %all-to-all-done.1.refs_0_, bf16[2,256,256]{2,1,0:T(8,128)(2,1)} %constant.69.clone.refs_1_.refs_0_, bf16[256,256]{1,0:T(8,128)(2,1)} %constant.70.clone.refs_2_.refs_1_, f32[2,128,128]{2,1,0:T(8,128)} %constant.76.clone.refs_3_, ...), custom_call_target="tpu_custom_call" | custom-call | tf_op jit(solution)/shard_map/pallas_call | solution.py:648
  88.2 5.0 %all-to-all-done.3.refs_0_ = bf16[8,25,2,128]{3,2,1,0:T(2,128)(2,1)S(1)} async-done(((bf16[8,25,2,128]{3,2,1,0:T(2,128)(2,1)}), bf16[8,25,2,128]{3,2,1,0:T(2,128)(2,1)S(1)}, u32[]{:S(2)}, u32[]{:S(2)}) %all-to-all-start.3) | async-done | bytes 102432 | tf_op jit(solution)/shard_map/all_to_all | solution.py:731
  93.2 0.7 shard_map.308
Async XLA Ops:
  0.6 8.4 %collective-permute-start = (f32[2,4,4096]{2,1,0:T(4,128)}, f32[2,4,4096]{2,1,0:T(4,128)S(1)}, u32[]{:S(2)}, u32[]{:S(2)}) collective-permute-start(f32[2,4,4096]{2,1,0:T(4,128)} %refs_11_.1), channel_id=1, source_target_pairs={{0,2},{2,4},{4,6},{6,8},{8,10},{10,12},{12,14},{14,16},{16,18},{18... | collective-permute-start | bytes 393224 | tf_op jit(solution)/shard_map/ppermute | solution.py:743
  13.3 27.1 %all-to-all-start = ((bf16[128,2,2,128]{3,2,1,0:T(2,128)(2,1)}), bf16[128,2,2,128]{3,2,1,0:T(2,128)(2,1)S(1)}, u32[]{:S(2)}, u32[]{:S(2)}) async-start(bf16[128,2,2,128]{3,2,1,0:T(2,128)(2,1)} %get-tuple-element.50.refs_8_), calls=%async_computation | async-start | bytes 262144 | tf_op jit(solution)/shard_map/all_to_all | solution.py:731
  42.3 20.4 %all-to-all-start.1 = ((bf16[128,3,2,128]{3,2,1,0:T(2,128)(2,1)}), bf16[128,3,2,128]{3,2,1,0:T(2,128)(2,1)S(1)}, u32[]{:S(2)}, u32[]{:S(2)}) async-start(bf16[128,3,2,128]{3,2,1,0:T(2,128)(2,1)} %shard_map.303.refs_10_), calls=%async_computation.1 | async-start | bytes 393216 | tf_op jit(solution)/shard_map/all_to_all | solution.py:731
  82.4 10.8 %all-to-all-start.3 = ((bf16[8,25,2,128]{3,2,1,0:T(2,128)(2,1)}), bf16[8,25,2,128]{3,2,1,0:T(2,128)(2,1)S(1)}, u32[]{:S(2)}, u32[]{:S(2)}) async-start(bf16[8,25,2,128]{3,2,1,0:T(2,128)(2,1)} %shard_map.307), calls=%async_computation.3 | async-start | bytes 204800 | tf_op jit(solution)/shard_map/all_to_all | solution.py:731
